TPU v7x, 32 devices: a whole 2x2x4 slice. The times are simulated.
32 devices in a mesh: row: 8 (over z, x), col: 4 (over y, core).
Axes of the slice: x: 2, y: 2, z: 4, core: 2. Of those that a mesh axis runs over, the one named last changes fastest.
Arguments:
- pair: bfloat16 [320, 320, 128], P('row', 'col'), may hold values from -6 to 6
- token_mask: int32 [320], replicated, may hold values from 0 to 1, as said below
- chain_ids: int32 [320], replicated, may hold values from 0 to 7, never falling along the last dimension, each value on 1 to 80 neighbouring positions
- chain_bias: float32 [128], replicated, may hold values from -4 to 4
- in_weights: bfloat16 [2, 128, 640], replicated, may hold values from -0.5 to 0.5
- out_weights: bfloat16 [2, 128, 128], replicated, may hold values from -0.5 to 0.5
Outputs:
- pair_out: bfloat16 [320, 320, 128], P('row', 'col')
Inputs may be any that keep to these rules, and one draw needn't show every extreme that they name: token_mask is 0 on a run of padding at the end that always includes the last token; some tokens before it may be 0 as well. chain_ids never falls along the tokens.
All inputs are finite; a program needn't handle non-finite values.
Results may differ from a plain program's by a relative error of at most 0.015.
Values may be sent and summed in bfloat16 or wider, within the bound.
No kernel may reach another device: no remote copies, remote signals or barrier semaphores. Data moves between devices by JAX's collectives and lax.ppermute only.
A program may use at most 128 MiB of HBM per device.

v0:
```python
import jax
import jax.numpy as jnp
from jax import lax
from jax.sharding import PartitionSpec as P


def layer_norm(values):
    center = values - jnp.mean(values, axis=-1, keepdims=True)
    spread = jnp.mean(center * center, axis=-1, keepdims=True)
    return center * lax.rsqrt(spread + 1e-05)


def gated_inputs(field, weights, pair_mask):
    width = weights.shape[0]
    normed = layer_norm(field).astype(jnp.bfloat16)
    projected = jnp.einsum("ijc,cd->ijd", normed, weights, preferred_element_type=jnp.float32)
    first = (
        jax.nn.sigmoid(projected[..., :width])
        * projected[..., width : 2 * width]
        * pair_mask[:, :, None]
    ).astype(jnp.bfloat16)
    second = (
        jax.nn.sigmoid(projected[..., 2 * width : 3 * width])
        * projected[..., 3 * width : 4 * width]
        * pair_mask[:, :, None]
    ).astype(jnp.bfloat16)
    gate_value = jax.nn.sigmoid(projected[..., 4 * width :])
    return (first, second, gate_value)


def update(field, summed, gate_value, weights):
    normed_sum = layer_norm(summed).astype(jnp.bfloat16)
    output = jnp.einsum("ijc,cd->ijd", normed_sum, weights, preferred_element_type=jnp.float32)
    return field + gate_value * output


def per_device(pair, token_mask, chain_ids, chain_bias, in_weights, out_weights):
    row_count = pair.shape[0]
    col_count = pair.shape[1]
    row_start = lax.axis_index("row") * row_count
    col_start = lax.axis_index("col") * col_count
    valid_rows = lax.dynamic_slice_in_dim(token_mask, row_start, row_count).astype(jnp.float32)
    valid_cols = lax.dynamic_slice_in_dim(token_mask, col_start, col_count).astype(jnp.float32)
    chain_rows = lax.dynamic_slice_in_dim(chain_ids, row_start, row_count)
    chain_cols = lax.dynamic_slice_in_dim(chain_ids, col_start, col_count)
    pair_mask = valid_rows[:, None] * valid_cols[None, :]
    same_chain = (chain_rows[:, None] == chain_cols[None, :]).astype(jnp.float32)
    field = pair.astype(jnp.float32) + same_chain[:, :, None] * chain_bias
    first, second, gate_value = gated_inputs(field, in_weights[0], pair_mask)
    second_rows = lax.all_gather(second, "row", axis=0, tiled=True)
    block = second_rows
    summed = lax.psum_scatter(
        jnp.einsum("jkc,ikc->jic", block, first, preferred_element_type=jnp.float32).astype(
            jnp.bfloat16
        ),
        "col",
        scatter_dimension=0,
        tiled=True,
    ).astype(jnp.float32)
    summed = jnp.transpose(summed, (1, 0, 2))
    field = update(field, summed, gate_value, out_weights[0])
    first, second, gate_value = gated_inputs(field, in_weights[1], pair_mask)
    first_cols = lax.all_gather(first, "col", axis=1, tiled=True)
    block = first_cols
    summed = lax.psum_scatter(
        jnp.einsum("kic,kjc->ijc", block, second, preferred_element_type=jnp.float32).astype(
            jnp.bfloat16
        ),
        "row",
        scatter_dimension=0,
        tiled=True,
    ).astype(jnp.float32)
    field = update(field, summed, gate_value, out_weights[1])
    return field.astype(jnp.bfloat16)


def solution(mesh):
    return jax.shard_map(
        per_device,
        mesh=mesh,
        in_specs=(P("row", "col", None), P(), P(), P(), P(), P()),
        out_specs=P("row", "col", None),
        check_vma=False,
    )
```

profile of v0, /device:TPU:0, one launch (start us, length us, event | category | flops | bytes accessed | tf_op | source)
XLA Modules:
  0.0 396.2 jit_solution(9428536045843542747)
XLA Ops:
  9.7 2.3 fusion.39
  12.1 2.8 multiply_reduce_fusion.1
  15.0 1.9 fusion.41
  16.9 2.4 fusion.20
  20.4 1.6 copy.43
  22.0 103.4 %all-gather.3.cloned.1.call-done = bf16[320,80,128]{2,1,0:T(8,128)(2,1)} async-done(((bf16[40,80,128]{2,1,0:T(8,128)(2,1)}), bf16[320,80,128]{2,1,0:T(8,128)(2,1)}) %all-gather.3.cloned.1.call-update) | async-done | bytes 6553616 | tf_op jit(solution)/shard_map/all_gather | solution.py:50
  125.5 13.1 %copy.44 = bf16[320,80,128]{1,0,2:T(8,128)(2,1)} copy(bf16[320,80,128]{2,1,0:T(8,128)(2,1)} %all-gather.3.cloned.1.call-done) | data formatting | bytes 13107200 | tf_op jit(solution)/shard_map/all_gather | solution.py:50
  138.6 9.3 %convert_bitcast_fusion.1 = bf16[320,40,128]{0,1,2:T(8,128)(2,1)} fusion(bf16[40,80,128]{1,0,2:T(8,128)(2,1)S(1)} %copy.43, bf16[320,80,128]{1,0,2:T(8,128)(2,1)} %copy.44), kind=kOutput, calls=%fused_computation.1 | convolution fusion | flops 263782400 | bytes 10649600 | tf_op jit(solution)/shard_map/jkc,ikc->jic/dot_general | solution.py:53
  147.9 6.6 %copy.45 = bf16[320,40,128]{2,1,0:T(8,128)(2,1)} copy(bf16[320,40,128]{0,1,2:T(8,128)(2,1)} %convert_bitcast_fusion.1) | data formatting | bytes 6553600 | tf_op jit(solution)/shard_map/convert_element_type | solution.py:53
  154.8 36.8 %reduce-scatter.3.cloned.1.call-done = bf16[80,40,128]{2,1,0:T(8,128)(2,1)} async-done(((bf16[320,40,128]{2,1,0:T(8,128)(2,1)}), bf16[80,40,128]{2,1,0:T(8,128)(2,1)}) %reduce-scatter.3.cloned.1.call-update) | async-done | bytes 819216 | tf_op jit(solution)/shard_map/reduce_scatter | solution.py:52
  191.6 1.7 bitcast_reduce_fusion
  193.5 2.1 fusion.36
  196.8 2.6 fusion.61
  200.7 1.5 fusion.42
  202.2 2.4 fusion.5
  205.7 2.2 copy.51
  207.8 27.2 %all-gather.5.cloned.1.call-done = bf16[40,320,128]{2,1,0:T(8,128)(2,1)} async-done(((bf16[40,80,128]{2,1,0:T(8,128)(2,1)}), bf16[40,320,128]{2,1,0:T(8,128)(2,1)}) %all-gather.5.cloned.1.call-update) | async-done | bytes 3276816 | tf_op jit(solution)/shard_map/all_gather | solution.py:63
  235.1 6.2 %copy.52 = bf16[40,320,128]{1,0,2:T(8,128)(2,1)} copy(bf16[40,320,128]{2,1,0:T(8,128)(2,1)} %all-gather.5.cloned.1.call-done) | data formatting | bytes 6553600 | tf_op jit(solution)/shard_map/all_gather | solution.py:63
  241.2 7.9 %convert_bitcast_fusion = bf16[320,80,128]{0,1,2:T(8,128)(2,1)} fusion(bf16[40,80,128]{1,0,2:T(8,128)(2,1)} %copy.51, bf16[40,320,128]{1,0,2:T(8,128)(2,1)} %copy.52), kind=kOutput, calls=%fused_computation | convolution fusion | flops 265420800 | bytes 10649600 | tf_op jit(solution)/shard_map/kic,kjc->ijc/dot_general | solution.py:66
  249.1 11.5 %copy.53 = bf16[320,80,128]{2,1,0:T(8,128)(2,1)} copy(bf16[320,80,128]{0,1,2:T(8,128)(2,1)} %convert_bitcast_fusion) | data formatting | bytes 13107200 | tf_op jit(solution)/shard_map/convert_element_type | solution.py:66
  260.7 121.8 %reduce-scatter.5.cloned.1.call-done = bf16[40,80,128]{2,1,0:T(8,128)(2,1)} async-done(((bf16[320,80,128]{2,1,0:T(8,128)(2,1)}), bf16[40,80,128]{2,1,0:T(8,128)(2,1)}) %reduce-scatter.5.cloned.1.call-update) | async-done | bytes 819216 | tf_op jit(solution)/shard_map/reduce_scatter | solution.py:65
  382.5 1.6 convert_reduce_fusion
  384.1 2.3 fusion.2
  386.5 3.2 fusion.40
  (44 shorter events, 8.2 us)
Async XLA Ops:
  6.5 8.4 %copy-start.2 = (bf16[40,80,128]{2,1,0:T(8,128)(2,1)S(1)}, bf16[40,80,128]{2,1,0:T(8,128)(2,1)}, u32[]{:S(2)}) copy-start(bf16[40,80,128]{2,1,0:T(8,128)(2,1)} %param.6) | copy-start | bytes 2457604
  6.5 8.4 %copy-start.6 = (f32[128]{0:T(128)S(1)}, f32[128]{0:T(128)}, u32[]{:S(2)}) copy-start(f32[128]{0:T(128)} %param.9) | copy-start | bytes 1540
  6.5 8.4 %copy-start.5 = (bf16[2,128,640]{2,1,0:T(8,128)(2,1)S(1)}, bf16[2,128,640]{2,1,0:T(8,128)(2,1)}, u32[]{:S(2)}) copy-start(bf16[2,128,640]{2,1,0:T(8,128)(2,1)} %param.10) | copy-start | bytes 983044
  6.5 118.9 %all-gather.3.cloned.1.call-start = ((), (), s32[]{:S(2)}) async-start(), calls=%async_computation.2 | async-start | bytes 7372800 | tf_op jit(solution)/shard_map/all_gather | solution.py:50
  16.9 3.5 copy-start
  20.3 171.2 %reduce-scatter.3.cloned.1.call-start = ((), (), s32[]{:S(2)}) async-start(), calls=%async_computation.3 | async-start | bytes 4096000 | tf_op jit(solution)/shard_map/reduce_scatter | solution.py:52
  154.5 80.5 %all-gather.5.cloned.1.call-start = ((), (), s32[]{:S(2)}) async-start(), calls=%async_computation.4 | async-start | bytes 4096000 | tf_op jit(solution)/shard_map/all_gather | solution.py:63
  191.6 4.2 %copy-start.3 = (bf16[80,40,128]{2,1,0:T(8,128)(2,1)S(1)}, bf16[80,40,128]{2,1,0:T(8,128)(2,1)}, u32[]{:S(2)}) copy-start(bf16[80,40,128]{2,1,0:T(8,128)(2,1)} %reduce-scatter.3.cloned.1.call-done) | copy-start | bytes 2457604
  193.3 3.5 copy-start.7
  202.1 3.4 copy-start.1
  205.6 176.9 %reduce-scatter.5.cloned.1.call-start = ((), (), s32[]{:S(2)}) async-start(), calls=%async_computation.5 | async-start | bytes 7372800 | tf_op jit(solution)/shard_map/reduce_scatter | solution.py:65
  382.5 4.0 %copy-start.4 = (bf16[40,80,128]{2,1,0:T(8,128)(2,1)S(1)}, bf16[40,80,128]{2,1,0:T(8,128)(2,1)}, u32[]{:S(2)}) copy-start(bf16[40,80,128]{2,1,0:T(8,128)(2,1)} %reduce-scatter.5.cloned.1.call-done) | copy-start | bytes 2457604
Sparse Core Ops, SparseCore 0:
  20.5 104.9 all-gather.2
  154.7 36.8 reduce-scatter.2
  205.7 29.2 all-gather.4
  260.8 121.6 reduce-scatter.4
where the time goes:
time: 397 us; the launch traced here: 396 us
  waiting for transfers between devices  289 us (73%)
  local copies, waits for them, and re-layouts  45.1 us (11%)
  matrix products  26.3 us (7%)
  other arithmetic  21.7 us (5%)
  between operations  13.3 us (3%)
    reduce_scatter x1, waiting for transfers between devices, per_device(): lax.psum_scatter(jnp.einsum('kic,kjc->ijc', block, second, preferred_elem...  122 us
    all_gather x1, waiting for transfers between devices, per_device(): second_rows = lax.all_gather(second, 'row', axis=0, tiled=True)  103 us
    reduce_scatter x1, waiting for transfers between devices, per_device(): lax.psum_scatter(jnp.einsum('jkc,ikc->jic', block, first, preferred_eleme...  36.8 us
    all_gather x1, waiting for transfers between devices, per_device(): first_cols = lax.all_gather(first, 'col', axis=1, tiled=True)  27.2 us
    all_gather x1, local copies, waits for them, and re-layouts, per_device(): second_rows = lax.all_gather(second, 'row', axis=0, tiled=True)  13.1 us
    convert_element_type x1, local copies, waits for them, and re-layouts, per_device(): jnp.einsum('kic,kjc->ijc', block, second, preferred_element_type=jnp.floa...  11.5 us
    dot_general x1, matrix products, per_device(): jnp.einsum('jkc,ikc->jic', block, first, preferred_element_type=jnp.float32)  9.3 us
    reduce_sum x4, other arithmetic, layer_norm(): spread = jnp.mean(center * center, axis=-1, keepdims=True)  8.43 us
  transfers between devices with their start and end apart: 4, of which 4 were waited for; matrix products, arithmetic and copies ran while one was open for 1% of the time, Pallas kernels for 0%

commit v1 on v0

v1 whole, which is shorter than its diff:
```python
import functools

import jax
import jax.numpy as jnp
from jax import lax
from jax.experimental import pallas as pl
from jax.experimental.pallas import tpu as pltpu
from jax.sharding import PartitionSpec as P

LANES = 128
SUB = 8
F32 = jnp.float32
BF16 = jnp.bfloat16


def layer_norm(values, axis=-1):
    center = values - jnp.mean(values, axis=axis, keepdims=True)
    spread = jnp.mean(center * center, axis=axis, keepdims=True)
    return center * lax.rsqrt(spread + 1e-05)


def matmul(left, right, dims):
    return lax.dot_general(left, right, (dims, ((), ())), preferred_element_type=F32)


def identity(size, scale):
    row = lax.broadcasted_iota(jnp.int32, (size, size), 0)
    col = lax.broadcasted_iota(jnp.int32, (size, size), 1)
    return jnp.where(row == col, scale, 0.0).astype(BF16)


def column(row_ref):
    width = row_ref.shape[1]
    return jnp.broadcast_to(row_ref[...], (width, width)).T[:, 0:1]


def first_field(pair_ref, eye, bias_col, same, group, lanes):
    rows = pair_ref[group * lanes : (group + 1) * lanes, :]
    return matmul(eye, rows, ((1,), (1,))) + bias_col * same


def transposed(weights, scale):
    eye = identity(weights.shape[1], scale)
    return matmul(eye, weights, ((1,), (1,))).astype(BF16)


def interleaved(first, second, share):
    width = first.shape[1]
    both = jnp.concatenate([first, second], axis=1)
    row = lax.broadcasted_iota(jnp.int32, (2 * width, 1), 0)
    col = lax.broadcasted_iota(jnp.int32, (2 * width, 2 * width), 1)
    owner, place = row // (2 * share), row % (2 * share)
    source = owner * share + place % share + jnp.where(place >= share, width, 0)
    pick = jnp.where(col == source, 0.5, 0.0).astype(BF16)
    return matmul(pick, both, ((1,), (1,))).astype(BF16)


def load_in_weights(weights, share):
    width = weights.shape[0]
    blocks = [weights[:, k * width : (k + 1) * width] for k in range(5)]
    return (
        interleaved(blocks[0], blocks[2], share),
        interleaved(blocks[1], blocks[3], share),
        transposed(blocks[4], 0.5),
    )


def token_vectors(tokens, row_start, col_start, rows, cols):
    groups = rows // SUB
    wide = tokens.shape[1]
    many = jnp.broadcast_to(tokens.astype(F32), (SUB, wide))
    lane = lax.broadcasted_iota(jnp.int32, (1, SUB * cols), 1)
    at_row = jnp.zeros_like(lane)
    for step in range(1, SUB):
        at_row = at_row + jnp.where(lane >= step * cols, 1, 0)
    at_col = lane - at_row * cols
    key = lax.broadcasted_iota(jnp.int32, (LANES, SUB * cols), 0)
    pick_row = jnp.where(key == at_row, 1.0, 0.0).astype(BF16)
    pick_col = jnp.where(key == at_col, 1.0, 0.0).astype(BF16)

    def window(start):
        return pltpu.roll(many, wide - start, 1)[:, :LANES]

    by_col = matmul(window(col_start).astype(BF16), pick_col, ((1,), (0,)))[0:1]
    windows = [window(row_start + group * SUB)[0:1] for group in range(groups)]
    windows.append(jnp.zeros((-groups % SUB, LANES), F32))
    by_row = matmul(jnp.concatenate(windows, axis=0).astype(BF16), pick_row, ((1,), (0,)))
    by_row = by_row.astype(jnp.int32)
    by_col = by_col.astype(jnp.int32)
    masks = (by_row & by_col & 1).astype(F32)
    sames = jnp.where((by_row >> 1) == (by_col >> 1), 1.0, 0.0)
    return masks, sames


def send_inputs(field, mask, in_t, group, share, sent_ref, gate_ref):
    width = field.shape[0]
    lanes = field.shape[1]
    pieces = lanes // LANES
    normed = layer_norm(field, 0).astype(BF16)
    gates_t, values_t, out_gate_t = in_t
    gates = jnp.tanh(matmul(gates_t, normed, ((1,), (0,))))
    values = matmul(values_t, normed, ((1,), (0,)))
    sent = (gates * values + values) * mask
    gate = jnp.tanh(matmul(out_gate_t, normed, ((1,), (0,))))
    gate_ref[:, group * lanes : (group + 1) * lanes] = gate
    for owner in range(width // share):
        block = sent[owner * 2 * share : (owner + 1) * 2 * share]
        lines = [block[:, piece * LANES : (piece + 1) * LANES] for piece in range(pieces)]
        sent_ref[owner, group] = jnp.concatenate(lines, axis=0).astype(BF16)


def start_kernel(share, rows, cols, mask_hbm, chain_hbm, pair_hbm, bias_hbm, w_hbm,
                 sent_hbm, gate_hbm, mask_same_hbm, sent_ref, gate_ref, mask_same_ref,
                 pair_ref, w_ref, bias_ref, valid_ref, chain_ref, sems):
    lanes = SUB * cols
    groups = rows // SUB
    width = pair_ref.shape[1]
    count = mask_hbm.shape[0]
    copies = [
        pltpu.make_async_copy(mask_hbm, valid_ref.at[0], sems.at[0]),
        pltpu.make_async_copy(chain_hbm, chain_ref.at[0], sems.at[1]),
        pltpu.make_async_copy(w_hbm.at[0], w_ref, sems.at[2]),
        pltpu.make_async_copy(bias_hbm, bias_ref.at[0], sems.at[3]),
    ]
    for group in range(groups):
        at = pl.ds(group * lanes, lanes)
        copies.append(pltpu.make_async_copy(pair_hbm.at[at], pair_ref.at[at], sems.at[4 + group]))
    for copy in copies:
        copy.start()
    eye = identity(width, 1.0)
    copies[0].wait()
    copies[1].wait()
    row_start = lax.axis_index("row") * rows
    col_start = lax.axis_index("col") * cols
    tokens = chain_ref[...] * 2 + valid_ref[...]
    tokens = jnp.concatenate([tokens, jnp.zeros((1, -count % LANES), jnp.int32)], axis=1)
    masks, sames = token_vectors(tokens, row_start, col_start, rows, cols)
    copies[3].wait()
    bias_col = column(bias_ref)
    copies[2].wait()
    in_t = load_in_weights(w_ref[...], share)
    outs = []
    for group in range(groups):
        copies[4 + group].wait()
        at = slice(group * lanes, (group + 1) * lanes)
        mask = masks[group : group + 1]
        same = sames[group : group + 1]
        field = first_field(pair_ref, eye, bias_col, same, group, lanes)
        mask_same_ref[:, at] = jnp.concatenate([mask, same], axis=0)
        send_inputs(field, mask, in_t, group, share, sent_ref, gate_ref)
        at = pl.ds(group * lanes, lanes)
        sem = sems.at[4 + groups + group]
        outs.append(pltpu.make_async_copy(gate_ref.at[:, at], gate_hbm.at[:, at], sem))
        sem = sems.at[4 + 2 * groups + group]
        outs.append(pltpu.make_async_copy(sent_ref.at[:, group], sent_hbm.at[:, group], sem))
        outs[-2].start()
        outs[-1].start()
    outs.append(pltpu.make_async_copy(mask_same_ref, mask_same_hbm, sems.at[4 + 3 * groups]))
    outs[-1].start()
    for copy in outs:
        copy.wait()


def updated(wide, field, gate, out_t, group, line):
    width, lanes = field.shape
    pieces = lanes // LANES
    parts = []
    for piece in range(pieces):
        parts.append(wide[pl.ds(group * pieces + piece, width, stride=line), :])
    summed = jnp.concatenate(parts, axis=1)
    normed = layer_norm(summed, 0).astype(BF16)
    output = matmul(out_t, normed, ((1,), (0,)))
    return field + (gate * output + output)


def middle_kernel(share, rows, cols, line, mask_same_ref, got_ref, pair_ref, bias_ref, gate_in,
                  wo_ref, w_ref, sent_ref, gate_ref, field_ref, wide):
    lanes = SUB * cols
    width = pair_ref.shape[1]
    in_t = load_in_weights(w_ref[1], share)
    out_t = transposed(wo_ref[0], 0.5)
    eye = identity(width, 1.0)
    bias_col = column(bias_ref)
    wide[...] = got_ref[...].astype(F32)
    for group in range(rows // SUB):
        at = slice(group * lanes, (group + 1) * lanes)
        field = first_field(pair_ref, eye, bias_col, mask_same_ref[1:2, at], group, lanes)
        field = updated(wide, field, gate_in[:, at], out_t, group, line)
        field_ref[:, at] = field
        send_inputs(field, mask_same_ref[0:1, at], in_t, group, share, sent_ref, gate_ref)


def end_kernel(rows, cols, line, got_ref, field_in, gate_in, wo_ref, out_ref, wide):
    lanes = SUB * cols
    out_t = transposed(wo_ref[1], 0.5)
    wide[...] = got_ref[...].astype(F32)
    for group in range(rows // SUB):
        at = slice(group * lanes, (group + 1) * lanes)
        field = updated(wide, field_in[:, at], gate_in[:, at], out_t, group, line)
        out_ref[at, :] = field.T.astype(BF16)


def moved(source, moves, count):
    shape = None
    lane = None
    targets = [[] for _ in range(count)]
    for row, begin, length, target in moves:
        shift = (target - begin) % LANES
        while length > 0:
            size = min(length, LANES - begin % LANES, LANES - target % LANES)
            targets[target // LANES].append((target % LANES, row, begin // LANES, shift))
            begin, target, length = begin + size, target + size, length - size
    rolled = {}
    registers = []
    for pieces in targets:
        value = None
        for start, row, register, shift in sorted(pieces, key=lambda piece: piece[0]):
            key = (row, register, shift)
            if key not in rolled:
                tile = source(row, register)
                rolled[key] = pltpu.roll(tile, shift, 1) if shift else tile
            if value is None:
                value = rolled[key]
            else:
                if lane is None:
                    shape = value.shape
                    lane = lax.broadcasted_iota(jnp.int32, shape, 1)
                value = jnp.where(lane < start, value, rolled[key])
        registers.append(value)
    return registers


def wide_steps(tiles):
    place_step = tiles + 1 - tiles % 2
    return place_step, SUB * place_step + 1


def stacked(low, high):
    return jnp.concatenate([low, high], axis=0).astype(BF16)


def triangle_kernel(direction, share, rows, cols, row_devices, col_devices, line, got_ref, sent_ref,
                    wide, left_ref, right_ref, even_ref, result_ref, packed):
    groups = rows // SUB
    pieces = SUB * cols // LANES
    total = row_devices * rows
    blocks = -(-total // LANES)
    pairs = -(-groups // 2)
    rest = total - (blocks - 1) * LANES
    tail = lax.broadcasted_iota(jnp.int32, (2 * SUB, LANES), 1) < rest
    place_step, row_step = wide_steps(col_devices * groups * pieces)

    def spot(tile):
        device, number = divmod(tile, groups * pieces)
        col, row = divmod(device, row_devices)
        return row * row_step + col * groups * pieces + number

    for unit in range(got_ref.shape[0] // (2 * SUB)):
        both = got_ref[unit * 2 * SUB : (unit + 1) * 2 * SUB, :].astype(F32)
        for half in range(2):
            at = pl.ds(spot(2 * unit + half), SUB, stride=place_step)
            wide[at, :] = both[half * SUB : (half + 1) * SUB]

    def loaded(place, group, col, piece):
        if group >= groups:
            return jnp.zeros((SUB, LANES), F32)
        start = place * place_step + (col * groups + group) * pieces + piece
        return wide[pl.ds(start, row_devices, stride=row_step), :]

    for channel in range(share):
        spare = channel % 2
        for is_right, place in ((False, channel), (True, share + channel)):
            for pair in range(pairs):
                tiles = {}
                for col in range(col_devices):
                    for piece in range(pieces):
                        tiles[col, piece] = stacked(
                            loaded(place, 2 * pair, col, piece), loaded(place, 2 * pair + 1, col, piece)
                        )
                for step in range(SUB):
                    moves = [(col, step * cols, cols, col * cols) for col in range(col_devices)]
                    registers = moved(lambda col, piece: tiles[col, piece], moves, blocks)
                    registers[-1] = jnp.where(tail, registers[-1], jnp.zeros_like(registers[-1]))
                    for block in range(blocks):
                        if is_right and direction == 0:
                            both = registers[block].astype(F32)
                            for half in range(2):
                                group = 2 * pair + half
                                if group < groups:
                                    at = pl.ds(group * SUB + step, row_devices, stride=rows)
                                    even_ref[spare, block, at, :] = both[half * SUB : (half + 1) * SUB]
                        else:
                            target = right_ref if is_right else left_ref
                            start = (pair * SUB + step) * 2 * SUB
                            target[spare, start : start + 2 * SUB, block * LANES : (block + 1) * LANES] = (
                                registers[block]
                            )
        if direction == 0:
            right = [even_ref[spare, block].astype(BF16) for block in range(blocks)]
            right = jnp.concatenate(right, axis=1)
            summed = matmul(left_ref[spare], right, ((1,), (1,)))
            for block in range(blocks):
                size = min(LANES, total - block * LANES)
                part = summed[:, block * LANES : block * LANES + size].astype(BF16)
                result_ref[spare, block, :, 0:size] = part
        else:
            summed = matmul(left_ref[spare], right_ref[spare], ((0,), (0,)))
            for block in range(blocks):
                result_ref[spare, block] = summed[:, block * LANES : (block + 1) * LANES]

        def result_at(pair, step, block):
            if direction == 0:
                start = (pair * SUB + step) * 2 * SUB
                return result_ref[spare, block, start : start + 2 * SUB, :]
            halves = []
            for group in (2 * pair, 2 * pair + 1):
                if group < groups:
                    at = pl.ds(group * SUB + step, row_devices, stride=rows)
                    halves.append(result_ref[spare, block, at, :])
                else:
                    halves.append(jnp.zeros((SUB, LANES), F32))
            return stacked(*halves)

        for pair in range(pairs):
            tiles = {}
            for step in range(SUB):
                for block in range(blocks):
                    tiles[step, block] = result_at(pair, step, block)
            for col in range(col_devices):
                moves = [(step, col * cols, cols, step * cols) for step in range(SUB)]
                registers = moved(lambda step, block: tiles[step, block], moves, pieces)
                for piece in range(pieces):
                    both = registers[piece].astype(F32)
                    for half in range(2):
                        group = 2 * pair + half
                        if group < groups:
                            start = (col * row_devices * share + channel) * line + group * pieces + piece
                            packed[pl.ds(start, row_devices, stride=share * line), :] = (
                                both[half * SUB : (half + 1) * SUB]
                            )
    sent_ref[...] = packed[...].astype(BF16)


def by_channels(pair, token_mask, chain_ids, chain_bias, in_weights, out_weights, row_devices, col_devices):
    rows, cols, width = pair.shape
    devices = row_devices * col_devices
    share = width // devices
    lanes = SUB * cols
    pieces = lanes // LANES
    groups = rows // SUB
    chunk = groups * pieces * SUB
    spots = rows * cols
    line = -(-groups * pieces * share // SUB) * SUB // share
    total = row_devices * rows
    blocks = -(-total // LANES)
    tall = -(-groups // 2) * 2 * SUB * row_devices
    params = pltpu.CompilerParams(vmem_limit_bytes=40 * 1024 * 1024)
    whole = pl.BlockSpec(memory_space=pltpu.VMEM)
    far = pl.BlockSpec(memory_space=pltpu.HBM)

    sent_shape = jax.ShapeDtypeStruct((devices, groups, pieces * SUB, LANES), BF16)
    sum_shape = jax.ShapeDtypeStruct((devices * share * line, LANES), BF16)
    state_shape = jax.ShapeDtypeStruct((width, spots), F32)
    flags_shape = jax.ShapeDtypeStruct((2, spots), F32)

    def exchange(array, rows):
        split = array.reshape(devices, rows, LANES)
        return lax.all_to_all(split, ("col", "row"), 0, 0, tiled=True).reshape(devices * rows, LANES)

    def triangle(direction, sent):
        result_rows, result_type = (tall, BF16) if direction == 0 else (blocks * LANES, F32)
        wide_rows = row_devices * wide_steps(col_devices * groups * pieces)[1]
        summed = pl.pallas_call(
            functools.partial(
                triangle_kernel, direction, share, rows, cols, row_devices, col_devices, line
            ),
            out_shape=sum_shape,
            in_specs=[whole],
            out_specs=whole,
            scratch_shapes=[
                pltpu.VMEM((-(-wide_rows // SUB) * SUB, LANES), F32),
                pltpu.VMEM((2, tall, blocks * LANES), BF16),
                pltpu.VMEM((2, tall, blocks * LANES), BF16),
                pltpu.VMEM((2, blocks, total, LANES), F32),
                pltpu.VMEM((2, blocks, result_rows, LANES), result_type),
                pltpu.VMEM(sum_shape.shape, F32),
            ],
            compiler_params=params,
            name="triangle",
        )(exchange(sent, chunk))
        return exchange(summed, share * line)

    flat_pair = pair.reshape(spots, width)
    flat_bias = chain_bias.reshape(1, width)
    sent, gate, flags = pl.pallas_call(
        functools.partial(start_kernel, share, rows, cols),
        out_shape=[sent_shape, state_shape, flags_shape],
        in_specs=[far] * 5,
        out_specs=[far] * 3,
        scratch_shapes=[
            pltpu.VMEM(sent_shape.shape, BF16),
            pltpu.VMEM(state_shape.shape, F32),
            pltpu.VMEM(flags_shape.shape, F32),
            pltpu.VMEM((spots, width), BF16),
            pltpu.VMEM(in_weights.shape[1:], BF16),
            pltpu.VMEM((1, width), F32),
            pltpu.VMEM((1,) + token_mask.shape, jnp.int32),
            pltpu.VMEM((1,) + chain_ids.shape, jnp.int32),
            pltpu.SemaphoreType.DMA((5 + 3 * groups,)),
        ],
        compiler_params=pltpu.CompilerParams(vmem_limit_bytes=60 * 1024 * 1024),
        name="start",
    )(token_mask, chain_ids, flat_pair, chain_bias, in_weights)
    got = triangle(0, sent)
    sent, gate, field = pl.pallas_call(
        functools.partial(middle_kernel, share, rows, cols, line),
        out_shape=[sent_shape, state_shape, state_shape],
        in_specs=[whole] * 7,
        out_specs=[whole] * 3,
        scratch_shapes=[pltpu.VMEM(sum_shape.shape, F32)],
        compiler_params=params,
        name="middle",
    )(flags, got, flat_pair, flat_bias, gate, out_weights, in_weights)
    got = triangle(1, sent)
    out = pl.pallas_call(
        functools.partial(end_kernel, rows, cols, line),
        out_shape=jax.ShapeDtypeStruct((spots, width), BF16),
        in_specs=[whole] * 4,
        out_specs=whole,
        scratch_shapes=[pltpu.VMEM(sum_shape.shape, F32)],
        compiler_params=params,
        name="end",
    )(got, field, gate, out_weights)
    return out.reshape(pair.shape)


def gated_inputs(field, weights, pair_mask):
    width = weights.shape[0]
    normed = layer_norm(field).astype(BF16)
    projected = jnp.einsum("ijc,cd->ijd", normed, weights, preferred_element_type=F32)
    first = (
        jax.nn.sigmoid(projected[..., :width])
        * projected[..., width : 2 * width]
        * pair_mask[:, :, None]
    ).astype(BF16)
    second = (
        jax.nn.sigmoid(projected[..., 2 * width : 3 * width])
        * projected[..., 3 * width : 4 * width]
        * pair_mask[:, :, None]
    ).astype(BF16)
    gate_value = jax.nn.sigmoid(projected[..., 4 * width :])
    return (first, second, gate_value)


def update(field, summed, gate_value, weights):
    normed_sum = layer_norm(summed).astype(BF16)
    output = jnp.einsum("ijc,cd->ijd", normed_sum, weights, preferred_element_type=F32)
    return field + gate_value * output


def by_blocks(pair, token_mask, chain_ids, chain_bias, in_weights, out_weights):
    row_count = pair.shape[0]
    col_count = pair.shape[1]
    row_start = lax.axis_index("row") * row_count
    col_start = lax.axis_index("col") * col_count
    valid_rows = lax.dynamic_slice_in_dim(token_mask, row_start, row_count).astype(F32)
    valid_cols = lax.dynamic_slice_in_dim(token_mask, col_start, col_count).astype(F32)
    chain_rows = lax.dynamic_slice_in_dim(chain_ids, row_start, row_count)
    chain_cols = lax.dynamic_slice_in_dim(chain_ids, col_start, col_count)
    pair_mask = valid_rows[:, None] * valid_cols[None, :]
    same_chain = (chain_rows[:, None] == chain_cols[None, :]).astype(F32)
    field = pair.astype(F32) + same_chain[:, :, None] * chain_bias
    first, second, gate_value = gated_inputs(field, in_weights[0], pair_mask)
    second_rows = lax.all_gather(second, "row", axis=0, tiled=True)
    part = jnp.einsum("jkc,ikc->jic", second_rows, first, preferred_element_type=F32).astype(BF16)
    summed = lax.psum_scatter(part, "col", scatter_dimension=0, tiled=True).astype(F32)
    summed = jnp.transpose(summed, (1, 0, 2))
    field = update(field, summed, gate_value, out_weights[0])
    first, second, gate_value = gated_inputs(field, in_weights[1], pair_mask)
    first_cols = lax.all_gather(first, "col", axis=1, tiled=True)
    part = jnp.einsum("kic,kjc->ijc", first_cols, second, preferred_element_type=F32).astype(BF16)
    summed = lax.psum_scatter(part, "row", scatter_dimension=0, tiled=True).astype(F32)
    field = update(field, summed, gate_value, out_weights[1])
    return field.astype(BF16)


def solution(mesh):
    row_devices, col_devices = mesh.shape["row"], mesh.shape["col"]

    def per_device(pair, *rest):
        rows, cols, width = pair.shape
        devices = row_devices * col_devices
        fits = (
            width % devices == 0
            and 2 * (width // devices) == SUB
            and row_devices == SUB
            and rows % SUB == 0
            and (SUB * cols) % LANES == 0
            and max(rows, cols) <= LANES
        )
        if fits:
            return by_channels(pair, *rest, row_devices, col_devices)
        return by_blocks(pair, *rest)

    return jax.shard_map(
        per_device,
        mesh=mesh,
        in_specs=(P("row", "col", None), P(), P(), P(), P(), P()),
        out_specs=P("row", "col", None),
        check_vma=False,
    )
```

time: 397 us -> 159 us (0.40)
  waiting for transfers between devices: 289 us -> 0 us
  blocking collectives: 0 us -> 141 us
  local copies, waits for them, and re-layouts: 45.1 us -> 0.03 us
  matrix products: 26.3 us -> 0 us
  other arithmetic: 21.7 us -> 0 us
  Pallas kernels: 0 us -> 17.7 us
  between operations: 13.3 us -> 0.08 us
    reduce_scatter x2 -> x0, waiting for transfers between devices: 159 us -> none  [the longest x1 122 us: per_device(): lax.psum_scatter(jnp.einsum('kic,kjc->ijc', block, second, preferred_elem...]
    all_to_all x0 -> x4, blocking collectives: none -> 141 us  [exchange(): lax.all_to_all(split, ('col', 'row'), 0, 0, tiled=True)]
    all_gather x2 -> x0, waiting for transfers between devices: 131 us -> none  [the longest x1 103 us: per_device(): second_rows = lax.all_gather(second, 'row', axis=0, tiled=True)]
    dot_general x6 -> x0, matrix products: 26.3 us -> none  [the longest x1 9.3 us: per_device(): jnp.einsum('jkc,ikc->jic', block, first, preferred_element_type=jnp.float32)]
    convert_element_type x4 -> x0, local copies, waits for them, and re-layouts: 21.9 us -> none  [the longest x1 11.5 us: per_device(): jnp.einsum('kic,kjc->ijc', block, second, preferred_element_type=jnp.floa...]
    all_gather x2 -> x0, local copies, waits for them, and re-layouts: 19.3 us -> none  [the longest x1 13.1 us: per_device(): second_rows = lax.all_gather(second, 'row', axis=0, tiled=True)]
    pallas_call x0 -> x5, Pallas kernels: none -> 17.7 us  [the longest x2 7.21 us: triangle(): pl.pallas_call(functools.partial(triangle_kernel, direction, share, rows,...]
    reduce_sum x7 -> x0, other arithmetic: 14.1 us -> none  [the longest x4 8.43 us: layer_norm(): spread = jnp.mean(center * center, axis=-1, keepdims=True)]
  transfers between devices with their start and end apart: 4 -> 0, of which waited for: 4 -> 0; matrix products, arithmetic and copies ran while one was open for 1% -> 0% of each run, Pallas kernels for 0% -> 0%
where the time goes in v1:
time: 159 us
  blocking collectives  141 us (89%)
  Pallas kernels  17.7 us (11%)
    all_to_all x4, blocking collectives, exchange(): lax.all_to_all(split, ('col', 'row'), 0, 0, tiled=True)  141 us
    pallas_call x2, Pallas kernels, triangle(): pl.pallas_call(functools.partial(triangle_kernel, direction, share, rows,...  7.21 us
    pallas_call x1, Pallas kernels, by_channels(): pl.pallas_call(functools.partial(start_kernel, share, rows, cols), out_sh...  5.47 us

profile of v1, /device:TPU:0, one launch (start us, length us, event | category | flops | bytes accessed | tf_op | source)
XLA Modules:
  0.0 158.5 jit_solution(16202713094594838576)
XLA Ops:
  0.0 5.5 %start.1 = (bf16[32,5,40,128]{3,2,1,0:T(8,128)(2,1)}, f32[128,3200]{1,0:T(8,128)}, f32[2,3200]{1,0:T(2,128)}) custom-call(s32[320]{0:T(512)} %mask_hbm.1, s32[320]{0:T(512)} %chain_hbm.1, bf16[3200,128]{1,0:T(8,128)(2,1)} %bitcast.17, f32[128]{0:T(128)} %bias_hbm.1, bf16[2,128,640]{2,1,0:T(8,128)(2,1)} %w_ref.1), custom_call_target="tpu_custom_call" | custom-call | tf_op jit(solution)/shard_map/start/pallas_call | solution.py:395
  5.5 47.5 %all_to_all.20 = bf16[32,200,128]{2,1,0:T(8,128)(2,1)S(1)} all-to-all(bf16[32,200,128]{2,1,0:T(8,128)(2,1)} %bitcast.21), channel_id=1, replica_groups=mesh['row'=8,'col'=4] {'col','row'}, dimensions={0} | all-to-all | bytes 3276800 | tf_op jit(solution)/shard_map/all_to_all | solution.py:368
  53.0 0.0 copy-start
  53.0 0.0 copy-start.1
  53.0 0.0 copy-start.2
  53.0 0.0 copy-start.3
  53.0 0.0 copy-start.4
  53.0 0.0 copy-start.5
  53.1 3.3 %triangle.2 = bf16[3328,128]{1,0:T(8,128)(2,1)S(1)} custom-call(bf16[6400,128]{1,0:T(8,128)(2,1)S(1)} %bitcast.11), custom_call_target="tpu_custom_call" | custom-call | tf_op jit(solution)/shard_map/triangle/pallas_call | solution.py:373
  56.4 25.5 %all_to_all.21 = bf16[32,104,128]{2,1,0:T(8,128)(2,1)S(1)} all-to-all(bf16[32,104,128]{2,1,0:T(8,128)(2,1)S(1)} %bitcast.15), channel_id=1, replica_groups=mesh['row'=8,'col'=4] {'col','row'}, dimensions={0} | all-to-all | bytes 1703936 | tf_op jit(solution)/shard_map/all_to_all | solution.py:368
  81.8 0.0 copy-done
  81.8 0.0 copy-done.1
  81.8 0.0 copy-done.2
  81.8 0.0 copy-done.3
  81.9 0.0 copy-done.4
  81.9 0.0 copy-done.5
  81.9 3.2 %middle.1 = (bf16[32,5,40,128]{3,2,1,0:T(8,128)(2,1)S(1)}, f32[128,3200]{1,0:T(8,128)S(1)}, f32[128,3200]{1,0:T(8,128)S(1)}) custom-call(f32[2,3200]{1,0:T(2,128)S(1)} %copy-done.4, bf16[3328,128]{1,0:T(8,128)(2,1)S(1)} %bitcast.14, bf16[3200,128]{1,0:T(8,128)(2,1)S(1)} %bitcast.18, f32[1,128]{1,0:T(1,128)S(1)} %bitcast.20, f32[128,3200]{1,0:T(8,128)S(1)} %copy-done.1, ...), custom_call_target="tpu_custom_call" | custom-call | tf_op jit(solution)/shard_map/middle/pallas_call | solution.py:415
  85.1 42.3 %all_to_all.22 = bf16[32,200,128]{2,1,0:T(8,128)(2,1)S(1)} all-to-all(bf16[32,200,128]{2,1,0:T(8,128)(2,1)S(1)} %bitcast.19), channel_id=1, replica_groups=mesh['row'=8,'col'=4] {'col','row'}, dimensions={0} | all-to-all | bytes 3276800 | tf_op jit(solution)/shard_map/all_to_all | solution.py:368
  127.4 3.9 %triangle.3 = bf16[3328,128]{1,0:T(8,128)(2,1)S(1)} custom-call(bf16[6400,128]{1,0:T(8,128)(2,1)S(1)} %bitcast.12), custom_call_target="tpu_custom_call" | custom-call | tf_op jit(solution)/shard_map/triangle/pallas_call | solution.py:373
  131.3 25.4 %all_to_all.23 = bf16[32,104,128]{2,1,0:T(8,128)(2,1)S(1)} all-to-all(bf16[32,104,128]{2,1,0:T(8,128)(2,1)S(1)} %bitcast.16), channel_id=1, replica_groups=mesh['row'=8,'col'=4] {'col','row'}, dimensions={0} | all-to-all | bytes 1703936 | tf_op jit(solution)/shard_map/all_to_all | solution.py:368
  156.7 1.8 %end.1 = bf16[3200,128]{1,0:T(8,128)(2,1)} custom-call(bf16[3328,128]{1,0:T(8,128)(2,1)S(1)} %bitcast.13, f32[128,3200]{1,0:T(8,128)S(1)} %get-tuple-element.15.field_in, f32[128,3200]{1,0:T(8,128)S(1)} %get-tuple-element.16.gate_in, bf16[2,128,128]{2,1,0:T(8,128)(2,1)S(1)} %copy-done.3), custom_call_target="tpu_custom_call" | custom-call | tf_op jit(solution)/shard_map/end/pallas_call | solution.py:425
Async XLA Ops:
  53.0 28.8 %copy-start = (bf16[40,80,128]{2,1,0:T(8,128)(2,1)S(1)}, bf16[40,80,128]{2,1,0:T(8,128)(2,1)}, u32[]{:S(2)}) copy-start(bf16[40,80,128]{2,1,0:T(8,128)(2,1)} %param.6) | copy-start | bytes 2457604
  53.0 28.8 %copy-start.1 = (f32[128,3200]{1,0:T(8,128)S(1)}, f32[128,3200]{1,0:T(8,128)}, u32[]{:S(2)}) copy-start(f32[128,3200]{1,0:T(8,128)} %get-tuple-element.13.gate_in) | copy-start | bytes 4915204
  53.0 28.8 %copy-start.2 = (bf16[2,128,640]{2,1,0:T(8,128)(2,1)S(1)}, bf16[2,128,640]{2,1,0:T(8,128)(2,1)}, u32[]{:S(2)}) copy-start(bf16[2,128,640]{2,1,0:T(8,128)(2,1)} %w_ref.1) | copy-start | bytes 983044
  53.0 28.8 %copy-start.3 = (bf16[2,128,128]{2,1,0:T(8,128)(2,1)S(1)}, bf16[2,128,128]{2,1,0:T(8,128)(2,1)}, u32[]{:S(2)}) copy-start(bf16[2,128,128]{2,1,0:T(8,128)(2,1)} %wo_ref.3) | copy-start | bytes 196612
  53.0 28.8 %copy-start.4 = (f32[2,3200]{1,0:T(2,128)S(1)}, f32[2,3200]{1,0:T(2,128)}, u32[]{:S(2)}) copy-start(f32[2,3200]{1,0:T(2,128)} %get-tuple-element.11.mask_same_ref) | copy-start | bytes 76804
  53.0 28.8 %copy-start.5 = (f32[128]{0:T(128)S(1)}, f32[128]{0:T(128)}, u32[]{:S(2)}) copy-start(f32[128]{0:T(128)} %bias_hbm.1) | copy-start | bytes 1540

commit v2 on v1

--- a/solution.py
+++ b/solution.py
@@ -32,11 +32,6 @@
 def column(row_ref):
     width = row_ref.shape[1]
     return jnp.broadcast_to(row_ref[...], (width, width)).T[:, 0:1]
-
-
-def first_field(pair_ref, eye, bias_col, same, group, lanes):
-    rows = pair_ref[group * lanes : (group + 1) * lanes, :]
-    return matmul(eye, rows, ((1,), (1,))) + bias_col * same
 
 
 def transposed(weights, scale):
@@ -92,112 +87,143 @@
     return masks, sames
 
 
-def send_inputs(field, mask, in_t, group, share, sent_ref, gate_ref):
-    width = field.shape[0]
-    lanes = field.shape[1]
-    pieces = lanes // LANES
+def staged(count, stages):
+    held = {}
+    for step in range(count + len(stages) - 1):
+        for number, stage in enumerate(stages):
+            item = step - number
+            if 0 <= item < count:
+                held[item] = stage(item, held.get(item))
+
+
+def projected(field, in_t):
     normed = layer_norm(field, 0).astype(BF16)
-    gates_t, values_t, out_gate_t = in_t
-    gates = jnp.tanh(matmul(gates_t, normed, ((1,), (0,))))
-    values = matmul(values_t, normed, ((1,), (0,)))
-    sent = (gates * values + values) * mask
-    gate = jnp.tanh(matmul(out_gate_t, normed, ((1,), (0,))))
-    gate_ref[:, group * lanes : (group + 1) * lanes] = gate
+    return [matmul(weights, normed, ((1,), (0,))) for weights in in_t]
+
+
+def gated(products, mask, group, share, sent_ref, gate_ref):
+    gates, values, gate = products
+    width, lanes = gate.shape
+    sent = (jnp.tanh(gates) * values + values) * mask
     for owner in range(width // share):
         block = sent[owner * 2 * share : (owner + 1) * 2 * share]
-        lines = [block[:, piece * LANES : (piece + 1) * LANES] for piece in range(pieces)]
+        lines = [block[:, at : at + LANES] for at in range(0, lanes, LANES)]
         sent_ref[owner, group] = jnp.concatenate(lines, axis=0).astype(BF16)
-
-
-def start_kernel(share, rows, cols, mask_hbm, chain_hbm, pair_hbm, bias_hbm, w_hbm,
-                 sent_hbm, gate_hbm, mask_same_hbm, sent_ref, gate_ref, mask_same_ref,
+    gate_ref[:, group * lanes : (group + 1) * lanes] = jnp.tanh(gate)
+
+
+def start_kernel(share, rows, cols, valid_hbm, chain_hbm, pair_hbm, bias_hbm, w_hbm,
+                 sent_hbm, gate_hbm, field_hbm, mask_hbm, sent_ref, gate_ref, field_ref, mask_ref,
                  pair_ref, w_ref, bias_ref, valid_ref, chain_ref, sems):
     lanes = SUB * cols
     groups = rows // SUB
     width = pair_ref.shape[1]
-    count = mask_hbm.shape[0]
-    copies = [
-        pltpu.make_async_copy(mask_hbm, valid_ref.at[0], sems.at[0]),
-        pltpu.make_async_copy(chain_hbm, chain_ref.at[0], sems.at[1]),
-        pltpu.make_async_copy(w_hbm.at[0], w_ref, sems.at[2]),
-        pltpu.make_async_copy(bias_hbm, bias_ref.at[0], sems.at[3]),
-    ]
-    for group in range(groups):
-        at = pl.ds(group * lanes, lanes)
-        copies.append(pltpu.make_async_copy(pair_hbm.at[at], pair_ref.at[at], sems.at[4 + group]))
-    for copy in copies:
-        copy.start()
+    count = valid_hbm.shape[0]
+    started = []
+
+    def copy(near, far):
+        started.append(pltpu.make_async_copy(near, far, sems.at[len(started)]))
+        started[-1].start()
+
+    copy(valid_hbm, valid_ref.at[0])
+    copy(chain_hbm, chain_ref.at[0])
+    copy(w_hbm.at[0], w_ref)
+    copy(bias_hbm, bias_ref.at[0])
+    copy(pair_hbm, pair_ref)
+    arriving = len(started)
     eye = identity(width, 1.0)
-    copies[0].wait()
-    copies[1].wait()
     row_start = lax.axis_index("row") * rows
     col_start = lax.axis_index("col") * cols
+    for number in range(arriving):
+        started[number].wait()
     tokens = chain_ref[...] * 2 + valid_ref[...]
     tokens = jnp.concatenate([tokens, jnp.zeros((1, -count % LANES), jnp.int32)], axis=1)
     masks, sames = token_vectors(tokens, row_start, col_start, rows, cols)
-    copies[3].wait()
+    in_t = load_in_weights(w_ref[...], share)
     bias_col = column(bias_ref)
-    copies[2].wait()
-    in_t = load_in_weights(w_ref[...], share)
-    outs = []
-    for group in range(groups):
-        copies[4 + group].wait()
+    early = groups // 2 * lanes
+
+    def make_field(group, _):
         at = slice(group * lanes, (group + 1) * lanes)
-        mask = masks[group : group + 1]
-        same = sames[group : group + 1]
-        field = first_field(pair_ref, eye, bias_col, same, group, lanes)
-        mask_same_ref[:, at] = jnp.concatenate([mask, same], axis=0)
-        send_inputs(field, mask, in_t, group, share, sent_ref, gate_ref)
-        at = pl.ds(group * lanes, lanes)
-        sem = sems.at[4 + groups + group]
-        outs.append(pltpu.make_async_copy(gate_ref.at[:, at], gate_hbm.at[:, at], sem))
-        sem = sems.at[4 + 2 * groups + group]
-        outs.append(pltpu.make_async_copy(sent_ref.at[:, group], sent_hbm.at[:, group], sem))
-        outs[-2].start()
-        outs[-1].start()
-    outs.append(pltpu.make_async_copy(mask_same_ref, mask_same_hbm, sems.at[4 + 3 * groups]))
-    outs[-1].start()
-    for copy in outs:
-        copy.wait()
-
-
-def updated(wide, field, gate, out_t, group, line):
-    width, lanes = field.shape
+        field = matmul(eye, pair_ref[at, :], ((1,), (1,))) + bias_col * sames[group : group + 1]
+        field_ref[:, at] = field
+        mask_ref[:, at] = masks[group : group + 1]
+        return field
+
+    def project(group, field):
+        if group == groups - 1:
+            copy(field_ref, field_hbm)
+            copy(mask_ref, mask_hbm)
+        return projected(field, in_t)
+
+    def finish(group, products):
+        gated(products, masks[group : group + 1], group, share, sent_ref, gate_ref)
+        copy(sent_ref.at[:, group], sent_hbm.at[:, group])
+        if (group + 1) * lanes == early:
+            copy(gate_ref.at[:, 0:early], gate_hbm.at[:, 0:early])
+
+    staged(groups, (make_field, project, finish))
+    late = pl.ds(early, groups * lanes - early)
+    copy(gate_ref.at[:, late], gate_hbm.at[:, late])
+    for number in range(arriving, len(started)):
+        started[number].wait()
+
+
+def output_of(wide, out_t, group, lanes, line):
+    width = out_t.shape[1]
     pieces = lanes // LANES
     parts = []
     for piece in range(pieces):
         parts.append(wide[pl.ds(group * pieces + piece, width, stride=line), :])
-    summed = jnp.concatenate(parts, axis=1)
-    normed = layer_norm(summed, 0).astype(BF16)
-    output = matmul(out_t, normed, ((1,), (0,)))
-    return field + (gate * output + output)
-
-
-def middle_kernel(share, rows, cols, line, mask_same_ref, got_ref, pair_ref, bias_ref, gate_in,
-                  wo_ref, w_ref, sent_ref, gate_ref, field_ref, wide):
+    normed = layer_norm(jnp.concatenate(parts, axis=1), 0).astype(BF16)
+    return matmul(out_t, normed, ((1,), (0,)))
+
+
+def middle_kernel(share, rows, cols, line, mask_ref, got_ref, field_in, gate_in, wo_ref, w_ref,
+                  sent_ref, gate_ref, field_ref, wide):
     lanes = SUB * cols
-    width = pair_ref.shape[1]
     in_t = load_in_weights(w_ref[1], share)
     out_t = transposed(wo_ref[0], 0.5)
-    eye = identity(width, 1.0)
-    bias_col = column(bias_ref)
     wide[...] = got_ref[...].astype(F32)
-    for group in range(rows // SUB):
-        at = slice(group * lanes, (group + 1) * lanes)
-        field = first_field(pair_ref, eye, bias_col, mask_same_ref[1:2, at], group, lanes)
-        field = updated(wide, field, gate_in[:, at], out_t, group, line)
+
+    def span(group):
+        return slice(group * lanes, (group + 1) * lanes)
+
+    def outgoing(group, _):
+        return output_of(wide, out_t, group, lanes, line)
+
+    def project(group, output):
+        at = span(group)
+        field = field_in[:, at] + (gate_in[:, at] * output + output)
         field_ref[:, at] = field
-        send_inputs(field, mask_same_ref[0:1, at], in_t, group, share, sent_ref, gate_ref)
-
-
-def end_kernel(rows, cols, line, got_ref, field_in, gate_in, wo_ref, out_ref, wide):
+        return projected(field, in_t)
+
+    def finish(group, products):
+        gated(products, mask_ref[:, span(group)], group, share, sent_ref, gate_ref)
+
+    staged(rows // SUB, (outgoing, project, finish))
+
+
+def end_kernel(rows, cols, line, got_ref, field_in, gate_in, wo_ref, out_hbm, wide, out_ref, sems):
     lanes = SUB * cols
     out_t = transposed(wo_ref[1], 0.5)
     wide[...] = got_ref[...].astype(F32)
-    for group in range(rows // SUB):
+    copies = []
+
+    def outgoing(group, _):
+        return output_of(wide, out_t, group, lanes, line)
+
+    def finish(group, output):
         at = slice(group * lanes, (group + 1) * lanes)
-        field = updated(wide, field_in[:, at], gate_in[:, at], out_t, group, line)
+        field = field_in[:, at] + (gate_in[:, at] * output + output)
         out_ref[at, :] = field.T.astype(BF16)
+        at = pl.ds(group * lanes, lanes)
+        copies.append(pltpu.make_async_copy(out_ref.at[at], out_hbm.at[at], sems.at[group]))
+        copies[-1].start()
+
+    staged(rows // SUB, (outgoing, finish))
+    for copy in copies:
+        copy.wait()
 
 
 def moved(source, moves, count):
@@ -255,11 +281,15 @@
         col, row = divmod(device, row_devices)
         return row * row_step + col * groups * pieces + number
 
-    for unit in range(got_ref.shape[0] // (2 * SUB)):
-        both = got_ref[unit * 2 * SUB : (unit + 1) * 2 * SUB, :].astype(F32)
-        for half in range(2):
-            at = pl.ds(spot(2 * unit + half), SUB, stride=place_step)
-            wide[at, :] = both[half * SUB : (half + 1) * SUB]
+    def widen(pair):
+        for unit in range(got_ref.shape[0] // (2 * SUB)):
+            owners = [tile % (groups * pieces) // pieces // 2 for tile in (2 * unit, 2 * unit + 1)]
+            if min(owners) != pair:
+                continue
+            both = got_ref[unit * 2 * SUB : (unit + 1) * 2 * SUB, :].astype(F32)
+            for half in range(2):
+                at = pl.ds(spot(2 * unit + half), SUB, stride=place_step)
+                wide[at, :] = both[half * SUB : (half + 1) * SUB]
 
     def loaded(place, group, col, piece):
         if group >= groups:
@@ -267,10 +297,10 @@
         start = place * place_step + (col * groups + group) * pieces + piece
         return wide[pl.ds(start, row_devices, stride=row_step), :]
 
-    for channel in range(share):
+    def unpack(channel, only=range(pairs)):
         spare = channel % 2
-        for is_right, place in ((False, channel), (True, share + channel)):
-            for pair in range(pairs):
+        for pair in only:
+            for is_right, place in ((False, channel), (True, share + channel)):
                 tiles = {}
                 for col in range(col_devices):
                     for piece in range(pieces):
@@ -295,6 +325,9 @@
                             target[spare, start : start + 2 * SUB, block * LANES : (block + 1) * LANES] = (
                                 registers[block]
                             )
+
+    def product(channel):
+        spare = channel % 2
         if direction == 0:
             right = [even_ref[spare, block].astype(BF16) for block in range(blocks)]
             right = jnp.concatenate(right, axis=1)
@@ -307,6 +340,9 @@
             summed = matmul(left_ref[spare], right_ref[spare], ((0,), (0,)))
             for block in range(blocks):
                 result_ref[spare, block] = summed[:, block * LANES : (block + 1) * LANES]
+
+    def pack(channel):
+        spare = channel % 2
 
         def result_at(pair, step, block):
             if direction == 0:
@@ -338,6 +374,19 @@
                             packed[pl.ds(start, row_devices, stride=share * line), :] = (
                                 both[half * SUB : (half + 1) * SUB]
                             )
+
+    widen(0)
+    for pair in range(pairs):
+        if pair + 1 < pairs:
+            widen(pair + 1)
+        unpack(0, [pair])
+    for channel in range(share):
+        product(channel)
+        if channel > 0:
+            pack(channel - 1)
+        if channel + 1 < share:
+            unpack(channel + 1)
+    pack(share - 1)
     sent_ref[...] = packed[...].astype(BF16)
 
 
@@ -361,7 +410,7 @@
     sent_shape = jax.ShapeDtypeStruct((devices, groups, pieces * SUB, LANES), BF16)
     sum_shape = jax.ShapeDtypeStruct((devices * share * line, LANES), BF16)
     state_shape = jax.ShapeDtypeStruct((width, spots), F32)
-    flags_shape = jax.ShapeDtypeStruct((2, spots), F32)
+    mask_shape = jax.ShapeDtypeStruct((1, spots), F32)
 
     def exchange(array, rows):
         split = array.reshape(devices, rows, LANES)
@@ -391,22 +440,22 @@
         return exchange(summed, share * line)
 
     flat_pair = pair.reshape(spots, width)
-    flat_bias = chain_bias.reshape(1, width)
-    sent, gate, flags = pl.pallas_call(
+    sent, gate, field, mask = pl.pallas_call(
         functools.partial(start_kernel, share, rows, cols),
-        out_shape=[sent_shape, state_shape, flags_shape],
+        out_shape=[sent_shape, state_shape, state_shape, mask_shape],
         in_specs=[far] * 5,
-        out_specs=[far] * 3,
+        out_specs=[far] * 4,
         scratch_shapes=[
             pltpu.VMEM(sent_shape.shape, BF16),
             pltpu.VMEM(state_shape.shape, F32),
-            pltpu.VMEM(flags_shape.shape, F32),
+            pltpu.VMEM(state_shape.shape, F32),
+            pltpu.VMEM(mask_shape.shape, F32),
             pltpu.VMEM((spots, width), BF16),
             pltpu.VMEM(in_weights.shape[1:], BF16),
             pltpu.VMEM((1, width), F32),
             pltpu.VMEM((1,) + token_mask.shape, jnp.int32),
             pltpu.VMEM((1,) + chain_ids.shape, jnp.int32),
-            pltpu.SemaphoreType.DMA((5 + 3 * groups,)),
+            pltpu.SemaphoreType.DMA((9 + groups,)),
         ],
         compiler_params=pltpu.CompilerParams(vmem_limit_bytes=60 * 1024 * 1024),
         name="start",
@@ -415,19 +464,23 @@
     sent, gate, field = pl.pallas_call(
         functools.partial(middle_kernel, share, rows, cols, line),
         out_shape=[sent_shape, state_shape, state_shape],
-        in_specs=[whole] * 7,
+        in_specs=[whole] * 6,
         out_specs=[whole] * 3,
         scratch_shapes=[pltpu.VMEM(sum_shape.shape, F32)],
         compiler_params=params,
         name="middle",
-    )(flags, got, flat_pair, flat_bias, gate, out_weights, in_weights)
+    )(mask, got, field, gate, out_weights, in_weights)
     got = triangle(1, sent)
     out = pl.pallas_call(
         functools.partial(end_kernel, rows, cols, line),
         out_shape=jax.ShapeDtypeStruct((spots, width), BF16),
         in_specs=[whole] * 4,
-        out_specs=whole,
-        scratch_shapes=[pltpu.VMEM(sum_shape.shape, F32)],
+        out_specs=far,
+        scratch_shapes=[
+            pltpu.VMEM(sum_shape.shape, F32),
+            pltpu.VMEM((spots, width), BF16),
+            pltpu.SemaphoreType.DMA((groups,)),
+        ],
         compiler_params=params,
         name="end",
     )(got, field, gate, out_weights)

time: 159 us -> 155 us (0.975)
  Pallas kernels: 17.7 us -> 13.6 us
    pallas_call x2, Pallas kernels: 7.21 us -> 5.05 us  [triangle(): pl.pallas_call(functools.partial(triangle_kernel, direction, share, rows,...]
where the time goes in v2:
time: 155 us; the launch traced here: 154 us
  blocking collectives  141 us (91%)
  Pallas kernels  13.6 us (9%)
    all_to_all x4, blocking collectives, exchange(): lax.all_to_all(split, ('col', 'row'), 0, 0, tiled=True)  141 us
    pallas_call x2, Pallas kernels, triangle(): pl.pallas_call(functools.partial(triangle_kernel, direction, share, rows,...  5.05 us
    pallas_call x1, Pallas kernels, by_channels(): pl.pallas_call(functools.partial(start_kernel, share, rows, cols), out_sh...  4.68 us

profile of v2, /device:TPU:0, one launch (start us, length us, event | category | flops | bytes accessed | tf_op | source)
XLA Modules:
  0.0 154.4 jit_solution(10388036514423909373)
XLA Ops:
  0.0 4.7 %start.1 = (bf16[32,5,40,128]{3,2,1,0:T(8,128)(2,1)}, f32[128,3200]{1,0:T(8,128)}, f32[128,3200]{1,0:T(8,128)}, f32[1,3200]{1,0:T(1,128)}) custom-call(s32[320]{0:T(512)} %valid_hbm.1, s32[320]{0:T(512)} %chain_hbm.1, bf16[3200,128]{1,0:T(8,128)(2,1)} %bitcast.18, f32[128]{0:T(128)} %bias_hbm.1, bf16[2,128,640]{2,1,0:T(8,128)(2,1)} %w_ref.1), custom_call_target="tpu_custom_call" | custom-call | tf_op jit(solution)/shard_map/start/pallas_call | solution.py:443
  4.7 47.5 %all_to_all.20 = bf16[32,200,128]{2,1,0:T(8,128)(2,1)S(1)} all-to-all(bf16[32,200,128]{2,1,0:T(8,128)(2,1)} %bitcast.17), channel_id=1, replica_groups=mesh['row'=8,'col'=4] {'col','row'}, dimensions={0} | all-to-all | bytes 3276800 | tf_op jit(solution)/shard_map/all_to_all | solution.py:417
  52.2 0.0 copy-start
  52.2 0.0 copy-start.1
  52.2 0.0 copy-start.2
  52.2 0.0 copy-start.3
  52.2 0.0 copy-start.4
  52.3 2.3 %triangle.2 = bf16[3328,128]{1,0:T(8,128)(2,1)S(1)} custom-call(bf16[6400,128]{1,0:T(8,128)(2,1)S(1)} %bitcast.10), custom_call_target="tpu_custom_call" | custom-call | tf_op jit(solution)/shard_map/triangle/pallas_call | solution.py:422
  54.6 25.5 %all_to_all.21 = bf16[32,104,128]{2,1,0:T(8,128)(2,1)S(1)} all-to-all(bf16[32,104,128]{2,1,0:T(8,128)(2,1)S(1)} %bitcast.14), channel_id=1, replica_groups=mesh['row'=8,'col'=4] {'col','row'}, dimensions={0} | all-to-all | bytes 1703936 | tf_op jit(solution)/shard_map/all_to_all | solution.py:417
  80.0 0.0 copy-done
  80.0 0.0 copy-done.1
  80.0 0.0 copy-done.2
  80.0 0.0 copy-done.3
  80.0 0.0 copy-done.4
  80.0 2.2 %middle.1 = (bf16[32,5,40,128]{3,2,1,0:T(8,128)(2,1)S(1)}, f32[128,3200]{1,0:T(8,128)S(1)}, f32[128,3200]{1,0:T(8,128)S(1)}) custom-call(f32[1,3200]{1,0:T(1,128)S(1)} %copy-done.4, bf16[3328,128]{1,0:T(8,128)(2,1)S(1)} %bitcast.13, f32[128,3200]{1,0:T(8,128)S(1)} %copy-done.1, f32[128,3200]{1,0:T(8,128)S(1)} %copy-done, bf16[2,128,128]{2,1,0:T(8,128)(2,1)S(1)} %copy-done.3, ...), custom_call_target="tpu_custom_call" | custom-call | tf_op jit(solution)/shard_map/middle/pallas_call | solution.py:464
  82.3 42.3 %all_to_all.22 = bf16[32,200,128]{2,1,0:T(8,128)(2,1)S(1)} all-to-all(bf16[32,200,128]{2,1,0:T(8,128)(2,1)S(1)} %bitcast.16), channel_id=1, replica_groups=mesh['row'=8,'col'=4] {'col','row'}, dimensions={0} | all-to-all | bytes 3276800 | tf_op jit(solution)/shard_map/all_to_all | solution.py:417
  124.6 2.7 %triangle.3 = bf16[3328,128]{1,0:T(8,128)(2,1)S(1)} custom-call(bf16[6400,128]{1,0:T(8,128)(2,1)S(1)} %bitcast.11), custom_call_target="tpu_custom_call" | custom-call | tf_op jit(solution)/shard_map/triangle/pallas_call | solution.py:422
  127.3 25.4 %all_to_all.23 = bf16[32,104,128]{2,1,0:T(8,128)(2,1)S(1)} all-to-all(bf16[32,104,128]{2,1,0:T(8,128)(2,1)S(1)} %bitcast.15), channel_id=1, replica_groups=mesh['row'=8,'col'=4] {'col','row'}, dimensions={0} | all-to-all | bytes 1703936 | tf_op jit(solution)/shard_map/all_to_all | solution.py:417
  152.8 1.6 %end.1 = bf16[3200,128]{1,0:T(8,128)(2,1)} custom-call(bf16[3328,128]{1,0:T(8,128)(2,1)S(1)} %bitcast.12, f32[128,3200]{1,0:T(8,128)S(1)} %get-tuple-element.17.field_in, f32[128,3200]{1,0:T(8,128)S(1)} %get-tuple-element.18.gate_in, bf16[2,128,128]{2,1,0:T(8,128)(2,1)S(1)} %copy-done.3), custom_call_target="tpu_custom_call" | custom-call | tf_op jit(solution)/shard_map/end/pallas_call | solution.py:474
Async XLA Ops:
  52.2 27.8 %copy-start = (f32[128,3200]{1,0:T(8,128)S(1)}, f32[128,3200]{1,0:T(8,128)}, u32[]{:S(2)}) copy-start(f32[128,3200]{1,0:T(8,128)} %get-tuple-element.15.gate_in) | copy-start | bytes 4915204
  52.2 27.8 %copy-start.1 = (f32[128,3200]{1,0:T(8,128)S(1)}, f32[128,3200]{1,0:T(8,128)}, u32[]{:S(2)}) copy-start(f32[128,3200]{1,0:T(8,128)} %get-tuple-element.14.field_in) | copy-start | bytes 4915204
  52.2 27.8 %copy-start.2 = (bf16[2,128,640]{2,1,0:T(8,128)(2,1)S(1)}, bf16[2,128,640]{2,1,0:T(8,128)(2,1)}, u32[]{:S(2)}) copy-start(bf16[2,128,640]{2,1,0:T(8,128)(2,1)} %w_ref.1) | copy-start | bytes 983044
  52.2 27.8 %copy-start.3 = (bf16[2,128,128]{2,1,0:T(8,128)(2,1)S(1)}, bf16[2,128,128]{2,1,0:T(8,128)(2,1)}, u32[]{:S(2)}) copy-start(bf16[2,128,128]{2,1,0:T(8,128)(2,1)} %wo_ref.3) | copy-start | bytes 196612
  52.2 27.8 %copy-start.4 = (f32[1,3200]{1,0:T(1,128)S(1)}, f32[1,3200]{1,0:T(1,128)}, u32[]{:S(2)}) copy-start(f32[1,3200]{1,0:T(1,128)} %get-tuple-element.12.mask_ref) | copy-start | bytes 38404

commit v3 on v2

--- a/solution.py
+++ b/solution.py
@@ -136,6 +136,12 @@
     col_start = lax.axis_index("col") * cols
     for number in range(arriving):
         started[number].wait()
+
+    def lift(group):
+        rows_of = pair_ref[group * lanes : (group + 1) * lanes, :]
+        return matmul(eye, rows_of, ((1,), (1,)))
+
+    lifted = {0: lift(0)}
     tokens = chain_ref[...] * 2 + valid_ref[...]
     tokens = jnp.concatenate([tokens, jnp.zeros((1, -count % LANES), jnp.int32)], axis=1)
     masks, sames = token_vectors(tokens, row_start, col_start, rows, cols)
@@ -145,7 +151,9 @@
 
     def make_field(group, _):
         at = slice(group * lanes, (group + 1) * lanes)
-        field = matmul(eye, pair_ref[at, :], ((1,), (1,))) + bias_col * sames[group : group + 1]
+        if group + 1 < groups:
+            lifted[group + 1] = lift(group + 1)
+        field = lifted.pop(group) + bias_col * sames[group : group + 1]
         field_ref[:, at] = field
         mask_ref[:, at] = masks[group : group + 1]
         return field
@@ -216,7 +224,7 @@
     def finish(group, output):
         at = slice(group * lanes, (group + 1) * lanes)
         field = field_in[:, at] + (gate_in[:, at] * output + output)
-        out_ref[at, :] = field.T.astype(BF16)
+        out_ref[at, :] = field.astype(BF16).T
         at = pl.ds(group * lanes, lanes)
         copies.append(pltpu.make_async_copy(out_ref.at[at], out_hbm.at[at], sems.at[group]))
         copies[-1].start()
@@ -292,39 +300,66 @@
                 wide[at, :] = both[half * SUB : (half + 1) * SUB]
 
     def loaded(place, group, col, piece):
-        if group >= groups:
-            return jnp.zeros((SUB, LANES), F32)
         start = place * place_step + (col * groups + group) * pieces + piece
         return wide[pl.ds(start, row_devices, stride=row_step), :]
+
+    def spread(tiles, step):
+        moves = [(col, step * cols, cols, col * cols) for col in range(col_devices)]
+        registers = moved(lambda col, piece: tiles[col, piece], moves, blocks)
+        registers[-1] = jnp.where(tail, registers[-1], jnp.zeros_like(registers[-1]))
+        return registers
+
+    def put(target, spare, start, block, value):
+        target[spare, start : start + 2 * SUB, block * LANES : (block + 1) * LANES] = value
+
+    def put_even(spare, group, step, block, value):
+        even_ref[spare, block, pl.ds(group * SUB + step, row_devices, stride=rows), :] = value
 
     def unpack(channel, only=range(pairs)):
         spare = channel % 2
         for pair in only:
-            for is_right, place in ((False, channel), (True, share + channel)):
-                tiles = {}
-                for col in range(col_devices):
-                    for piece in range(pieces):
-                        tiles[col, piece] = stacked(
-                            loaded(place, 2 * pair, col, piece), loaded(place, 2 * pair + 1, col, piece)
-                        )
-                for step in range(SUB):
-                    moves = [(col, step * cols, cols, col * cols) for col in range(col_devices)]
-                    registers = moved(lambda col, piece: tiles[col, piece], moves, blocks)
-                    registers[-1] = jnp.where(tail, registers[-1], jnp.zeros_like(registers[-1]))
-                    for block in range(blocks):
-                        if is_right and direction == 0:
-                            both = registers[block].astype(F32)
-                            for half in range(2):
-                                group = 2 * pair + half
-                                if group < groups:
-                                    at = pl.ds(group * SUB + step, row_devices, stride=rows)
-                                    even_ref[spare, block, at, :] = both[half * SUB : (half + 1) * SUB]
-                        else:
-                            target = right_ref if is_right else left_ref
-                            start = (pair * SUB + step) * 2 * SUB
-                            target[spare, start : start + 2 * SUB, block * LANES : (block + 1) * LANES] = (
-                                registers[block]
-                            )
+            if 2 * pair + 1 < groups:
+                unpack_pair(channel, spare, pair)
+            else:
+                unpack_last(channel, spare, 2 * pair)
+
+    def unpack_pair(channel, spare, pair):
+        for is_right, place in ((False, channel), (True, share + channel)):
+            tiles = {}
+            for col in range(col_devices):
+                for piece in range(pieces):
+                    tiles[col, piece] = stacked(
+                        loaded(place, 2 * pair, col, piece), loaded(place, 2 * pair + 1, col, piece)
+                    )
+            for step in range(SUB):
+                for block, register in enumerate(spread(tiles, step)):
+                    if is_right and direction == 0:
+                        both = register.astype(F32)
+                        for half in range(2):
+                            put_even(spare, 2 * pair + half, step, block, both[half * SUB : (half + 1) * SUB])
+                    else:
+                        target = right_ref if is_right else left_ref
+                        put(target, spare, (pair * SUB + step) * 2 * SUB, block, register)
+
+    def unpack_last(channel, spare, group):
+        tiles = {}
+        for col in range(col_devices):
+            for piece in range(pieces):
+                tiles[col, piece] = stacked(
+                    loaded(channel, group, col, piece), loaded(share + channel, group, col, piece)
+                )
+        before = None
+        for step in range(SUB):
+            now = [register.astype(F32) for register in spread(tiles, step)]
+            for block in range(blocks):
+                if direction == 0:
+                    put_even(spare, group, step, block, now[block][SUB:])
+                if step % 2:
+                    start = (group * SUB + step - 1) * SUB
+                    put(left_ref, spare, start, block, stacked(before[block][:SUB], now[block][:SUB]))
+                    if direction == 1:
+                        put(right_ref, spare, start, block, stacked(before[block][SUB:], now[block][SUB:]))
+            before = now
 
     def product(channel):
         spare = channel % 2
@@ -345,16 +380,20 @@
         spare = channel % 2
 
         def result_at(pair, step, block):
-            if direction == 0:
-                start = (pair * SUB + step) * 2 * SUB
-                return result_ref[spare, block, start : start + 2 * SUB, :]
             halves = []
             for group in (2 * pair, 2 * pair + 1):
-                if group < groups:
+                if group >= groups:
+                    halves.append(jnp.zeros((SUB, LANES), F32))
+                elif direction == 1:
                     at = pl.ds(group * SUB + step, row_devices, stride=rows)
                     halves.append(result_ref[spare, block, at, :])
+                elif 2 * pair + 1 < groups:
+                    start = (pair * SUB + step) * 2 * SUB
+                    return result_ref[spare, block, start : start + 2 * SUB, :]
                 else:
-                    halves.append(jnp.zeros((SUB, LANES), F32))
+                    start = (group * SUB + step // 2 * 2) * SUB
+                    both = result_ref[spare, block, start : start + 2 * SUB, :].astype(F32)
+                    halves.append(both[step % 2 * SUB : (step % 2 + 1) * SUB])
             return stacked(*halves)
 
         for pair in range(pairs):
@@ -402,7 +441,7 @@
     line = -(-groups * pieces * share // SUB) * SUB // share
     total = row_devices * rows
     blocks = -(-total // LANES)
-    tall = -(-groups // 2) * 2 * SUB * row_devices
+    tall = groups * SUB * row_devices
     params = pltpu.CompilerParams(vmem_limit_bytes=40 * 1024 * 1024)
     whole = pl.BlockSpec(memory_space=pltpu.VMEM)
     far = pl.BlockSpec(memory_space=pltpu.HBM)

time: 155 us -> 155 us (level)
  no operation moved by 1% of the time
where the time goes in v3:
time: 155 us
  blocking collectives  141 us (91%)
  Pallas kernels  13.7 us (9%)
    all_to_all x4, blocking collectives, exchange(): lax.all_to_all(split, ('col', 'row'), 0, 0, tiled=True)  141 us
    pallas_call x2, Pallas kernels, triangle(): pl.pallas_call(functools.partial(triangle_kernel, direction, share, rows,...  5.12 us
    pallas_call x1, Pallas kernels, by_channels(): pl.pallas_call(functools.partial(start_kernel, share, rows, cols), out_sh...  4.68 us

profile of v3, /device:TPU:0, one launch (start us, length us, event | category | flops | bytes accessed | tf_op | source)
XLA Modules:
  0.0 154.5 jit_solution(15991504502384143933)
XLA Ops:
  0.0 4.7 %start.1 = (bf16[32,5,40,128]{3,2,1,0:T(8,128)(2,1)}, f32[128,3200]{1,0:T(8,128)}, f32[128,3200]{1,0:T(8,128)}, f32[1,3200]{1,0:T(1,128)}) custom-call(s32[320]{0:T(512)} %valid_hbm.1, s32[320]{0:T(512)} %chain_hbm.1, bf16[3200,128]{1,0:T(8,128)(2,1)} %bitcast.18, f32[128]{0:T(128)} %bias_hbm.1, bf16[2,128,640]{2,1,0:T(8,128)(2,1)} %w_ref.1), custom_call_target="tpu_custom_call" | custom-call | tf_op jit(solution)/shard_map/start/pallas_call | solution.py:482
  4.7 47.5 %all_to_all.20 = bf16[32,200,128]{2,1,0:T(8,128)(2,1)S(1)} all-to-all(bf16[32,200,128]{2,1,0:T(8,128)(2,1)} %bitcast.17), channel_id=1, replica_groups=mesh['row'=8,'col'=4] {'col','row'}, dimensions={0} | all-to-all | bytes 3276800 | tf_op jit(solution)/shard_map/all_to_all | solution.py:456
  52.2 0.0 copy-start
  52.2 0.0 copy-start.1
  52.2 0.0 copy-start.2
  52.2 0.0 copy-start.3
  52.2 0.0 copy-start.4
  52.3 2.2 %triangle.2 = bf16[3328,128]{1,0:T(8,128)(2,1)S(1)} custom-call(bf16[6400,128]{1,0:T(8,128)(2,1)S(1)} %bitcast.10), custom_call_target="tpu_custom_call" | custom-call | tf_op jit(solution)/shard_map/triangle/pallas_call | solution.py:461
  54.5 25.5 %all_to_all.21 = bf16[32,104,128]{2,1,0:T(8,128)(2,1)S(1)} all-to-all(bf16[32,104,128]{2,1,0:T(8,128)(2,1)S(1)} %bitcast.14), channel_id=1, replica_groups=mesh['row'=8,'col'=4] {'col','row'}, dimensions={0} | all-to-all | bytes 1703936 | tf_op jit(solution)/shard_map/all_to_all | solution.py:456
  79.9 0.0 copy-done
  79.9 0.0 copy-done.1
  79.9 0.0 copy-done.2
  79.9 0.0 copy-done.3
  80.0 0.0 copy-done.4
  80.0 2.2 %middle.1 = (bf16[32,5,40,128]{3,2,1,0:T(8,128)(2,1)S(1)}, f32[128,3200]{1,0:T(8,128)S(1)}, f32[128,3200]{1,0:T(8,128)S(1)}) custom-call(f32[1,3200]{1,0:T(1,128)S(1)} %copy-done.4, bf16[3328,128]{1,0:T(8,128)(2,1)S(1)} %bitcast.13, f32[128,3200]{1,0:T(8,128)S(1)} %copy-done.1, f32[128,3200]{1,0:T(8,128)S(1)} %copy-done, bf16[2,128,128]{2,1,0:T(8,128)(2,1)S(1)} %copy-done.3, ...), custom_call_target="tpu_custom_call" | custom-call | tf_op jit(solution)/shard_map/middle/pallas_call | solution.py:503
  82.2 42.3 %all_to_all.22 = bf16[32,200,128]{2,1,0:T(8,128)(2,1)S(1)} all-to-all(bf16[32,200,128]{2,1,0:T(8,128)(2,1)S(1)} %bitcast.16), channel_id=1, replica_groups=mesh['row'=8,'col'=4] {'col','row'}, dimensions={0} | all-to-all | bytes 3276800 | tf_op jit(solution)/shard_map/all_to_all | solution.py:456
  124.5 2.9 %triangle.3 = bf16[3328,128]{1,0:T(8,128)(2,1)S(1)} custom-call(bf16[6400,128]{1,0:T(8,128)(2,1)S(1)} %bitcast.11), custom_call_target="tpu_custom_call" | custom-call | tf_op jit(solution)/shard_map/triangle/pallas_call | solution.py:461
  127.4 25.4 %all_to_all.23 = bf16[32,104,128]{2,1,0:T(8,128)(2,1)S(1)} all-to-all(bf16[32,104,128]{2,1,0:T(8,128)(2,1)S(1)} %bitcast.15), channel_id=1, replica_groups=mesh['row'=8,'col'=4] {'col','row'}, dimensions={0} | all-to-all | bytes 1703936 | tf_op jit(solution)/shard_map/all_to_all | solution.py:456
  152.9 1.6 %end.1 = bf16[3200,128]{1,0:T(8,128)(2,1)} custom-call(bf16[3328,128]{1,0:T(8,128)(2,1)S(1)} %bitcast.12, f32[128,3200]{1,0:T(8,128)S(1)} %get-tuple-element.17.field_in, f32[128,3200]{1,0:T(8,128)S(1)} %get-tuple-element.18.gate_in, bf16[2,128,128]{2,1,0:T(8,128)(2,1)S(1)} %copy-done.3), custom_call_target="tpu_custom_call" | custom-call | tf_op jit(solution)/shard_map/end/pallas_call | solution.py:513
Async XLA Ops:
  52.2 27.7 %copy-start = (f32[128,3200]{1,0:T(8,128)S(1)}, f32[128,3200]{1,0:T(8,128)}, u32[]{:S(2)}) copy-start(f32[128,3200]{1,0:T(8,128)} %get-tuple-element.15.gate_in) | copy-start | bytes 4915204
  52.2 27.7 %copy-start.1 = (f32[128,3200]{1,0:T(8,128)S(1)}, f32[128,3200]{1,0:T(8,128)}, u32[]{:S(2)}) copy-start(f32[128,3200]{1,0:T(8,128)} %get-tuple-element.14.field_in) | copy-start | bytes 4915204
  52.2 27.7 %copy-start.2 = (bf16[2,128,640]{2,1,0:T(8,128)(2,1)S(1)}, bf16[2,128,640]{2,1,0:T(8,128)(2,1)}, u32[]{:S(2)}) copy-start(bf16[2,128,640]{2,1,0:T(8,128)(2,1)} %w_ref.1) | copy-start | bytes 983044
  52.2 27.7 %copy-start.3 = (bf16[2,128,128]{2,1,0:T(8,128)(2,1)S(1)}, bf16[2,128,128]{2,1,0:T(8,128)(2,1)}, u32[]{:S(2)}) copy-start(bf16[2,128,128]{2,1,0:T(8,128)(2,1)} %wo_ref.3) | copy-start | bytes 196612
  52.2 27.7 %copy-start.4 = (f32[1,3200]{1,0:T(1,128)S(1)}, f32[1,3200]{1,0:T(1,128)}, u32[]{:S(2)}) copy-start(f32[1,3200]{1,0:T(1,128)} %get-tuple-element.12.mask_ref) | copy-start | bytes 38404

commit v4 on v3

--- a/solution.py
+++ b/solution.py
@@ -125,16 +125,18 @@
         started.append(pltpu.make_async_copy(near, far, sems.at[len(started)]))
         started[-1].start()
 
+    copy(w_hbm.at[0], w_ref)
     copy(valid_hbm, valid_ref.at[0])
     copy(chain_hbm, chain_ref.at[0])
-    copy(w_hbm.at[0], w_ref)
     copy(bias_hbm, bias_ref.at[0])
     copy(pair_hbm, pair_ref)
     arriving = len(started)
     eye = identity(width, 1.0)
     row_start = lax.axis_index("row") * rows
     col_start = lax.axis_index("col") * cols
-    for number in range(arriving):
+    started[0].wait()
+    in_t = load_in_weights(w_ref[...], share)
+    for number in range(1, arriving):
         started[number].wait()
 
     def lift(group):
@@ -145,9 +147,7 @@
     tokens = chain_ref[...] * 2 + valid_ref[...]
     tokens = jnp.concatenate([tokens, jnp.zeros((1, -count % LANES), jnp.int32)], axis=1)
     masks, sames = token_vectors(tokens, row_start, col_start, rows, cols)
-    in_t = load_in_weights(w_ref[...], share)
     bias_col = column(bias_ref)
-    early = groups // 2 * lanes
 
     def make_field(group, _):
         at = slice(group * lanes, (group + 1) * lanes)
@@ -167,12 +167,10 @@
     def finish(group, products):
         gated(products, masks[group : group + 1], group, share, sent_ref, gate_ref)
         copy(sent_ref.at[:, group], sent_hbm.at[:, group])
-        if (group + 1) * lanes == early:
-            copy(gate_ref.at[:, 0:early], gate_hbm.at[:, 0:early])
+        at = pl.ds(group * lanes, lanes)
+        copy(gate_ref.at[:, at], gate_hbm.at[:, at])
 
     staged(groups, (make_field, project, finish))
-    late = pl.ds(early, groups * lanes - early)
-    copy(gate_ref.at[:, late], gate_hbm.at[:, late])
     for number in range(arriving, len(started)):
         started[number].wait()
 
@@ -269,6 +267,17 @@
     return place_step, SUB * place_step + 1
 
 
+def row_order(groups, row_devices, rows, width):
+    line = lax.broadcasted_iota(jnp.int32, (groups * SUB * row_devices, 1), 0)
+    row, rest = line % row_devices, line // row_devices
+    paired = groups // 2 * 2
+    pair, inside = rest // (2 * SUB), rest % (2 * SUB)
+    of_pair = (2 * pair + inside % 2) * SUB + inside // 2
+    place = jnp.where(rest < paired * SUB, of_pair, rest)
+    lane = lax.broadcasted_iota(jnp.int32, (groups * SUB * row_devices, width), 1)
+    return jnp.where(lane == row * rows + place, 1.0, 0.0).astype(BF16)
+
+
 def stacked(low, high):
     return jnp.concatenate([low, high], axis=0).astype(BF16)
 
@@ -283,6 +292,7 @@
     rest = total - (blocks - 1) * LANES
     tail = lax.broadcasted_iota(jnp.int32, (2 * SUB, LANES), 1) < rest
     place_step, row_step = wide_steps(col_devices * groups * pieces)
+    pick = row_order(groups, row_devices, rows, blocks * LANES) if direction == 1 else None
 
     def spot(tile):
         device, number = divmod(tile, groups * pieces)
@@ -367,14 +377,13 @@
             right = [even_ref[spare, block].astype(BF16) for block in range(blocks)]
             right = jnp.concatenate(right, axis=1)
             summed = matmul(left_ref[spare], right, ((1,), (1,)))
-            for block in range(blocks):
-                size = min(LANES, total - block * LANES)
-                part = summed[:, block * LANES : block * LANES + size].astype(BF16)
-                result_ref[spare, block, :, 0:size] = part
         else:
-            summed = matmul(left_ref[spare], right_ref[spare], ((0,), (0,)))
-            for block in range(blocks):
-                result_ref[spare, block] = summed[:, block * LANES : (block + 1) * LANES]
+            turned = matmul(pick, left_ref[spare], ((1,), (1,))).astype(BF16)
+            summed = matmul(turned, right_ref[spare], ((1,), (0,)))
+        for block in range(blocks):
+            size = min(LANES, total - block * LANES)
+            part = summed[:, block * LANES : block * LANES + size].astype(BF16)
+            result_ref[spare, block, :, 0:size] = part
 
     def pack(channel):
         spare = channel % 2
@@ -384,9 +393,6 @@
             for group in (2 * pair, 2 * pair + 1):
                 if group >= groups:
                     halves.append(jnp.zeros((SUB, LANES), F32))
-                elif direction == 1:
-                    at = pl.ds(group * SUB + step, row_devices, stride=rows)
-                    halves.append(result_ref[spare, block, at, :])
                 elif 2 * pair + 1 < groups:
                     start = (pair * SUB + step) * 2 * SUB
                     return result_ref[spare, block, start : start + 2 * SUB, :]
@@ -438,7 +444,7 @@
     groups = rows // SUB
     chunk = groups * pieces * SUB
     spots = rows * cols
-    line = -(-groups * pieces * share // SUB) * SUB // share
+    line = groups * pieces
     total = row_devices * rows
     blocks = -(-total // LANES)
     tall = groups * SUB * row_devices
@@ -452,11 +458,11 @@
     mask_shape = jax.ShapeDtypeStruct((1, spots), F32)
 
     def exchange(array, rows):
-        split = array.reshape(devices, rows, LANES)
+        shape = (devices, rows) if rows % SUB == 0 else (devices, rows * 2 // SUB, SUB // 2)
+        split = array.reshape(*shape, LANES)
         return lax.all_to_all(split, ("col", "row"), 0, 0, tiled=True).reshape(devices * rows, LANES)
 
     def triangle(direction, sent):
-        result_rows, result_type = (tall, BF16) if direction == 0 else (blocks * LANES, F32)
         wide_rows = row_devices * wide_steps(col_devices * groups * pieces)[1]
         summed = pl.pallas_call(
             functools.partial(
@@ -470,7 +476,7 @@
                 pltpu.VMEM((2, tall, blocks * LANES), BF16),
                 pltpu.VMEM((2, tall, blocks * LANES), BF16),
                 pltpu.VMEM((2, blocks, total, LANES), F32),
-                pltpu.VMEM((2, blocks, result_rows, LANES), result_type),
+                pltpu.VMEM((2, blocks, tall, LANES), BF16),
                 pltpu.VMEM(sum_shape.shape, F32),
             ],
             compiler_params=params,
@@ -494,7 +500,7 @@
             pltpu.VMEM((1, width), F32),
             pltpu.VMEM((1,) + token_mask.shape, jnp.int32),
             pltpu.VMEM((1,) + chain_ids.shape, jnp.int32),
-            pltpu.SemaphoreType.DMA((9 + groups,)),
+            pltpu.SemaphoreType.DMA((7 + 2 * groups,)),
         ],
         compiler_params=pltpu.CompilerParams(vmem_limit_bytes=60 * 1024 * 1024),
         name="start",

time: 155 us -> 153 us (0.987)
  blocking collectives: 141 us -> 139 us
where the time goes in v4:
time: 153 us; the launch traced here: 152 us
  blocking collectives  139 us (91%)
  Pallas kernels  13.1 us (9%)
    all_to_all x4, blocking collectives, exchange(): lax.all_to_all(split, ('col', 'row'), 0, 0, tiled=True)  139 us
    pallas_call x1, Pallas kernels, by_channels(): pl.pallas_call(functools.partial(start_kernel, share, rows, cols), out_sh...  4.65 us
    pallas_call x2, Pallas kernels, triangle(): pl.pallas_call(functools.partial(triangle_kernel, direction, share, rows,...  4.54 us

profile of v4, /device:TPU:0, one launch (start us, length us, event | category | flops | bytes accessed | tf_op | source)
XLA Modules:
  0.0 152.5 jit_solution(11379338567838942055)
XLA Ops:
  0.0 4.7 %start.1 = (bf16[32,5,40,128]{3,2,1,0:T(8,128)(2,1)}, f32[128,3200]{1,0:T(8,128)}, f32[128,3200]{1,0:T(8,128)}, f32[1,3200]{1,0:T(1,128)}) custom-call(s32[320]{0:T(512)} %valid_hbm.1, s32[320]{0:T(512)} %chain_hbm.1, bf16[3200,128]{1,0:T(8,128)(2,1)} %bitcast.18, f32[128]{0:T(128)} %bias_hbm.1, bf16[2,128,640]{2,1,0:T(8,128)(2,1)} %w_ref.1), custom_call_target="tpu_custom_call" | custom-call | tf_op jit(solution)/shard_map/start/pallas_call | solution.py:488
  4.7 47.5 %all_to_all.20 = bf16[32,200,128]{2,1,0:T(8,128)(2,1)S(1)} all-to-all(bf16[32,200,128]{2,1,0:T(8,128)(2,1)} %bitcast.17), channel_id=1, replica_groups=mesh['row'=8,'col'=4] {'col','row'}, dimensions={0} | all-to-all | bytes 3276800 | tf_op jit(solution)/shard_map/all_to_all | solution.py:463
  52.2 0.0 copy-start
  52.2 0.0 copy-start.1
  52.2 0.0 copy-start.2
  52.2 0.0 copy-start.3
  52.2 0.0 copy-start.4
  52.2 2.2 %triangle.2 = bf16[3200,128]{1,0:T(8,128)(2,1)S(1)} custom-call(bf16[6400,128]{1,0:T(8,128)(2,1)S(1)} %bitcast.10), custom_call_target="tpu_custom_call" | custom-call | tf_op jit(solution)/shard_map/triangle/pallas_call | solution.py:467
  54.5 24.7 %all_to_all.21 = bf16[32,25,4,128]{3,2,1,0:T(4,128)(2,1)S(1)} all-to-all(bf16[32,25,4,128]{3,2,1,0:T(4,128)(2,1)S(1)} %bitcast.13), channel_id=1, replica_groups=mesh['row'=8,'col'=4] {'col','row'}, dimensions={0} | all-to-all | bytes 1638400 | tf_op jit(solution)/shard_map/all_to_all | solution.py:463
  79.2 0.0 copy-done
  79.2 0.0 copy-done.1
  79.2 0.0 copy-done.2
  79.2 0.0 copy-done.3
  79.2 0.0 copy-done.4
  79.2 2.2 %middle.1 = (bf16[32,5,40,128]{3,2,1,0:T(8,128)(2,1)S(1)}, f32[128,3200]{1,0:T(8,128)S(1)}, f32[128,3200]{1,0:T(8,128)S(1)}) custom-call(f32[1,3200]{1,0:T(1,128)S(1)} %copy-done.4, bf16[3200,128]{1,0:T(8,128)(2,1)S(1)} %bitcast.15, f32[128,3200]{1,0:T(8,128)S(1)} %copy-done.1, f32[128,3200]{1,0:T(8,128)S(1)} %copy-done, bf16[2,128,128]{2,1,0:T(8,128)(2,1)S(1)} %copy-done.3, ...), custom_call_target="tpu_custom_call" | custom-call | tf_op jit(solution)/shard_map/middle/pallas_call | solution.py:509
  81.5 42.3 %all_to_all.22 = bf16[32,200,128]{2,1,0:T(8,128)(2,1)S(1)} all-to-all(bf16[32,200,128]{2,1,0:T(8,128)(2,1)S(1)} %bitcast.16), channel_id=1, replica_groups=mesh['row'=8,'col'=4] {'col','row'}, dimensions={0} | all-to-all | bytes 3276800 | tf_op jit(solution)/shard_map/all_to_all | solution.py:463
  123.8 2.3 %triangle.3 = bf16[3200,128]{1,0:T(8,128)(2,1)S(1)} custom-call(bf16[6400,128]{1,0:T(8,128)(2,1)S(1)} %bitcast.11), custom_call_target="tpu_custom_call" | custom-call | tf_op jit(solution)/shard_map/triangle/pallas_call | solution.py:467
  126.1 24.8 %all_to_all.23 = bf16[32,25,4,128]{3,2,1,0:T(4,128)(2,1)S(1)} all-to-all(bf16[32,25,4,128]{3,2,1,0:T(4,128)(2,1)S(1)} %bitcast.14), channel_id=1, replica_groups=mesh['row'=8,'col'=4] {'col','row'}, dimensions={0} | all-to-all | bytes 1638400 | tf_op jit(solution)/shard_map/all_to_all | solution.py:463
  150.9 1.6 %end.1 = bf16[3200,128]{1,0:T(8,128)(2,1)} custom-call(bf16[3200,128]{1,0:T(8,128)(2,1)S(1)} %bitcast.12, f32[128,3200]{1,0:T(8,128)S(1)} %get-tuple-element.17.field_in, f32[128,3200]{1,0:T(8,128)S(1)} %get-tuple-element.18.gate_in, bf16[2,128,128]{2,1,0:T(8,128)(2,1)S(1)} %copy-done.3), custom_call_target="tpu_custom_call" | custom-call | tf_op jit(solution)/shard_map/end/pallas_call | solution.py:519
Async XLA Ops:
  52.2 27.0 %copy-start = (f32[128,3200]{1,0:T(8,128)S(1)}, f32[128,3200]{1,0:T(8,128)}, u32[]{:S(2)}) copy-start(f32[128,3200]{1,0:T(8,128)} %get-tuple-element.15.gate_in) | copy-start | bytes 4915204
  52.2 27.0 %copy-start.1 = (f32[128,3200]{1,0:T(8,128)S(1)}, f32[128,3200]{1,0:T(8,128)}, u32[]{:S(2)}) copy-start(f32[128,3200]{1,0:T(8,128)} %get-tuple-element.14.field_in) | copy-start | bytes 4915204
  52.2 27.0 %copy-start.2 = (bf16[2,128,640]{2,1,0:T(8,128)(2,1)S(1)}, bf16[2,128,640]{2,1,0:T(8,128)(2,1)}, u32[]{:S(2)}) copy-start(bf16[2,128,640]{2,1,0:T(8,128)(2,1)} %w_ref.1) | copy-start | bytes 983044
  52.2 27.0 %copy-start.3 = (bf16[2,128,128]{2,1,0:T(8,128)(2,1)S(1)}, bf16[2,128,128]{2,1,0:T(8,128)(2,1)}, u32[]{:S(2)}) copy-start(bf16[2,128,128]{2,1,0:T(8,128)(2,1)} %wo_ref.3) | copy-start | bytes 196612
  52.2 27.0 %copy-start.4 = (f32[1,3200]{1,0:T(1,128)S(1)}, f32[1,3200]{1,0:T(1,128)}, u32[]{:S(2)}) copy-start(f32[1,3200]{1,0:T(1,128)} %get-tuple-element.12.mask_ref) | copy-start | bytes 38404

commit v5 on v4

--- a/solution.py
+++ b/solution.py
@@ -129,17 +129,20 @@
     copy(valid_hbm, valid_ref.at[0])
     copy(chain_hbm, chain_ref.at[0])
     copy(bias_hbm, bias_ref.at[0])
-    copy(pair_hbm, pair_ref)
+    for at in (pl.ds(0, 2 * lanes), pl.ds(2 * lanes, (groups - 2) * lanes)):
+        copy(pair_hbm.at[at], pair_ref.at[at])
     arriving = len(started)
     eye = identity(width, 1.0)
     row_start = lax.axis_index("row") * rows
     col_start = lax.axis_index("col") * cols
     started[0].wait()
     in_t = load_in_weights(w_ref[...], share)
-    for number in range(1, arriving):
+    for number in range(1, arriving - 1):
         started[number].wait()
 
     def lift(group):
+        if group == 2:
+            started[arriving - 1].wait()
         rows_of = pair_ref[group * lanes : (group + 1) * lanes, :]
         return matmul(eye, rows_of, ((1,), (1,)))
 
@@ -188,9 +191,11 @@
 def middle_kernel(share, rows, cols, line, mask_ref, got_ref, field_in, gate_in, wo_ref, w_ref,
                   sent_ref, gate_ref, field_ref, wide):
     lanes = SUB * cols
+    half = got_ref.shape[0] // 2
+    wide[:half, :] = got_ref[:half, :].astype(F32)
+    out_t = transposed(wo_ref[0], 0.5)
+    wide[half:, :] = got_ref[half:, :].astype(F32)
     in_t = load_in_weights(w_ref[1], share)
-    out_t = transposed(wo_ref[0], 0.5)
-    wide[...] = got_ref[...].astype(F32)
 
     def span(group):
         return slice(group * lanes, (group + 1) * lanes)
@@ -313,10 +318,11 @@
         start = place * place_step + (col * groups + group) * pieces + piece
         return wide[pl.ds(start, row_devices, stride=row_step), :]
 
-    def spread(tiles, step):
+    def spread(tiles, step, cleared):
         moves = [(col, step * cols, cols, col * cols) for col in range(col_devices)]
         registers = moved(lambda col, piece: tiles[col, piece], moves, blocks)
-        registers[-1] = jnp.where(tail, registers[-1], jnp.zeros_like(registers[-1]))
+        if cleared:
+            registers[-1] = jnp.where(tail, registers[-1], jnp.zeros_like(registers[-1]))
         return registers
 
     def put(target, spare, start, block, value):
@@ -342,7 +348,7 @@
                         loaded(place, 2 * pair, col, piece), loaded(place, 2 * pair + 1, col, piece)
                     )
             for step in range(SUB):
-                for block, register in enumerate(spread(tiles, step)):
+                for block, register in enumerate(spread(tiles, step, direction == 0 and not is_right)):
                     if is_right and direction == 0:
                         both = register.astype(F32)
                         for half in range(2):
@@ -360,7 +366,7 @@
                 )
         before = None
         for step in range(SUB):
-            now = [register.astype(F32) for register in spread(tiles, step)]
+            now = [register.astype(F32) for register in spread(tiles, step, direction == 0)]
             for block in range(blocks):
                 if direction == 0:
                     put_even(spare, group, step, block, now[block][SUB:])
@@ -383,42 +389,41 @@
         for block in range(blocks):
             size = min(LANES, total - block * LANES)
             part = summed[:, block * LANES : block * LANES + size].astype(BF16)
-            result_ref[spare, block, :, 0:size] = part
+            result_ref[channel, block, :, 0:size] = part
+
+    def send(tiles, targets):
+        for col in range(col_devices):
+            moves = [(step, col * cols, cols, step * cols) for step in range(SUB)]
+            registers = moved(lambda step, block: tiles[step, block], moves, pieces)
+            for piece in range(pieces):
+                both = registers[piece].astype(F32)
+                for half, (channel, group) in enumerate(targets):
+                    start = (col * row_devices * share + channel) * line + group * pieces + piece
+                    packed[pl.ds(start, row_devices, stride=share * line), :] = (
+                        both[half * SUB : (half + 1) * SUB]
+                    )
 
     def pack(channel):
-        spare = channel % 2
-
-        def result_at(pair, step, block):
-            halves = []
-            for group in (2 * pair, 2 * pair + 1):
-                if group >= groups:
-                    halves.append(jnp.zeros((SUB, LANES), F32))
-                elif 2 * pair + 1 < groups:
-                    start = (pair * SUB + step) * 2 * SUB
-                    return result_ref[spare, block, start : start + 2 * SUB, :]
-                else:
-                    start = (group * SUB + step // 2 * 2) * SUB
-                    both = result_ref[spare, block, start : start + 2 * SUB, :].astype(F32)
-                    halves.append(both[step % 2 * SUB : (step % 2 + 1) * SUB])
-            return stacked(*halves)
-
-        for pair in range(pairs):
+        for pair in range(groups // 2):
             tiles = {}
             for step in range(SUB):
                 for block in range(blocks):
-                    tiles[step, block] = result_at(pair, step, block)
-            for col in range(col_devices):
-                moves = [(step, col * cols, cols, step * cols) for step in range(SUB)]
-                registers = moved(lambda step, block: tiles[step, block], moves, pieces)
-                for piece in range(pieces):
-                    both = registers[piece].astype(F32)
-                    for half in range(2):
-                        group = 2 * pair + half
-                        if group < groups:
-                            start = (col * row_devices * share + channel) * line + group * pieces + piece
-                            packed[pl.ds(start, row_devices, stride=share * line), :] = (
-                                both[half * SUB : (half + 1) * SUB]
-                            )
+                    start = (pair * SUB + step) * 2 * SUB
+                    tiles[step, block] = result_ref[channel, block, start : start + 2 * SUB, :]
+            send(tiles, [(channel, 2 * pair), (channel, 2 * pair + 1)])
+        if groups % 2 and channel % 2:
+            group = groups - 1
+            tiles = {}
+            for block in range(blocks):
+                for step in range(0, SUB, 2):
+                    start = (group * SUB + step) * SUB
+                    low, high = [
+                        result_ref[one, block, start : start + 2 * SUB, :].astype(F32)
+                        for one in (channel - 1, channel)
+                    ]
+                    tiles[step, block] = stacked(low[:SUB], high[:SUB])
+                    tiles[step + 1, block] = stacked(low[SUB:], high[SUB:])
+            send(tiles, [(channel - 1, group), (channel, group)])
 
     widen(0)
     for pair in range(pairs):
@@ -476,7 +481,7 @@
                 pltpu.VMEM((2, tall, blocks * LANES), BF16),
                 pltpu.VMEM((2, tall, blocks * LANES), BF16),
                 pltpu.VMEM((2, blocks, total, LANES), F32),
-                pltpu.VMEM((2, blocks, tall, LANES), BF16),
+                pltpu.VMEM((share, blocks, tall, LANES), BF16),
                 pltpu.VMEM(sum_shape.shape, F32),
             ],
             compiler_params=params,
@@ -500,7 +505,7 @@
             pltpu.VMEM((1, width), F32),
             pltpu.VMEM((1,) + token_mask.shape, jnp.int32),
             pltpu.VMEM((1,) + chain_ids.shape, jnp.int32),
-            pltpu.SemaphoreType.DMA((7 + 2 * groups,)),
+            pltpu.SemaphoreType.DMA((8 + 2 * groups,)),
         ],
         compiler_params=pltpu.CompilerParams(vmem_limit_bytes=60 * 1024 * 1024),
         name="start",
@@ -593,6 +598,7 @@
             and 2 * (width // devices) == SUB
             and row_devices == SUB
             and rows % SUB == 0
+            and rows >= 3 * SUB
             and (SUB * cols) % LANES == 0
             and max(rows, cols) <= LANES
         )

time: 153 us -> 153 us (level)
  no operation moved by 1% of the time
where the time goes in v5:
time: 153 us; the launch traced here: 152 us
  blocking collectives  139 us (91%)
  Pallas kernels  12.8 us (8%)
    all_to_all x4, blocking collectives, exchange(): lax.all_to_all(split, ('col', 'row'), 0, 0, tiled=True)  139 us
    pallas_call x1, Pallas kernels, by_channels(): pl.pallas_call(functools.partial(start_kernel, share, rows, cols), out_sh...  4.55 us
    pallas_call x2, Pallas kernels, triangle(): pl.pallas_call(functools.partial(triangle_kernel, direction, share, rows,...  4.45 us

profile of v5, /device:TPU:0, one launch (start us, length us, event | category | flops | bytes accessed | tf_op | source)
XLA Modules:
  0.0 152.3 jit_solution(15709677837988886082)
XLA Ops:
  0.0 4.5 %start.1 = (bf16[32,5,40,128]{3,2,1,0:T(8,128)(2,1)}, f32[128,3200]{1,0:T(8,128)}, f32[128,3200]{1,0:T(8,128)}, f32[1,3200]{1,0:T(1,128)}) custom-call(s32[320]{0:T(512)} %valid_hbm.1, s32[320]{0:T(512)} %chain_hbm.1, bf16[3200,128]{1,0:T(8,128)(2,1)} %bitcast.18, f32[128]{0:T(128)} %bias_hbm.1, bf16[2,128,640]{2,1,0:T(8,128)(2,1)} %w_ref.1), custom_call_target="tpu_custom_call" | custom-call | tf_op jit(solution)/shard_map/start/pallas_call | solution.py:493
  4.6 47.5 %all_to_all.20 = bf16[32,200,128]{2,1,0:T(8,128)(2,1)S(1)} all-to-all(bf16[32,200,128]{2,1,0:T(8,128)(2,1)} %bitcast.17), channel_id=1, replica_groups=mesh['row'=8,'col'=4] {'col','row'}, dimensions={0} | all-to-all | bytes 3276800 | tf_op jit(solution)/shard_map/all_to_all | solution.py:468
  52.1 0.0 copy-start
  52.1 0.0 copy-start.1
  52.1 0.0 copy-start.2
  52.1 0.0 copy-start.3
  52.1 0.0 copy-start.4
  52.1 2.2 %triangle.2 = bf16[3200,128]{1,0:T(8,128)(2,1)S(1)} custom-call(bf16[6400,128]{1,0:T(8,128)(2,1)S(1)} %bitcast.10), custom_call_target="tpu_custom_call" | custom-call | tf_op jit(solution)/shard_map/triangle/pallas_call | solution.py:472
  54.3 24.8 %all_to_all.21 = bf16[32,25,4,128]{3,2,1,0:T(4,128)(2,1)S(1)} all-to-all(bf16[32,25,4,128]{3,2,1,0:T(4,128)(2,1)S(1)} %bitcast.13), channel_id=1, replica_groups=mesh['row'=8,'col'=4] {'col','row'}, dimensions={0} | all-to-all | bytes 1638400 | tf_op jit(solution)/shard_map/all_to_all | solution.py:468
  79.0 0.0 copy-done
  79.0 0.0 copy-done.1
  79.1 0.0 copy-done.2
  79.1 0.0 copy-done.3
  79.1 0.0 copy-done.4
  79.1 2.2 %middle.1 = (bf16[32,5,40,128]{3,2,1,0:T(8,128)(2,1)S(1)}, f32[128,3200]{1,0:T(8,128)S(1)}, f32[128,3200]{1,0:T(8,128)S(1)}) custom-call(f32[1,3200]{1,0:T(1,128)S(1)} %copy-done.4, bf16[3200,128]{1,0:T(8,128)(2,1)S(1)} %bitcast.15, f32[128,3200]{1,0:T(8,128)S(1)} %copy-done.1, f32[128,3200]{1,0:T(8,128)S(1)} %copy-done, bf16[2,128,128]{2,1,0:T(8,128)(2,1)S(1)} %copy-done.3, ...), custom_call_target="tpu_custom_call" | custom-call | tf_op jit(solution)/shard_map/middle/pallas_call | solution.py:514
  81.3 42.3 %all_to_all.22 = bf16[32,200,128]{2,1,0:T(8,128)(2,1)S(1)} all-to-all(bf16[32,200,128]{2,1,0:T(8,128)(2,1)S(1)} %bitcast.16), channel_id=1, replica_groups=mesh['row'=8,'col'=4] {'col','row'}, dimensions={0} | all-to-all | bytes 3276800 | tf_op jit(solution)/shard_map/all_to_all | solution.py:468
  123.6 2.3 %triangle.3 = bf16[3200,128]{1,0:T(8,128)(2,1)S(1)} custom-call(bf16[6400,128]{1,0:T(8,128)(2,1)S(1)} %bitcast.11), custom_call_target="tpu_custom_call" | custom-call | tf_op jit(solution)/shard_map/triangle/pallas_call | solution.py:472
  125.9 24.7 %all_to_all.23 = bf16[32,25,4,128]{3,2,1,0:T(4,128)(2,1)S(1)} all-to-all(bf16[32,25,4,128]{3,2,1,0:T(4,128)(2,1)S(1)} %bitcast.14), channel_id=1, replica_groups=mesh['row'=8,'col'=4] {'col','row'}, dimensions={0} | all-to-all | bytes 1638400 | tf_op jit(solution)/shard_map/all_to_all | solution.py:468
  150.6 1.6 %end.1 = bf16[3200,128]{1,0:T(8,128)(2,1)} custom-call(bf16[3200,128]{1,0:T(8,128)(2,1)S(1)} %bitcast.12, f32[128,3200]{1,0:T(8,128)S(1)} %get-tuple-element.17.field_in, f32[128,3200]{1,0:T(8,128)S(1)} %get-tuple-element.18.gate_in, bf16[2,128,128]{2,1,0:T(8,128)(2,1)S(1)} %copy-done.3), custom_call_target="tpu_custom_call" | custom-call | tf_op jit(solution)/shard_map/end/pallas_call | solution.py:524
Async XLA Ops:
  52.1 26.9 %copy-start = (f32[128,3200]{1,0:T(8,128)S(1)}, f32[128,3200]{1,0:T(8,128)}, u32[]{:S(2)}) copy-start(f32[128,3200]{1,0:T(8,128)} %get-tuple-element.15.gate_in) | copy-start | bytes 4915204
  52.1 26.9 %copy-start.1 = (f32[128,3200]{1,0:T(8,128)S(1)}, f32[128,3200]{1,0:T(8,128)}, u32[]{:S(2)}) copy-start(f32[128,3200]{1,0:T(8,128)} %get-tuple-element.14.field_in) | copy-start | bytes 4915204
  52.1 26.9 %copy-start.2 = (bf16[2,128,640]{2,1,0:T(8,128)(2,1)S(1)}, bf16[2,128,640]{2,1,0:T(8,128)(2,1)}, u32[]{:S(2)}) copy-start(bf16[2,128,640]{2,1,0:T(8,128)(2,1)} %w_ref.1) | copy-start | bytes 983044
  52.1 27.0 %copy-start.3 = (bf16[2,128,128]{2,1,0:T(8,128)(2,1)S(1)}, bf16[2,128,128]{2,1,0:T(8,128)(2,1)}, u32[]{:S(2)}) copy-start(bf16[2,128,128]{2,1,0:T(8,128)(2,1)} %wo_ref.3) | copy-start | bytes 196612
  52.1 27.0 %copy-start.4 = (f32[1,3200]{1,0:T(1,128)S(1)}, f32[1,3200]{1,0:T(1,128)}, u32[]{:S(2)}) copy-start(f32[1,3200]{1,0:T(1,128)} %get-tuple-element.12.mask_ref) | copy-start | bytes 38404

commit v6 on v5

--- a/solution.py
+++ b/solution.py
@@ -191,10 +191,11 @@
 def middle_kernel(share, rows, cols, line, mask_ref, got_ref, field_in, gate_in, wo_ref, w_ref,
                   sent_ref, gate_ref, field_ref, wide):
     lanes = SUB * cols
-    half = got_ref.shape[0] // 2
+    count = got_ref.shape[0]
+    half = count // 2
     wide[:half, :] = got_ref[:half, :].astype(F32)
     out_t = transposed(wo_ref[0], 0.5)
-    wide[half:, :] = got_ref[half:, :].astype(F32)
+    wide[half:count, :] = got_ref[half:, :].astype(F32)
     in_t = load_in_weights(w_ref[1], share)
 
     def span(group):
@@ -218,7 +219,7 @@
 def end_kernel(rows, cols, line, got_ref, field_in, gate_in, wo_ref, out_hbm, wide, out_ref, sems):
     lanes = SUB * cols
     out_t = transposed(wo_ref[1], 0.5)
-    wide[...] = got_ref[...].astype(F32)
+    wide[: got_ref.shape[0], :] = got_ref[...].astype(F32)
     copies = []
 
     def outgoing(group, _):
@@ -380,7 +381,7 @@
     def product(channel):
         spare = channel % 2
         if direction == 0:
-            right = [even_ref[spare, block].astype(BF16) for block in range(blocks)]
+            right = [even_ref[spare, block, 0:total].astype(BF16) for block in range(blocks)]
             right = jnp.concatenate(right, axis=1)
             summed = matmul(left_ref[spare], right, ((1,), (1,)))
         else:
@@ -402,6 +403,19 @@
                     packed[pl.ds(start, row_devices, stride=share * line), :] = (
                         both[half * SUB : (half + 1) * SUB]
                     )
+        missing.difference_update(targets)
+
+    missing = set((channel, group) for channel in range(share) for group in range(groups))
+    waiting = list(range(sent_ref.shape[0] // (2 * SUB)))
+
+    def finish():
+        for unit in list(waiting):
+            lines = range(unit * 2 * SUB, (unit + 1) * 2 * SUB)
+            if any((at // line % share, at % line // pieces) in missing for at in lines):
+                continue
+            waiting.remove(unit)
+            at = slice(unit * 2 * SUB, (unit + 1) * 2 * SUB)
+            sent_ref[at, :] = packed[at, :].astype(BF16)
 
     def pack(channel):
         for pair in range(groups // 2):
@@ -436,8 +450,10 @@
             pack(channel - 1)
         if channel + 1 < share:
             unpack(channel + 1)
+        else:
+            finish()
     pack(share - 1)
-    sent_ref[...] = packed[...].astype(BF16)
+    finish()
 
 
 def by_channels(pair, token_mask, chain_ids, chain_bias, in_weights, out_weights, row_devices, col_devices):
@@ -461,6 +477,7 @@
     sum_shape = jax.ShapeDtypeStruct((devices * share * line, LANES), BF16)
     state_shape = jax.ShapeDtypeStruct((width, spots), F32)
     mask_shape = jax.ShapeDtypeStruct((1, spots), F32)
+    padded_sum = pltpu.VMEM((-(-(devices + 1) * share * line // SUB) * SUB, LANES), F32)
 
     def exchange(array, rows):
         shape = (devices, rows) if rows % SUB == 0 else (devices, rows * 2 // SUB, SUB // 2)
@@ -468,7 +485,7 @@
         return lax.all_to_all(split, ("col", "row"), 0, 0, tiled=True).reshape(devices * rows, LANES)
 
     def triangle(direction, sent):
-        wide_rows = row_devices * wide_steps(col_devices * groups * pieces)[1]
+        wide_rows = (row_devices + 1) * wide_steps(col_devices * groups * pieces)[1]
         summed = pl.pallas_call(
             functools.partial(
                 triangle_kernel, direction, share, rows, cols, row_devices, col_devices, line
@@ -480,9 +497,9 @@
                 pltpu.VMEM((-(-wide_rows // SUB) * SUB, LANES), F32),
                 pltpu.VMEM((2, tall, blocks * LANES), BF16),
                 pltpu.VMEM((2, tall, blocks * LANES), BF16),
-                pltpu.VMEM((2, blocks, total, LANES), F32),
+                pltpu.VMEM((2, blocks, total + rows, LANES), F32),
                 pltpu.VMEM((share, blocks, tall, LANES), BF16),
-                pltpu.VMEM(sum_shape.shape, F32),
+                padded_sum,
             ],
             compiler_params=params,
             name="triangle",
@@ -516,7 +533,7 @@
         out_shape=[sent_shape, state_shape, state_shape],
         in_specs=[whole] * 6,
         out_specs=[whole] * 3,
-        scratch_shapes=[pltpu.VMEM(sum_shape.shape, F32)],
+        scratch_shapes=[padded_sum],
         compiler_params=params,
         name="middle",
     )(mask, got, field, gate, out_weights, in_weights)
@@ -527,7 +544,7 @@
         in_specs=[whole] * 4,
         out_specs=far,
         scratch_shapes=[
-            pltpu.VMEM(sum_shape.shape, F32),
+            padded_sum,
             pltpu.VMEM((spots, width), BF16),
             pltpu.SemaphoreType.DMA((groups,)),
         ],

time: 153 us -> 153 us (level)
  no operation moved by 1% of the time
where the time goes in v6:
time: 153 us; the launch traced here: 152 us
  blocking collectives  139 us (91%)
  Pallas kernels  12.8 us (8%)
    all_to_all x4, blocking collectives, exchange(): lax.all_to_all(split, ('col', 'row'), 0, 0, tiled=True)  139 us
    pallas_call x1, Pallas kernels, by_channels(): pl.pallas_call(functools.partial(start_kernel, share, rows, cols), out_sh...  4.55 us
    pallas_call x2, Pallas kernels, triangle(): pl.pallas_call(functools.partial(triangle_kernel, direction, share, rows,...  4.44 us

profile of v6, /device:TPU:0, one launch (start us, length us, event | category | flops | bytes accessed | tf_op | source)
XLA Modules:
  0.0 152.3 jit_solution(12351177178023234158)
XLA Ops:
  0.0 4.5 %start.1 = (bf16[32,5,40,128]{3,2,1,0:T(8,128)(2,1)}, f32[128,3200]{1,0:T(8,128)}, f32[128,3200]{1,0:T(8,128)}, f32[1,3200]{1,0:T(1,128)}) custom-call(s32[320]{0:T(512)} %valid_hbm.1, s32[320]{0:T(512)} %chain_hbm.1, bf16[3200,128]{1,0:T(8,128)(2,1)} %bitcast.18, f32[128]{0:T(128)} %bias_hbm.1, bf16[2,128,640]{2,1,0:T(8,128)(2,1)} %w_ref.1), custom_call_target="tpu_custom_call" | custom-call | tf_op jit(solution)/shard_map/start/pallas_call | solution.py:510
  4.6 47.5 %all_to_all.20 = bf16[32,200,128]{2,1,0:T(8,128)(2,1)S(1)} all-to-all(bf16[32,200,128]{2,1,0:T(8,128)(2,1)} %bitcast.17), channel_id=1, replica_groups=mesh['row'=8,'col'=4] {'col','row'}, dimensions={0} | all-to-all | bytes 3276800 | tf_op jit(solution)/shard_map/all_to_all | solution.py:485
  52.1 0.0 copy-start
  52.1 0.0 copy-start.1
  52.1 0.0 copy-start.2
  52.1 0.0 copy-start.3
  52.1 0.0 copy-start.4
  52.1 2.2 %triangle.2 = bf16[3200,128]{1,0:T(8,128)(2,1)S(1)} custom-call(bf16[6400,128]{1,0:T(8,128)(2,1)S(1)} %bitcast.10), custom_call_target="tpu_custom_call" | custom-call | tf_op jit(solution)/shard_map/triangle/pallas_call | solution.py:489
  54.3 24.8 %all_to_all.21 = bf16[32,25,4,128]{3,2,1,0:T(4,128)(2,1)S(1)} all-to-all(bf16[32,25,4,128]{3,2,1,0:T(4,128)(2,1)S(1)} %bitcast.13), channel_id=1, replica_groups=mesh['row'=8,'col'=4] {'col','row'}, dimensions={0} | all-to-all | bytes 1638400 | tf_op jit(solution)/shard_map/all_to_all | solution.py:485
  79.0 0.0 copy-done
  79.0 0.0 copy-done.1
  79.0 0.0 copy-done.2
  79.1 0.0 copy-done.3
  79.1 0.0 copy-done.4
  79.1 2.2 %middle.1 = (bf16[32,5,40,128]{3,2,1,0:T(8,128)(2,1)S(1)}, f32[128,3200]{1,0:T(8,128)S(1)}, f32[128,3200]{1,0:T(8,128)S(1)}) custom-call(f32[1,3200]{1,0:T(1,128)S(1)} %copy-done.4, bf16[3200,128]{1,0:T(8,128)(2,1)S(1)} %bitcast.15, f32[128,3200]{1,0:T(8,128)S(1)} %copy-done.1, f32[128,3200]{1,0:T(8,128)S(1)} %copy-done, bf16[2,128,128]{2,1,0:T(8,128)(2,1)S(1)} %copy-done.3, ...), custom_call_target="tpu_custom_call" | custom-call | tf_op jit(solution)/shard_map/middle/pallas_call | solution.py:531
  81.3 42.3 %all_to_all.22 = bf16[32,200,128]{2,1,0:T(8,128)(2,1)S(1)} all-to-all(bf16[32,200,128]{2,1,0:T(8,128)(2,1)S(1)} %bitcast.16), channel_id=1, replica_groups=mesh['row'=8,'col'=4] {'col','row'}, dimensions={0} | all-to-all | bytes 3276800 | tf_op jit(solution)/shard_map/all_to_all | solution.py:485
  123.6 2.3 %triangle.3 = bf16[3200,128]{1,0:T(8,128)(2,1)S(1)} custom-call(bf16[6400,128]{1,0:T(8,128)(2,1)S(1)} %bitcast.11), custom_call_target="tpu_custom_call" | custom-call | tf_op jit(solution)/shard_map/triangle/pallas_call | solution.py:489
  125.9 24.8 %all_to_all.23 = bf16[32,25,4,128]{3,2,1,0:T(4,128)(2,1)S(1)} all-to-all(bf16[32,25,4,128]{3,2,1,0:T(4,128)(2,1)S(1)} %bitcast.14), channel_id=1, replica_groups=mesh['row'=8,'col'=4] {'col','row'}, dimensions={0} | all-to-all | bytes 1638400 | tf_op jit(solution)/shard_map/all_to_all | solution.py:485
  150.6 1.6 %end.1 = bf16[3200,128]{1,0:T(8,128)(2,1)} custom-call(bf16[3200,128]{1,0:T(8,128)(2,1)S(1)} %bitcast.12, f32[128,3200]{1,0:T(8,128)S(1)} %get-tuple-element.17.field_in, f32[128,3200]{1,0:T(8,128)S(1)} %get-tuple-element.18.gate_in, bf16[2,128,128]{2,1,0:T(8,128)(2,1)S(1)} %copy-done.3), custom_call_target="tpu_custom_call" | custom-call | tf_op jit(solution)/shard_map/end/pallas_call | solution.py:541
Async XLA Ops:
  52.1 26.9 %copy-start = (f32[128,3200]{1,0:T(8,128)S(1)}, f32[128,3200]{1,0:T(8,128)}, u32[]{:S(2)}) copy-start(f32[128,3200]{1,0:T(8,128)} %get-tuple-element.15.gate_in) | copy-start | bytes 4915204
  52.1 26.9 %copy-start.1 = (f32[128,3200]{1,0:T(8,128)S(1)}, f32[128,3200]{1,0:T(8,128)}, u32[]{:S(2)}) copy-start(f32[128,3200]{1,0:T(8,128)} %get-tuple-element.14.field_in) | copy-start | bytes 4915204
  52.1 26.9 %copy-start.2 = (bf16[2,128,640]{2,1,0:T(8,128)(2,1)S(1)}, bf16[2,128,640]{2,1,0:T(8,128)(2,1)}, u32[]{:S(2)}) copy-start(bf16[2,128,640]{2,1,0:T(8,128)(2,1)} %w_ref.1) | copy-start | bytes 983044
  52.1 26.9 %copy-start.3 = (bf16[2,128,128]{2,1,0:T(8,128)(2,1)S(1)}, bf16[2,128,128]{2,1,0:T(8,128)(2,1)}, u32[]{:S(2)}) copy-start(bf16[2,128,128]{2,1,0:T(8,128)(2,1)} %wo_ref.3) | copy-start | bytes 196612
  52.1 27.0 %copy-start.4 = (f32[1,3200]{1,0:T(1,128)S(1)}, f32[1,3200]{1,0:T(1,128)}, u32[]{:S(2)}) copy-start(f32[1,3200]{1,0:T(1,128)} %get-tuple-element.12.mask_ref) | copy-start | bytes 38404

commit v7 on v6

--- a/solution.py
+++ b/solution.py
@@ -113,7 +113,7 @@
 
 
 def start_kernel(share, rows, cols, valid_hbm, chain_hbm, pair_hbm, bias_hbm, w_hbm,
-                 sent_hbm, gate_hbm, field_hbm, mask_hbm, sent_ref, gate_ref, field_ref, mask_ref,
+                 sent_ref, gate_ref, field_ref, mask_ref,
                  pair_ref, w_ref, bias_ref, valid_ref, chain_ref, sems):
     lanes = SUB * cols
     groups = rows // SUB
@@ -162,20 +162,12 @@
         return field
 
     def project(group, field):
-        if group == groups - 1:
-            copy(field_ref, field_hbm)
-            copy(mask_ref, mask_hbm)
         return projected(field, in_t)
 
     def finish(group, products):
         gated(products, masks[group : group + 1], group, share, sent_ref, gate_ref)
-        copy(sent_ref.at[:, group], sent_hbm.at[:, group])
-        at = pl.ds(group * lanes, lanes)
-        copy(gate_ref.at[:, at], gate_hbm.at[:, at])
 
     staged(groups, (make_field, project, finish))
-    for number in range(arriving, len(started)):
-        started[number].wait()
 
 
 def output_of(wide, out_t, group, lanes, line):
@@ -511,22 +503,21 @@
         functools.partial(start_kernel, share, rows, cols),
         out_shape=[sent_shape, state_shape, state_shape, mask_shape],
         in_specs=[far] * 5,
-        out_specs=[far] * 4,
+        out_specs=[whole] * 4,
         scratch_shapes=[
-            pltpu.VMEM(sent_shape.shape, BF16),
-            pltpu.VMEM(state_shape.shape, F32),
-            pltpu.VMEM(state_shape.shape, F32),
-            pltpu.VMEM(mask_shape.shape, F32),
             pltpu.VMEM((spots, width), BF16),
             pltpu.VMEM(in_weights.shape[1:], BF16),
             pltpu.VMEM((1, width), F32),
             pltpu.VMEM((1,) + token_mask.shape, jnp.int32),
             pltpu.VMEM((1,) + chain_ids.shape, jnp.int32),
-            pltpu.SemaphoreType.DMA((8 + 2 * groups,)),
+            pltpu.SemaphoreType.DMA((6,)),
         ],
-        compiler_params=pltpu.CompilerParams(vmem_limit_bytes=60 * 1024 * 1024),
+        compiler_params=params,
         name="start",
-    )(token_mask, chain_ids, flat_pair, chain_bias, in_weights)
+    )(*[
+        pltpu.with_memory_space_constraint(array, pltpu.HBM)
+        for array in (token_mask, chain_ids, flat_pair, chain_bias, in_weights)
+    ])
     got = triangle(0, sent)
     sent, gate, field = pl.pallas_call(
         functools.partial(middle_kernel, share, rows, cols, line),

time: 153 us -> 151 us (0.987)
  no operation moved by 1% of the time
where the time goes in v7:
time: 151 us
  blocking collectives  139 us (92%)
  Pallas kernels  11.4 us (8%)
    all_to_all x4, blocking collectives, exchange(): lax.all_to_all(split, ('col', 'row'), 0, 0, tiled=True)  139 us
    pallas_call x2, Pallas kernels, triangle(): pl.pallas_call(functools.partial(triangle_kernel, direction, share, rows,...  4.44 us
    pallas_call x1, Pallas kernels, by_channels(): pl.pallas_call(functools.partial(start_kernel, share, rows, cols), out_sh...  3.14 us

profile of v7, /device:TPU:0, one launch (start us, length us, event | category | flops | bytes accessed | tf_op | source)
XLA Modules:
  0.0 150.6 jit_solution(5667360621321684317)
XLA Ops:
  0.0 3.1 %start.1 = (bf16[32,5,40,128]{3,2,1,0:T(8,128)(2,1)S(1)}, f32[128,3200]{1,0:T(8,128)S(1)}, f32[128,3200]{1,0:T(8,128)S(1)}, f32[1,3200]{1,0:T(1,128)S(1)}) custom-call(s32[320]{0:T(512)} %valid_hbm.1, s32[320]{0:T(512)} %chain_hbm.1, bf16[3200,128]{1,0:T(8,128)(2,1)} %bitcast.18, f32[128]{0:T(128)} %bias_hbm.1, bf16[2,128,640]{2,1,0:T(8,128)(2,1)} %w_ref.1), custom_call_target="tpu_custom_call" | custom-call | tf_op jit(solution)/shard_map/start/pallas_call | solution.py:502
  3.1 47.3 %all_to_all.20 = bf16[32,200,128]{2,1,0:T(8,128)(2,1)S(1)} all-to-all(bf16[32,200,128]{2,1,0:T(8,128)(2,1)S(1)} %bitcast.17), channel_id=1, replica_groups=mesh['row'=8,'col'=4] {'col','row'}, dimensions={0} | all-to-all | bytes 3276800 | tf_op jit(solution)/shard_map/all_to_all | solution.py:477
  50.5 0.0 copy-start
  50.5 0.0 copy-start.1
  50.5 2.2 %triangle.2 = bf16[3200,128]{1,0:T(8,128)(2,1)S(1)} custom-call(bf16[6400,128]{1,0:T(8,128)(2,1)S(1)} %bitcast.10), custom_call_target="tpu_custom_call" | custom-call | tf_op jit(solution)/shard_map/triangle/pallas_call | solution.py:481
  52.6 24.7 %all_to_all.21 = bf16[32,25,4,128]{3,2,1,0:T(4,128)(2,1)S(1)} all-to-all(bf16[32,25,4,128]{3,2,1,0:T(4,128)(2,1)S(1)} %bitcast.13), channel_id=1, replica_groups=mesh['row'=8,'col'=4] {'col','row'}, dimensions={0} | all-to-all | bytes 1638400 | tf_op jit(solution)/shard_map/all_to_all | solution.py:477
  77.4 0.0 copy-done
  77.4 0.0 copy-done.1
  77.4 2.2 %middle.1 = (bf16[32,5,40,128]{3,2,1,0:T(8,128)(2,1)S(1)}, f32[128,3200]{1,0:T(8,128)S(1)}, f32[128,3200]{1,0:T(8,128)S(1)}) custom-call(f32[1,3200]{1,0:T(1,128)S(1)} %get-tuple-element.12.mask_ref, bf16[3200,128]{1,0:T(8,128)(2,1)S(1)} %bitcast.15, f32[128,3200]{1,0:T(8,128)S(1)} %get-tuple-element.14.field_in, f32[128,3200]{1,0:T(8,128)S(1)} %get-tuple-element.15.gate_in, ...), custom_call_target="tpu_custom_call" | custom-call | tf_op jit(solution)/shard_map/middle/pallas_call | solution.py:522
  79.6 42.3 %all_to_all.22 = bf16[32,200,128]{2,1,0:T(8,128)(2,1)S(1)} all-to-all(bf16[32,200,128]{2,1,0:T(8,128)(2,1)S(1)} %bitcast.16), channel_id=1, replica_groups=mesh['row'=8,'col'=4] {'col','row'}, dimensions={0} | all-to-all | bytes 3276800 | tf_op jit(solution)/shard_map/all_to_all | solution.py:477
  121.9 2.3 %triangle.3 = bf16[3200,128]{1,0:T(8,128)(2,1)S(1)} custom-call(bf16[6400,128]{1,0:T(8,128)(2,1)S(1)} %bitcast.11), custom_call_target="tpu_custom_call" | custom-call | tf_op jit(solution)/shard_map/triangle/pallas_call | solution.py:481
  124.2 24.8 %all_to_all.23 = bf16[32,25,4,128]{3,2,1,0:T(4,128)(2,1)S(1)} all-to-all(bf16[32,25,4,128]{3,2,1,0:T(4,128)(2,1)S(1)} %bitcast.14), channel_id=1, replica_groups=mesh['row'=8,'col'=4] {'col','row'}, dimensions={0} | all-to-all | bytes 1638400 | tf_op jit(solution)/shard_map/all_to_all | solution.py:477
  149.0 1.6 %end.1 = bf16[3200,128]{1,0:T(8,128)(2,1)} custom-call(bf16[3200,128]{1,0:T(8,128)(2,1)S(1)} %bitcast.12, f32[128,3200]{1,0:T(8,128)S(1)} %get-tuple-element.17.field_in, f32[128,3200]{1,0:T(8,128)S(1)} %get-tuple-element.18.gate_in, bf16[2,128,128]{2,1,0:T(8,128)(2,1)S(1)} %copy-done.1), custom_call_target="tpu_custom_call" | custom-call | tf_op jit(solution)/shard_map/end/pallas_call | solution.py:532
Async XLA Ops:
  50.5 26.9 %copy-start = (bf16[2,128,640]{2,1,0:T(8,128)(2,1)S(1)}, bf16[2,128,640]{2,1,0:T(8,128)(2,1)}, u32[]{:S(2)}) copy-start(bf16[2,128,640]{2,1,0:T(8,128)(2,1)} %w_ref.1) | copy-start | bytes 983044
  50.5 26.9 %copy-start.1 = (bf16[2,128,128]{2,1,0:T(8,128)(2,1)S(1)}, bf16[2,128,128]{2,1,0:T(8,128)(2,1)}, u32[]{:S(2)}) copy-start(bf16[2,128,128]{2,1,0:T(8,128)(2,1)} %wo_ref.3) | copy-start | bytes 196612

commit v8 on v7

--- a/solution.py
+++ b/solution.py
@@ -9,6 +9,7 @@
 
 LANES = 128
 SUB = 8
+SPAN = 256
 F32 = jnp.float32
 BF16 = jnp.bfloat16
 
@@ -96,29 +97,36 @@
                 held[item] = stage(item, held.get(item))
 
 
+def spans(total):
+    return [slice(at, min(at + SPAN, total)) for at in range(0, total, SPAN)]
+
+
 def projected(field, in_t):
     normed = layer_norm(field, 0).astype(BF16)
     return [matmul(weights, normed, ((1,), (0,))) for weights in in_t]
 
 
-def gated(products, mask, group, share, sent_ref, gate_ref):
+def gated(products, mask, at, share, sent_ref, gate_ref):
     gates, values, gate = products
     width, lanes = gate.shape
     sent = (jnp.tanh(gates) * values + values) * mask
+    lines = slice(at.start // LANES * SUB, at.stop // LANES * SUB)
     for owner in range(width // share):
         block = sent[owner * 2 * share : (owner + 1) * 2 * share]
-        lines = [block[:, at : at + LANES] for at in range(0, lanes, LANES)]
-        sent_ref[owner, group] = jnp.concatenate(lines, axis=0).astype(BF16)
-    gate_ref[:, group * lanes : (group + 1) * lanes] = jnp.tanh(gate)
+        tiles = [block[:, lane : lane + LANES] for lane in range(0, lanes, LANES)]
+        sent_ref[owner, lines, :] = jnp.concatenate(tiles, axis=0).astype(BF16)
+    gate_ref[:, at] = jnp.tanh(gate)
 
 
 def start_kernel(share, rows, cols, valid_hbm, chain_hbm, pair_hbm, bias_hbm, w_hbm,
                  sent_ref, gate_ref, field_ref, mask_ref,
-                 pair_ref, w_ref, bias_ref, valid_ref, chain_ref, sems):
+                 same_ref, pair_ref, w_ref, bias_ref, valid_ref, chain_ref, sems):
     lanes = SUB * cols
     groups = rows // SUB
-    width = pair_ref.shape[1]
+    spots, width = pair_ref.shape
     count = valid_hbm.shape[0]
+    ranges = spans(spots)
+    first = ranges[len(ranges) // 3].start
     started = []
 
     def copy(near, far):
@@ -129,60 +137,60 @@
     copy(valid_hbm, valid_ref.at[0])
     copy(chain_hbm, chain_ref.at[0])
     copy(bias_hbm, bias_ref.at[0])
-    for at in (pl.ds(0, 2 * lanes), pl.ds(2 * lanes, (groups - 2) * lanes)):
+    for at in (pl.ds(0, first), pl.ds(first, spots - first)):
         copy(pair_hbm.at[at], pair_ref.at[at])
-    arriving = len(started)
     eye = identity(width, 1.0)
     row_start = lax.axis_index("row") * rows
     col_start = lax.axis_index("col") * cols
     started[0].wait()
     in_t = load_in_weights(w_ref[...], share)
-    for number in range(1, arriving - 1):
+    for number in range(1, len(started) - 1):
         started[number].wait()
 
-    def lift(group):
-        if group == 2:
-            started[arriving - 1].wait()
-        rows_of = pair_ref[group * lanes : (group + 1) * lanes, :]
-        return matmul(eye, rows_of, ((1,), (1,)))
+    def lift(item):
+        if ranges[item].start == first:
+            started[-1].wait()
+        return matmul(eye, pair_ref[ranges[item], :], ((1,), (1,)))
 
     lifted = {0: lift(0)}
     tokens = chain_ref[...] * 2 + valid_ref[...]
     tokens = jnp.concatenate([tokens, jnp.zeros((1, -count % LANES), jnp.int32)], axis=1)
     masks, sames = token_vectors(tokens, row_start, col_start, rows, cols)
+    for group in range(groups):
+        at = slice(group * lanes, (group + 1) * lanes)
+        mask_ref[:, at] = masks[group : group + 1]
+        same_ref[:, at] = sames[group : group + 1]
     bias_col = column(bias_ref)
 
-    def make_field(group, _):
-        at = slice(group * lanes, (group + 1) * lanes)
-        if group + 1 < groups:
-            lifted[group + 1] = lift(group + 1)
-        field = lifted.pop(group) + bias_col * sames[group : group + 1]
-        field_ref[:, at] = field
-        mask_ref[:, at] = masks[group : group + 1]
+    def make_field(item, _):
+        if item + 1 < len(ranges):
+            lifted[item + 1] = lift(item + 1)
+        field = lifted.pop(item) + bias_col * same_ref[:, ranges[item]]
+        field_ref[:, ranges[item]] = field
         return field
 
-    def project(group, field):
+    def project(item, field):
         return projected(field, in_t)
 
-    def finish(group, products):
-        gated(products, masks[group : group + 1], group, share, sent_ref, gate_ref)
-
-    staged(groups, (make_field, project, finish))
-
-
-def output_of(wide, out_t, group, lanes, line):
+    def finish(item, products):
+        at = ranges[item]
+        gated(products, mask_ref[:, at], at, share, sent_ref, gate_ref)
+
+    staged(len(ranges), (make_field, project, finish))
+
+
+def output_of(wide, out_t, at, line):
     width = out_t.shape[1]
-    pieces = lanes // LANES
     parts = []
-    for piece in range(pieces):
-        parts.append(wide[pl.ds(group * pieces + piece, width, stride=line), :])
+    for piece in range(at.start // LANES, at.stop // LANES):
+        parts.append(wide[pl.ds(piece, width, stride=line), :])
     normed = layer_norm(jnp.concatenate(parts, axis=1), 0).astype(BF16)
     return matmul(out_t, normed, ((1,), (0,)))
 
 
-def middle_kernel(share, rows, cols, line, mask_ref, got_ref, field_in, gate_in, wo_ref, w_ref,
+def middle_kernel(share, line, mask_ref, got_ref, field_in, gate_in, wo_ref, w_ref,
                   sent_ref, gate_ref, field_ref, wide):
-    lanes = SUB * cols
+    ranges = spans(field_in.shape[1])
     count = got_ref.shape[0]
     half = count // 2
     wide[:half, :] = got_ref[:half, :].astype(F32)
@@ -190,42 +198,43 @@
     wide[half:count, :] = got_ref[half:, :].astype(F32)
     in_t = load_in_weights(w_ref[1], share)
 
-    def span(group):
-        return slice(group * lanes, (group + 1) * lanes)
-
-    def outgoing(group, _):
-        return output_of(wide, out_t, group, lanes, line)
-
-    def project(group, output):
-        at = span(group)
+    def outgoing(item, _):
+        return output_of(wide, out_t, ranges[item], line)
+
+    def project(item, output):
+        at = ranges[item]
         field = field_in[:, at] + (gate_in[:, at] * output + output)
         field_ref[:, at] = field
         return projected(field, in_t)
 
-    def finish(group, products):
-        gated(products, mask_ref[:, span(group)], group, share, sent_ref, gate_ref)
-
-    staged(rows // SUB, (outgoing, project, finish))
-
-
-def end_kernel(rows, cols, line, got_ref, field_in, gate_in, wo_ref, out_hbm, wide, out_ref, sems):
-    lanes = SUB * cols
+    def finish(item, products):
+        at = ranges[item]
+        gated(products, mask_ref[:, at], at, share, sent_ref, gate_ref)
+
+    staged(len(ranges), (outgoing, project, finish))
+
+
+def end_kernel(line, got_ref, field_in, gate_in, wo_ref, out_hbm, wide, out_ref, sems):
+    ranges = spans(field_in.shape[1])
     out_t = transposed(wo_ref[1], 0.5)
     wide[: got_ref.shape[0], :] = got_ref[...].astype(F32)
     copies = []
-
-    def outgoing(group, _):
-        return output_of(wide, out_t, group, lanes, line)
-
-    def finish(group, output):
-        at = slice(group * lanes, (group + 1) * lanes)
+    done = [0]
+
+    def outgoing(item, _):
+        return output_of(wide, out_t, ranges[item], line)
+
+    def finish(item, output):
+        at = ranges[item]
         field = field_in[:, at] + (gate_in[:, at] * output + output)
         out_ref[at, :] = field.astype(BF16).T
-        at = pl.ds(group * lanes, lanes)
-        copies.append(pltpu.make_async_copy(out_ref.at[at], out_hbm.at[at], sems.at[group]))
-        copies[-1].start()
-
-    staged(rows // SUB, (outgoing, finish))
+        if item % 3 == 0 or item == len(ranges) - 1:
+            rows = pl.ds(done[0], at.stop - done[0])
+            done[0] = at.stop
+            copies.append(pltpu.make_async_copy(out_ref.at[rows], out_hbm.at[rows], sems.at[len(copies)]))
+            copies[-1].start()
+
+    staged(len(ranges), (outgoing, finish))
     for copy in copies:
         copy.wait()
 
@@ -465,7 +474,7 @@
     whole = pl.BlockSpec(memory_space=pltpu.VMEM)
     far = pl.BlockSpec(memory_space=pltpu.HBM)
 
-    sent_shape = jax.ShapeDtypeStruct((devices, groups, pieces * SUB, LANES), BF16)
+    sent_shape = jax.ShapeDtypeStruct((devices, chunk, LANES), BF16)
     sum_shape = jax.ShapeDtypeStruct((devices * share * line, LANES), BF16)
     state_shape = jax.ShapeDtypeStruct((width, spots), F32)
     mask_shape = jax.ShapeDtypeStruct((1, spots), F32)
@@ -505,6 +514,7 @@
         in_specs=[far] * 5,
         out_specs=[whole] * 4,
         scratch_shapes=[
+            pltpu.VMEM(mask_shape.shape, F32),
             pltpu.VMEM((spots, width), BF16),
             pltpu.VMEM(in_weights.shape[1:], BF16),
             pltpu.VMEM((1, width), F32),
@@ -520,7 +530,7 @@
     ])
     got = triangle(0, sent)
     sent, gate, field = pl.pallas_call(
-        functools.partial(middle_kernel, share, rows, cols, line),
+        functools.partial(middle_kernel, share, line),
         out_shape=[sent_shape, state_shape, state_shape],
         in_specs=[whole] * 6,
         out_specs=[whole] * 3,
@@ -530,14 +540,14 @@
     )(mask, got, field, gate, out_weights, in_weights)
     got = triangle(1, sent)
     out = pl.pallas_call(
-        functools.partial(end_kernel, rows, cols, line),
+        functools.partial(end_kernel, line),
         out_shape=jax.ShapeDtypeStruct((spots, width), BF16),
         in_specs=[whole] * 4,
         out_specs=far,
         scratch_shapes=[
             padded_sum,
             pltpu.VMEM((spots, width), BF16),
-            pltpu.SemaphoreType.DMA((groups,)),
+            pltpu.SemaphoreType.DMA((len(spans(spots)),)),
         ],
         compiler_params=params,
         name="end",

time: 151 us -> 152 us (level)
  no operation moved by 1% of the time
where the time goes in v8:
time: 152 us
  blocking collectives  139 us (91%)
  Pallas kernels  12.5 us (8%)
    all_to_all x4, blocking collectives, exchange(): lax.all_to_all(split, ('col', 'row'), 0, 0, tiled=True)  139 us
    pallas_call x2, Pallas kernels, triangle(): pl.pallas_call(functools.partial(triangle_kernel, direction, share, rows,...  4.44 us
    pallas_call x1, Pallas kernels, by_channels(): pl.pallas_call(functools.partial(start_kernel, share, rows, cols), out_sh...  3.79 us

profile of v8, /device:TPU:0, one launch (start us, length us, event | category | flops | bytes accessed | tf_op | source)
XLA Modules:
  0.0 151.7 jit_solution(2595595102446959004)
XLA Ops:
  0.0 3.8 %start.1 = (bf16[32,200,128]{2,1,0:T(8,128)(2,1)S(1)}, f32[128,3200]{1,0:T(8,128)S(1)}, f32[128,3200]{1,0:T(8,128)S(1)}, f32[1,3200]{1,0:T(1,128)S(1)}) custom-call(s32[320]{0:T(512)} %valid_hbm.1, s32[320]{0:T(512)} %chain_hbm.1, bf16[3200,128]{1,0:T(8,128)(2,1)} %bitcast.14, f32[128]{0:T(128)} %bias_hbm.1, bf16[2,128,640]{2,1,0:T(8,128)(2,1)} %w_ref.1), custom_call_target="tpu_custom_call" | custom-call | tf_op jit(solution)/shard_map/start/pallas_call | solution.py:511
  3.8 47.3 %all_to_all.20 = bf16[32,200,128]{2,1,0:T(8,128)(2,1)S(1)} all-to-all(bf16[32,200,128]{2,1,0:T(8,128)(2,1)S(1)} %get-tuple-element.13), channel_id=1, replica_groups=mesh['row'=8,'col'=4] {'col','row'}, dimensions={0} | all-to-all | bytes 3276800 | tf_op jit(solution)/shard_map/all_to_all | solution.py:486
  51.1 0.0 copy-start
  51.1 0.0 copy-start.1
  51.1 2.2 %triangle.2 = bf16[3200,128]{1,0:T(8,128)(2,1)S(1)} custom-call(bf16[6400,128]{1,0:T(8,128)(2,1)S(1)} %bitcast.8), custom_call_target="tpu_custom_call" | custom-call | tf_op jit(solution)/shard_map/triangle/pallas_call | solution.py:490
  53.3 24.7 %all_to_all.21 = bf16[32,25,4,128]{3,2,1,0:T(4,128)(2,1)S(1)} all-to-all(bf16[32,25,4,128]{3,2,1,0:T(4,128)(2,1)S(1)} %bitcast.11), channel_id=1, replica_groups=mesh['row'=8,'col'=4] {'col','row'}, dimensions={0} | all-to-all | bytes 1638400 | tf_op jit(solution)/shard_map/all_to_all | solution.py:486
  78.1 0.0 copy-done
  78.1 0.0 copy-done.1
  78.1 2.6 %middle.1 = (bf16[32,200,128]{2,1,0:T(8,128)(2,1)S(1)}, f32[128,3200]{1,0:T(8,128)S(1)}, f32[128,3200]{1,0:T(8,128)S(1)}) custom-call(f32[1,3200]{1,0:T(1,128)S(1)} %get-tuple-element.12.mask_ref, bf16[3200,128]{1,0:T(8,128)(2,1)S(1)} %bitcast.13, f32[128,3200]{1,0:T(8,128)S(1)} %get-tuple-element.14.field_in, f32[128,3200]{1,0:T(8,128)S(1)} %get-tuple-element.15.gate_in, ...), custom_call_target="tpu_custom_call" | custom-call | tf_op jit(solution)/shard_map/middle/pallas_call | solution.py:532
  80.7 42.3 %all_to_all.22 = bf16[32,200,128]{2,1,0:T(8,128)(2,1)S(1)} all-to-all(bf16[32,200,128]{2,1,0:T(8,128)(2,1)S(1)} %get-tuple-element.16), channel_id=1, replica_groups=mesh['row'=8,'col'=4] {'col','row'}, dimensions={0} | all-to-all | bytes 3276800 | tf_op jit(solution)/shard_map/all_to_all | solution.py:486
  123.0 2.3 %triangle.3 = bf16[3200,128]{1,0:T(8,128)(2,1)S(1)} custom-call(bf16[6400,128]{1,0:T(8,128)(2,1)S(1)} %bitcast.9), custom_call_target="tpu_custom_call" | custom-call | tf_op jit(solution)/shard_map/triangle/pallas_call | solution.py:490
  125.3 24.7 %all_to_all.23 = bf16[32,25,4,128]{3,2,1,0:T(4,128)(2,1)S(1)} all-to-all(bf16[32,25,4,128]{3,2,1,0:T(4,128)(2,1)S(1)} %bitcast.12), channel_id=1, replica_groups=mesh['row'=8,'col'=4] {'col','row'}, dimensions={0} | all-to-all | bytes 1638400 | tf_op jit(solution)/shard_map/all_to_all | solution.py:486
  150.0 1.7 %end.1 = bf16[3200,128]{1,0:T(8,128)(2,1)} custom-call(bf16[3200,128]{1,0:T(8,128)(2,1)S(1)} %bitcast.10, f32[128,3200]{1,0:T(8,128)S(1)} %get-tuple-element.17.field_in, f32[128,3200]{1,0:T(8,128)S(1)} %get-tuple-element.18.gate_in, bf16[2,128,128]{2,1,0:T(8,128)(2,1)S(1)} %copy-done.1), custom_call_target="tpu_custom_call" | custom-call | tf_op jit(solution)/shard_map/end/pallas_call | solution.py:542
Async XLA Ops:
  51.1 26.9 %copy-start = (bf16[2,128,640]{2,1,0:T(8,128)(2,1)S(1)}, bf16[2,128,640]{2,1,0:T(8,128)(2,1)}, u32[]{:S(2)}) copy-start(bf16[2,128,640]{2,1,0:T(8,128)(2,1)} %w_ref.1) | copy-start | bytes 983044
  51.1 26.9 %copy-start.1 = (bf16[2,128,128]{2,1,0:T(8,128)(2,1)S(1)}, bf16[2,128,128]{2,1,0:T(8,128)(2,1)}, u32[]{:S(2)}) copy-start(bf16[2,128,128]{2,1,0:T(8,128)(2,1)} %wo_ref.3) | copy-start | bytes 196612

commit v9 on v8

--- a/solution.py
+++ b/solution.py
@@ -9,7 +9,7 @@
 
 LANES = 128
 SUB = 8
-SPAN = 256
+SPAN = 1280
 F32 = jnp.float32
 BF16 = jnp.bfloat16
 

time: 152 us -> 151 us (level)
  no operation moved by 1% of the time
where the time goes in v9:
time: 151 us
  blocking collectives  139 us (92%)
  Pallas kernels  11.6 us (8%)
    all_to_all x4, blocking collectives, exchange(): lax.all_to_all(split, ('col', 'row'), 0, 0, tiled=True)  139 us
    pallas_call x2, Pallas kernels, triangle(): pl.pallas_call(functools.partial(triangle_kernel, direction, share, rows,...  4.44 us
    pallas_call x1, Pallas kernels, by_channels(): pl.pallas_call(functools.partial(start_kernel, share, rows, cols), out_sh...  3.25 us

profile of v9, /device:TPU:0, one launch (start us, length us, event | category | flops | bytes accessed | tf_op | source)
XLA Modules:
  0.0 150.8 jit_solution(16304759834073429635)
XLA Ops:
  0.0 3.2 %start.1 = (bf16[32,200,128]{2,1,0:T(8,128)(2,1)S(1)}, f32[128,3200]{1,0:T(8,128)S(1)}, f32[128,3200]{1,0:T(8,128)S(1)}, f32[1,3200]{1,0:T(1,128)S(1)}) custom-call(s32[320]{0:T(512)} %valid_hbm.1, s32[320]{0:T(512)} %chain_hbm.1, bf16[3200,128]{1,0:T(8,128)(2,1)} %bitcast.14, f32[128]{0:T(128)} %bias_hbm.1, bf16[2,128,640]{2,1,0:T(8,128)(2,1)} %w_ref.1), custom_call_target="tpu_custom_call" | custom-call | tf_op jit(solution)/shard_map/start/pallas_call | solution.py:511
  3.3 47.3 %all_to_all.20 = bf16[32,200,128]{2,1,0:T(8,128)(2,1)S(1)} all-to-all(bf16[32,200,128]{2,1,0:T(8,128)(2,1)S(1)} %get-tuple-element.13), channel_id=1, replica_groups=mesh['row'=8,'col'=4] {'col','row'}, dimensions={0} | all-to-all | bytes 3276800 | tf_op jit(solution)/shard_map/all_to_all | solution.py:486
  50.6 0.0 copy-start
  50.6 0.0 copy-start.1
  50.6 2.2 %triangle.2 = bf16[3200,128]{1,0:T(8,128)(2,1)S(1)} custom-call(bf16[6400,128]{1,0:T(8,128)(2,1)S(1)} %bitcast.8), custom_call_target="tpu_custom_call" | custom-call | tf_op jit(solution)/shard_map/triangle/pallas_call | solution.py:490
  52.8 24.8 %all_to_all.21 = bf16[32,25,4,128]{3,2,1,0:T(4,128)(2,1)S(1)} all-to-all(bf16[32,25,4,128]{3,2,1,0:T(4,128)(2,1)S(1)} %bitcast.11), channel_id=1, replica_groups=mesh['row'=8,'col'=4] {'col','row'}, dimensions={0} | all-to-all | bytes 1638400 | tf_op jit(solution)/shard_map/all_to_all | solution.py:486
  77.5 0.0 copy-done
  77.5 0.0 copy-done.1
  77.5 2.3 %middle.1 = (bf16[32,200,128]{2,1,0:T(8,128)(2,1)S(1)}, f32[128,3200]{1,0:T(8,128)S(1)}, f32[128,3200]{1,0:T(8,128)S(1)}) custom-call(f32[1,3200]{1,0:T(1,128)S(1)} %get-tuple-element.12.mask_ref, bf16[3200,128]{1,0:T(8,128)(2,1)S(1)} %bitcast.13, f32[128,3200]{1,0:T(8,128)S(1)} %get-tuple-element.14.field_in, f32[128,3200]{1,0:T(8,128)S(1)} %get-tuple-element.15.gate_in, ...), custom_call_target="tpu_custom_call" | custom-call | tf_op jit(solution)/shard_map/middle/pallas_call | solution.py:532
  79.8 42.3 %all_to_all.22 = bf16[32,200,128]{2,1,0:T(8,128)(2,1)S(1)} all-to-all(bf16[32,200,128]{2,1,0:T(8,128)(2,1)S(1)} %get-tuple-element.16), channel_id=1, replica_groups=mesh['row'=8,'col'=4] {'col','row'}, dimensions={0} | all-to-all | bytes 3276800 | tf_op jit(solution)/shard_map/all_to_all | solution.py:486
  122.1 2.3 %triangle.3 = bf16[3200,128]{1,0:T(8,128)(2,1)S(1)} custom-call(bf16[6400,128]{1,0:T(8,128)(2,1)S(1)} %bitcast.9), custom_call_target="tpu_custom_call" | custom-call | tf_op jit(solution)/shard_map/triangle/pallas_call | solution.py:490
  124.4 24.7 %all_to_all.23 = bf16[32,25,4,128]{3,2,1,0:T(4,128)(2,1)S(1)} all-to-all(bf16[32,25,4,128]{3,2,1,0:T(4,128)(2,1)S(1)} %bitcast.12), channel_id=1, replica_groups=mesh['row'=8,'col'=4] {'col','row'}, dimensions={0} | all-to-all | bytes 1638400 | tf_op jit(solution)/shard_map/all_to_all | solution.py:486
  149.1 1.7 %end.1 = bf16[3200,128]{1,0:T(8,128)(2,1)} custom-call(bf16[3200,128]{1,0:T(8,128)(2,1)S(1)} %bitcast.10, f32[128,3200]{1,0:T(8,128)S(1)} %get-tuple-element.17.field_in, f32[128,3200]{1,0:T(8,128)S(1)} %get-tuple-element.18.gate_in, bf16[2,128,128]{2,1,0:T(8,128)(2,1)S(1)} %copy-done.1), custom_call_target="tpu_custom_call" | custom-call | tf_op jit(solution)/shard_map/end/pallas_call | solution.py:542
Async XLA Ops:
  50.6 26.9 %copy-start = (bf16[2,128,640]{2,1,0:T(8,128)(2,1)S(1)}, bf16[2,128,640]{2,1,0:T(8,128)(2,1)}, u32[]{:S(2)}) copy-start(bf16[2,128,640]{2,1,0:T(8,128)(2,1)} %w_ref.1) | copy-start | bytes 983044
  50.6 26.9 %copy-start.1 = (bf16[2,128,128]{2,1,0:T(8,128)(2,1)S(1)}, bf16[2,128,128]{2,1,0:T(8,128)(2,1)}, u32[]{:S(2)}) copy-start(bf16[2,128,128]{2,1,0:T(8,128)(2,1)} %wo_ref.3) | copy-start | bytes 196612

commit v10 on v7

--- a/solution.py
+++ b/solution.py
@@ -180,15 +180,11 @@
     return matmul(out_t, normed, ((1,), (0,)))
 
 
-def middle_kernel(share, rows, cols, line, mask_ref, got_ref, field_in, gate_in, wo_ref, w_ref,
+def middle_kernel(share, rows, cols, line, mask_ref, got_ref, field_in, gate_in, prepared,
                   sent_ref, gate_ref, field_ref, wide):
     lanes = SUB * cols
-    count = got_ref.shape[0]
-    half = count // 2
-    wide[:half, :] = got_ref[:half, :].astype(F32)
-    out_t = transposed(wo_ref[0], 0.5)
-    wide[half:count, :] = got_ref[half:, :].astype(F32)
-    in_t = load_in_weights(w_ref[1], share)
+    *in_t, out_t, _ = prepared_parts(prepared)
+    wide[: got_ref.shape[0], :] = got_ref[...].astype(F32)
 
     def span(group):
         return slice(group * lanes, (group + 1) * lanes)
@@ -208,9 +204,9 @@
     staged(rows // SUB, (outgoing, project, finish))
 
 
-def end_kernel(rows, cols, line, got_ref, field_in, gate_in, wo_ref, out_hbm, wide, out_ref, sems):
+def end_kernel(rows, cols, line, got_ref, field_in, gate_in, prepared, out_hbm, wide, out_ref, sems):
     lanes = SUB * cols
-    out_t = transposed(wo_ref[1], 0.5)
+    out_t = prepared_parts(prepared)[-1]
     wide[: got_ref.shape[0], :] = got_ref[...].astype(F32)
     copies = []
 
@@ -280,8 +276,23 @@
     return jnp.concatenate([low, high], axis=0).astype(BF16)
 
 
-def triangle_kernel(direction, share, rows, cols, row_devices, col_devices, line, got_ref, sent_ref,
-                    wide, left_ref, right_ref, even_ref, result_ref, packed):
+def prepare_weights(w_ref, wo_ref, share, prepared):
+    parts = [*load_in_weights(w_ref[1], share), transposed(wo_ref[0], 0.5), transposed(wo_ref[1], 0.5)]
+    prepared[...] = jnp.concatenate(parts, axis=0)
+
+
+def prepared_parts(prepared):
+    width = prepared.shape[1]
+    cuts = [0, 2, 4, 5, 6, 7]
+    return [prepared[low * width : high * width, :] for low, high in zip(cuts, cuts[1:])]
+
+
+def triangle_kernel(direction, share, rows, cols, row_devices, col_devices, line, *refs):
+    if direction == 0:
+        got_ref, w_ref, wo_ref, sent_ref, prepared, *refs = refs
+    else:
+        got_ref, sent_ref, *refs = refs
+    wide, left_ref, right_ref, even_ref, result_ref, packed = refs
     groups = rows // SUB
     pieces = SUB * cols // LANES
     total = row_devices * rows
@@ -435,6 +446,8 @@
     for pair in range(pairs):
         if pair + 1 < pairs:
             widen(pair + 1)
+        elif direction == 0:
+            prepare_weights(w_ref, wo_ref, share, prepared)
         unpack(0, [pair])
     for channel in range(share):
         product(channel)
@@ -469,6 +482,7 @@
     sum_shape = jax.ShapeDtypeStruct((devices * share * line, LANES), BF16)
     state_shape = jax.ShapeDtypeStruct((width, spots), F32)
     mask_shape = jax.ShapeDtypeStruct((1, spots), F32)
+    prepared_shape = jax.ShapeDtypeStruct((7 * width, width), BF16)
     padded_sum = pltpu.VMEM((-(-(devices + 1) * share * line // SUB) * SUB, LANES), F32)
 
     def exchange(array, rows):
@@ -476,15 +490,15 @@
         split = array.reshape(*shape, LANES)
         return lax.all_to_all(split, ("col", "row"), 0, 0, tiled=True).reshape(devices * rows, LANES)
 
-    def triangle(direction, sent):
+    def triangle(direction, sent, *weights):
         wide_rows = (row_devices + 1) * wide_steps(col_devices * groups * pieces)[1]
-        summed = pl.pallas_call(
+        summed, *prepared = pl.pallas_call(
             functools.partial(
                 triangle_kernel, direction, share, rows, cols, row_devices, col_devices, line
             ),
-            out_shape=sum_shape,
-            in_specs=[whole],
-            out_specs=whole,
+            out_shape=[sum_shape] + [prepared_shape] * (len(weights) // 2),
+            in_specs=[whole] * (1 + len(weights)),
+            out_specs=[whole] * (1 + len(weights) // 2),
             scratch_shapes=[
                 pltpu.VMEM((-(-wide_rows // SUB) * SUB, LANES), F32),
                 pltpu.VMEM((2, tall, blocks * LANES), BF16),
@@ -495,8 +509,8 @@
             ],
             compiler_params=params,
             name="triangle",
-        )(exchange(sent, chunk))
-        return exchange(summed, share * line)
+        )(exchange(sent, chunk), *weights)
+        return exchange(summed, share * line), *prepared
 
     flat_pair = pair.reshape(spots, width)
     sent, gate, field, mask = pl.pallas_call(
@@ -518,17 +532,17 @@
         pltpu.with_memory_space_constraint(array, pltpu.HBM)
         for array in (token_mask, chain_ids, flat_pair, chain_bias, in_weights)
     ])
-    got = triangle(0, sent)
+    got, prepared = triangle(0, sent, in_weights, out_weights)
     sent, gate, field = pl.pallas_call(
         functools.partial(middle_kernel, share, rows, cols, line),
         out_shape=[sent_shape, state_shape, state_shape],
-        in_specs=[whole] * 6,
+        in_specs=[whole] * 5,
         out_specs=[whole] * 3,
         scratch_shapes=[padded_sum],
         compiler_params=params,
         name="middle",
-    )(mask, got, field, gate, out_weights, in_weights)
-    got = triangle(1, sent)
+    )(mask, got, field, gate, prepared)
+    (got,) = triangle(1, sent)
     out = pl.pallas_call(
         functools.partial(end_kernel, rows, cols, line),
         out_shape=jax.ShapeDtypeStruct((spots, width), BF16),
@@ -541,7 +555,7 @@
         ],
         compiler_params=params,
         name="end",
-    )(got, field, gate, out_weights)
+    )(got, field, gate, prepared)
     return out.reshape(pair.shape)
 
 

time: 151 us -> 151 us (level)
  no operation moved by 1% of the time
where the time goes in v10:
time: 151 us
  blocking collectives  139 us (92%)
  Pallas kernels  11.3 us (7%)
    all_to_all x4, blocking collectives, exchange(): lax.all_to_all(split, ('col', 'row'), 0, 0, tiled=True)  139 us
    pallas_call x2, Pallas kernels, triangle(): pl.pallas_call(functools.partial(triangle_kernel, direction, share, rows,...  4.49 us
    pallas_call x1, Pallas kernels, by_channels(): pl.pallas_call(functools.partial(start_kernel, share, rows, cols), out_sh...  3.14 us

profile of v10, /device:TPU:0, one launch (start us, length us, event | category | flops | bytes accessed | tf_op | source)
XLA Modules:
  0.0 150.5 jit_solution(154025218930148189)
XLA Ops:
  0.0 3.1 %start.1 = (bf16[32,5,40,128]{3,2,1,0:T(8,128)(2,1)S(1)}, f32[128,3200]{1,0:T(8,128)S(1)}, f32[128,3200]{1,0:T(8,128)S(1)}, f32[1,3200]{1,0:T(1,128)S(1)}) custom-call(s32[320]{0:T(512)} %valid_hbm.1, s32[320]{0:T(512)} %chain_hbm.1, bf16[3200,128]{1,0:T(8,128)(2,1)} %bitcast.18, f32[128]{0:T(128)} %bias_hbm.1, bf16[2,128,640]{2,1,0:T(8,128)(2,1)} %refs_1_.1), custom_call_target="tpu_custom_call" | custom-call | tf_op jit(solution)/shard_map/start/pallas_call | solution.py:516
  3.1 0.0 copy-start
  3.2 0.0 copy-start.1
  3.2 47.3 %all_to_all.20 = bf16[32,200,128]{2,1,0:T(8,128)(2,1)S(1)} all-to-all(bf16[32,200,128]{2,1,0:T(8,128)(2,1)S(1)} %bitcast.16), channel_id=1, replica_groups=mesh['row'=8,'col'=4] {'col','row'}, dimensions={0} | all-to-all | bytes 3276800 | tf_op jit(solution)/shard_map/all_to_all | solution.py:491
  50.5 0.0 copy-done
  50.5 0.0 copy-done.1
  50.5 2.2 %triangle.2 = (bf16[3200,128]{1,0:T(8,128)(2,1)S(1)}, bf16[896,128]{1,0:T(8,128)(2,1)S(1)}) custom-call(bf16[6400,128]{1,0:T(8,128)(2,1)S(1)} %bitcast.10, bf16[2,128,640]{2,1,0:T(8,128)(2,1)S(1)} %copy-done, bf16[2,128,128]{2,1,0:T(8,128)(2,1)S(1)} %copy-done.1), custom_call_target="tpu_custom_call" | custom-call | tf_op jit(solution)/shard_map/triangle/pallas_call | solution.py:495
  52.7 24.7 %all_to_all.21 = bf16[32,25,4,128]{3,2,1,0:T(4,128)(2,1)S(1)} all-to-all(bf16[32,25,4,128]{3,2,1,0:T(4,128)(2,1)S(1)} %bitcast.17), channel_id=1, replica_groups=mesh['row'=8,'col'=4] {'col','row'}, dimensions={0} | all-to-all | bytes 1638400 | tf_op jit(solution)/shard_map/all_to_all | solution.py:491
  77.5 2.1 %middle.1 = (bf16[32,5,40,128]{3,2,1,0:T(8,128)(2,1)S(1)}, f32[128,3200]{1,0:T(8,128)S(1)}, f32[128,3200]{1,0:T(8,128)S(1)}) custom-call(f32[1,3200]{1,0:T(1,128)S(1)} %get-tuple-element.14.mask_ref, bf16[3200,128]{1,0:T(8,128)(2,1)S(1)} %bitcast.14, f32[128,3200]{1,0:T(8,128)S(1)} %get-tuple-element.17.field_in, f32[128,3200]{1,0:T(8,128)S(1)} %get-tuple-element.18.gate_in, ...), custom_call_target="tpu_custom_call" | custom-call | tf_op jit(solution)/shard_map/middle/pallas_call | solution.py:536
  79.6 42.3 %all_to_all.22 = bf16[32,200,128]{2,1,0:T(8,128)(2,1)S(1)} all-to-all(bf16[32,200,128]{2,1,0:T(8,128)(2,1)S(1)} %bitcast.15), channel_id=1, replica_groups=mesh['row'=8,'col'=4] {'col','row'}, dimensions={0} | all-to-all | bytes 3276800 | tf_op jit(solution)/shard_map/all_to_all | solution.py:491
  121.9 2.3 %triangle.3 = bf16[3200,128]{1,0:T(8,128)(2,1)S(1)} custom-call(bf16[6400,128]{1,0:T(8,128)(2,1)S(1)} %bitcast.11), custom_call_target="tpu_custom_call" | custom-call | tf_op jit(solution)/shard_map/triangle/pallas_call | solution.py:495
  124.2 24.7 %all_to_all.23 = bf16[32,25,4,128]{3,2,1,0:T(4,128)(2,1)S(1)} all-to-all(bf16[32,25,4,128]{3,2,1,0:T(4,128)(2,1)S(1)} %bitcast.13), channel_id=1, replica_groups=mesh['row'=8,'col'=4] {'col','row'}, dimensions={0} | all-to-all | bytes 1638400 | tf_op jit(solution)/shard_map/all_to_all | solution.py:491
  148.9 1.6 %end.1 = bf16[3200,128]{1,0:T(8,128)(2,1)} custom-call(bf16[3200,128]{1,0:T(8,128)(2,1)S(1)} %bitcast.12, f32[128,3200]{1,0:T(8,128)S(1)} %get-tuple-element.21.field_in, f32[128,3200]{1,0:T(8,128)S(1)} %get-tuple-element.22.gate_in, bf16[896,128]{1,0:T(8,128)(2,1)S(1)} %get-tuple-element.19.prepared), custom_call_target="tpu_custom_call" | custom-call | tf_op jit(solution)/shard_map/end/pallas_call | solution.py:546
Async XLA Ops:
  3.1 47.4 %copy-start = (bf16[2,128,640]{2,1,0:T(8,128)(2,1)S(1)}, bf16[2,128,640]{2,1,0:T(8,128)(2,1)}, u32[]{:S(2)}) copy-start(bf16[2,128,640]{2,1,0:T(8,128)(2,1)} %refs_1_.1) | copy-start | bytes 983044
  3.2 47.3 %copy-start.1 = (bf16[2,128,128]{2,1,0:T(8,128)(2,1)S(1)}, bf16[2,128,128]{2,1,0:T(8,128)(2,1)}, u32[]{:S(2)}) copy-start(bf16[2,128,128]{2,1,0:T(8,128)(2,1)} %refs_2_.1) | copy-start | bytes 196612

commit v11 on v10

--- a/solution.py
+++ b/solution.py
@@ -96,8 +96,19 @@
                 held[item] = stage(item, held.get(item))
 
 
-def projected(field, in_t):
-    normed = layer_norm(field, 0).astype(BF16)
+def statistics(values):
+    center = values - jnp.mean(values, axis=0, keepdims=True)
+    spread = jnp.mean(center * center, axis=0, keepdims=True)
+    return center, lax.rsqrt(spread + 1e-05)
+
+
+def normalised(halves):
+    center, scale = halves
+    return (center * scale).astype(BF16)
+
+
+def projected(halves, in_t):
+    normed = normalised(halves)
     return [matmul(weights, normed, ((1,), (0,))) for weights in in_t]
 
 
@@ -159,10 +170,10 @@
         field = lifted.pop(group) + bias_col * sames[group : group + 1]
         field_ref[:, at] = field
         mask_ref[:, at] = masks[group : group + 1]
-        return field
-
-    def project(group, field):
-        return projected(field, in_t)
+        return statistics(field)
+
+    def project(group, halves):
+        return projected(halves, in_t)
 
     def finish(group, products):
         gated(products, masks[group : group + 1], group, share, sent_ref, gate_ref)
@@ -170,14 +181,12 @@
     staged(groups, (make_field, project, finish))
 
 
-def output_of(wide, out_t, group, lanes, line):
-    width = out_t.shape[1]
+def received(wide, width, group, lanes, line):
     pieces = lanes // LANES
     parts = []
     for piece in range(pieces):
         parts.append(wide[pl.ds(group * pieces + piece, width, stride=line), :])
-    normed = layer_norm(jnp.concatenate(parts, axis=1), 0).astype(BF16)
-    return matmul(out_t, normed, ((1,), (0,)))
+    return statistics(jnp.concatenate(parts, axis=1))
 
 
 def middle_kernel(share, rows, cols, line, mask_ref, got_ref, field_in, gate_in, prepared,
@@ -189,19 +198,25 @@
     def span(group):
         return slice(group * lanes, (group + 1) * lanes)
 
-    def outgoing(group, _):
-        return output_of(wide, out_t, group, lanes, line)
-
-    def project(group, output):
+    def receive(group, _):
+        return received(wide, out_t.shape[1], group, lanes, line)
+
+    def outgoing(group, halves):
+        return matmul(out_t, normalised(halves), ((1,), (0,)))
+
+    def update_field(group, output):
         at = span(group)
         field = field_in[:, at] + (gate_in[:, at] * output + output)
         field_ref[:, at] = field
-        return projected(field, in_t)
+        return statistics(field)
+
+    def project(group, halves):
+        return projected(halves, in_t)
 
     def finish(group, products):
         gated(products, mask_ref[:, span(group)], group, share, sent_ref, gate_ref)
 
-    staged(rows // SUB, (outgoing, project, finish))
+    staged(rows // SUB, (receive, outgoing, update_field, project, finish))
 
 
 def end_kernel(rows, cols, line, got_ref, field_in, gate_in, prepared, out_hbm, wide, out_ref, sems):
@@ -210,8 +225,11 @@
     wide[: got_ref.shape[0], :] = got_ref[...].astype(F32)
     copies = []
 
-    def outgoing(group, _):
-        return output_of(wide, out_t, group, lanes, line)
+    def receive(group, _):
+        return received(wide, out_t.shape[1], group, lanes, line)
+
+    def outgoing(group, halves):
+        return matmul(out_t, normalised(halves), ((1,), (0,)))
 
     def finish(group, output):
         at = slice(group * lanes, (group + 1) * lanes)
@@ -221,7 +239,7 @@
         copies.append(pltpu.make_async_copy(out_ref.at[at], out_hbm.at[at], sems.at[group]))
         copies[-1].start()
 
-    staged(rows // SUB, (outgoing, finish))
+    staged(rows // SUB, (receive, outgoing, finish))
     for copy in copies:
         copy.wait()
 

time: 151 us -> 151 us (level)
  no operation moved by 1% of the time
where the time goes in v11:
time: 151 us; the launch traced here: 150 us
  blocking collectives  139 us (92%)
  Pallas kernels  11.3 us (7%)
    all_to_all x4, blocking collectives, exchange(): lax.all_to_all(split, ('col', 'row'), 0, 0, tiled=True)  139 us
    pallas_call x2, Pallas kernels, triangle(): pl.pallas_call(functools.partial(triangle_kernel, direction, share, rows,...  4.49 us
    pallas_call x1, Pallas kernels, by_channels(): pl.pallas_call(functools.partial(start_kernel, share, rows, cols), out_sh...  3.2 us

profile of v11, /device:TPU:0, one launch (start us, length us, event | category | flops | bytes accessed | tf_op | source)
XLA Modules:
  0.0 150.5 jit_solution(5295365296565246948)
XLA Ops:
  0.0 3.2 %start.1 = (bf16[32,5,40,128]{3,2,1,0:T(8,128)(2,1)S(1)}, f32[128,3200]{1,0:T(8,128)S(1)}, f32[128,3200]{1,0:T(8,128)S(1)}, f32[1,3200]{1,0:T(1,128)S(1)}) custom-call(s32[320]{0:T(512)} %valid_hbm.1, s32[320]{0:T(512)} %chain_hbm.1, bf16[3200,128]{1,0:T(8,128)(2,1)} %bitcast.18, f32[128]{0:T(128)} %bias_hbm.1, bf16[2,128,640]{2,1,0:T(8,128)(2,1)} %refs_1_.1), custom_call_target="tpu_custom_call" | custom-call | tf_op jit(solution)/shard_map/start/pallas_call | solution.py:534
  3.2 0.0 copy-start
  3.2 0.0 copy-start.1
  3.2 47.3 %all_to_all.20 = bf16[32,200,128]{2,1,0:T(8,128)(2,1)S(1)} all-to-all(bf16[32,200,128]{2,1,0:T(8,128)(2,1)S(1)} %bitcast.16), channel_id=1, replica_groups=mesh['row'=8,'col'=4] {'col','row'}, dimensions={0} | all-to-all | bytes 3276800 | tf_op jit(solution)/shard_map/all_to_all | solution.py:509
  50.6 0.0 copy-done
  50.6 0.0 copy-done.1
  50.6 2.2 %triangle.2 = (bf16[3200,128]{1,0:T(8,128)(2,1)S(1)}, bf16[896,128]{1,0:T(8,128)(2,1)S(1)}) custom-call(bf16[6400,128]{1,0:T(8,128)(2,1)S(1)} %bitcast.10, bf16[2,128,640]{2,1,0:T(8,128)(2,1)S(1)} %copy-done, bf16[2,128,128]{2,1,0:T(8,128)(2,1)S(1)} %copy-done.1), custom_call_target="tpu_custom_call" | custom-call | tf_op jit(solution)/shard_map/triangle/pallas_call | solution.py:513
  52.8 24.8 %all_to_all.21 = bf16[32,25,4,128]{3,2,1,0:T(4,128)(2,1)S(1)} all-to-all(bf16[32,25,4,128]{3,2,1,0:T(4,128)(2,1)S(1)} %bitcast.17), channel_id=1, replica_groups=mesh['row'=8,'col'=4] {'col','row'}, dimensions={0} | all-to-all | bytes 1638400 | tf_op jit(solution)/shard_map/all_to_all | solution.py:509
  77.5 2.0 %middle.1 = (bf16[32,5,40,128]{3,2,1,0:T(8,128)(2,1)S(1)}, f32[128,3200]{1,0:T(8,128)S(1)}, f32[128,3200]{1,0:T(8,128)S(1)}) custom-call(f32[1,3200]{1,0:T(1,128)S(1)} %get-tuple-element.14.mask_ref, bf16[3200,128]{1,0:T(8,128)(2,1)S(1)} %bitcast.14, f32[128,3200]{1,0:T(8,128)S(1)} %get-tuple-element.17.field_in, f32[128,3200]{1,0:T(8,128)S(1)} %get-tuple-element.18.gate_in, ...), custom_call_target="tpu_custom_call" | custom-call | tf_op jit(solution)/shard_map/middle/pallas_call | solution.py:554
  79.6 42.3 %all_to_all.22 = bf16[32,200,128]{2,1,0:T(8,128)(2,1)S(1)} all-to-all(bf16[32,200,128]{2,1,0:T(8,128)(2,1)S(1)} %bitcast.15), channel_id=1, replica_groups=mesh['row'=8,'col'=4] {'col','row'}, dimensions={0} | all-to-all | bytes 3276800 | tf_op jit(solution)/shard_map/all_to_all | solution.py:509
  121.9 2.3 %triangle.3 = bf16[3200,128]{1,0:T(8,128)(2,1)S(1)} custom-call(bf16[6400,128]{1,0:T(8,128)(2,1)S(1)} %bitcast.11), custom_call_target="tpu_custom_call" | custom-call | tf_op jit(solution)/shard_map/triangle/pallas_call | solution.py:513
  124.2 24.8 %all_to_all.23 = bf16[32,25,4,128]{3,2,1,0:T(4,128)(2,1)S(1)} all-to-all(bf16[32,25,4,128]{3,2,1,0:T(4,128)(2,1)S(1)} %bitcast.13), channel_id=1, replica_groups=mesh['row'=8,'col'=4] {'col','row'}, dimensions={0} | all-to-all | bytes 1638400 | tf_op jit(solution)/shard_map/all_to_all | solution.py:509
  148.9 1.6 %end.1 = bf16[3200,128]{1,0:T(8,128)(2,1)} custom-call(bf16[3200,128]{1,0:T(8,128)(2,1)S(1)} %bitcast.12, f32[128,3200]{1,0:T(8,128)S(1)} %get-tuple-element.21.field_in, f32[128,3200]{1,0:T(8,128)S(1)} %get-tuple-element.22.gate_in, bf16[896,128]{1,0:T(8,128)(2,1)S(1)} %get-tuple-element.19.prepared), custom_call_target="tpu_custom_call" | custom-call | tf_op jit(solution)/shard_map/end/pallas_call | solution.py:564
Async XLA Ops:
  3.2 47.4 %copy-start = (bf16[2,128,640]{2,1,0:T(8,128)(2,1)S(1)}, bf16[2,128,640]{2,1,0:T(8,128)(2,1)}, u32[]{:S(2)}) copy-start(bf16[2,128,640]{2,1,0:T(8,128)(2,1)} %refs_1_.1) | copy-start | bytes 983044
  3.2 47.3 %copy-start.1 = (bf16[2,128,128]{2,1,0:T(8,128)(2,1)S(1)}, bf16[2,128,128]{2,1,0:T(8,128)(2,1)}, u32[]{:S(2)}) copy-start(bf16[2,128,128]{2,1,0:T(8,128)(2,1)} %refs_2_.1) | copy-start | bytes 196612

commit v12 on v10

--- a/solution.py
+++ b/solution.py
@@ -381,19 +381,24 @@
                         put(right_ref, spare, start, block, stacked(before[block][SUB:], now[block][SUB:]))
             before = now
 
-    def product(channel):
+    rights = {}
+
+    def product(channel, pair):
         spare = channel % 2
+        start = pair * 2 * SUB * row_devices
+        at = slice(start, min(start + 2 * SUB * row_devices, groups * SUB * row_devices))
         if direction == 0:
-            right = [even_ref[spare, block, 0:total].astype(BF16) for block in range(blocks)]
-            right = jnp.concatenate(right, axis=1)
-            summed = matmul(left_ref[spare], right, ((1,), (1,)))
+            if pair == 0:
+                right = [even_ref[spare, block, 0:total].astype(BF16) for block in range(blocks)]
+                rights[channel] = jnp.concatenate(right, axis=1)
+            summed = matmul(left_ref[spare, at, :], rights[channel], ((1,), (1,)))
         else:
-            turned = matmul(pick, left_ref[spare], ((1,), (1,))).astype(BF16)
+            turned = matmul(pick[at], left_ref[spare], ((1,), (1,))).astype(BF16)
             summed = matmul(turned, right_ref[spare], ((1,), (0,)))
         for block in range(blocks):
             size = min(LANES, total - block * LANES)
             part = summed[:, block * LANES : block * LANES + size].astype(BF16)
-            result_ref[channel, block, :, 0:size] = part
+            result_ref[channel, block, at, 0:size] = part
 
     def send(tiles, targets):
         for col in range(col_devices):
@@ -420,15 +425,15 @@
             at = slice(unit * 2 * SUB, (unit + 1) * 2 * SUB)
             sent_ref[at, :] = packed[at, :].astype(BF16)
 
-    def pack(channel):
-        for pair in range(groups // 2):
+    def pack(channel, pair):
+        if 2 * pair + 1 < groups:
             tiles = {}
             for step in range(SUB):
                 for block in range(blocks):
                     start = (pair * SUB + step) * 2 * SUB
                     tiles[step, block] = result_ref[channel, block, start : start + 2 * SUB, :]
             send(tiles, [(channel, 2 * pair), (channel, 2 * pair + 1)])
-        if groups % 2 and channel % 2:
+        elif channel % 2:
             group = groups - 1
             tiles = {}
             for block in range(blocks):
@@ -450,14 +455,16 @@
             prepare_weights(w_ref, wo_ref, share, prepared)
         unpack(0, [pair])
     for channel in range(share):
-        product(channel)
-        if channel > 0:
-            pack(channel - 1)
-        if channel + 1 < share:
-            unpack(channel + 1)
-        else:
-            finish()
-    pack(share - 1)
+        for pair in range(pairs):
+            product(channel, pair)
+            if channel > 0:
+                pack(channel - 1, pair)
+            if channel + 1 < share:
+                unpack(channel + 1, [pair])
+            elif pair > 0:
+                pack(channel, pair - 1)
+    finish()
+    pack(share - 1, pairs - 1)
     finish()
 
 

time: 151 us -> 152 us (level)
  no operation moved by 1% of the time
where the time goes in v12:
time: 152 us
  blocking collectives  139 us (91%)
  Pallas kernels  12.7 us (8%)
    all_to_all x4, blocking collectives, exchange(): lax.all_to_all(split, ('col', 'row'), 0, 0, tiled=True)  139 us
    pallas_call x2, Pallas kernels, triangle(): pl.pallas_call(functools.partial(triangle_kernel, direction, share, rows,...  5.91 us
    pallas_call x1, Pallas kernels, by_channels(): pl.pallas_call(functools.partial(start_kernel, share, rows, cols), out_sh...  3.14 us

profile of v12, /device:TPU:0, one launch (start us, length us, event | category | flops | bytes accessed | tf_op | source)
XLA Modules:
  0.0 151.9 jit_solution(5939204648630755365)
XLA Ops:
  0.0 3.1 %start.1 = (bf16[32,5,40,128]{3,2,1,0:T(8,128)(2,1)S(1)}, f32[128,3200]{1,0:T(8,128)S(1)}, f32[128,3200]{1,0:T(8,128)S(1)}, f32[1,3200]{1,0:T(1,128)S(1)}) custom-call(s32[320]{0:T(512)} %valid_hbm.1, s32[320]{0:T(512)} %chain_hbm.1, bf16[3200,128]{1,0:T(8,128)(2,1)} %bitcast.18, f32[128]{0:T(128)} %bias_hbm.1, bf16[2,128,640]{2,1,0:T(8,128)(2,1)} %refs_1_.1), custom_call_target="tpu_custom_call" | custom-call | tf_op jit(solution)/shard_map/start/pallas_call | solution.py:523
  3.1 0.0 copy-start
  3.2 0.0 copy-start.1
  3.2 47.3 %all_to_all.20 = bf16[32,200,128]{2,1,0:T(8,128)(2,1)S(1)} all-to-all(bf16[32,200,128]{2,1,0:T(8,128)(2,1)S(1)} %bitcast.16), channel_id=1, replica_groups=mesh['row'=8,'col'=4] {'col','row'}, dimensions={0} | all-to-all | bytes 3276800 | tf_op jit(solution)/shard_map/all_to_all | solution.py:498
  50.5 0.0 copy-done
  50.5 0.0 copy-done.1
  50.5 2.1 %triangle.2 = (bf16[3200,128]{1,0:T(8,128)(2,1)S(1)}, bf16[896,128]{1,0:T(8,128)(2,1)S(1)}) custom-call(bf16[6400,128]{1,0:T(8,128)(2,1)S(1)} %bitcast.10, bf16[2,128,640]{2,1,0:T(8,128)(2,1)S(1)} %copy-done, bf16[2,128,128]{2,1,0:T(8,128)(2,1)S(1)} %copy-done.1), custom_call_target="tpu_custom_call" | custom-call | tf_op jit(solution)/shard_map/triangle/pallas_call | solution.py:502
  52.6 24.7 %all_to_all.21 = bf16[32,25,4,128]{3,2,1,0:T(4,128)(2,1)S(1)} all-to-all(bf16[32,25,4,128]{3,2,1,0:T(4,128)(2,1)S(1)} %bitcast.17), channel_id=1, replica_groups=mesh['row'=8,'col'=4] {'col','row'}, dimensions={0} | all-to-all | bytes 1638400 | tf_op jit(solution)/shard_map/all_to_all | solution.py:498
  77.4 2.1 %middle.1 = (bf16[32,5,40,128]{3,2,1,0:T(8,128)(2,1)S(1)}, f32[128,3200]{1,0:T(8,128)S(1)}, f32[128,3200]{1,0:T(8,128)S(1)}) custom-call(f32[1,3200]{1,0:T(1,128)S(1)} %get-tuple-element.14.mask_ref, bf16[3200,128]{1,0:T(8,128)(2,1)S(1)} %bitcast.14, f32[128,3200]{1,0:T(8,128)S(1)} %get-tuple-element.17.field_in, f32[128,3200]{1,0:T(8,128)S(1)} %get-tuple-element.18.gate_in, ...), custom_call_target="tpu_custom_call" | custom-call | tf_op jit(solution)/shard_map/middle/pallas_call | solution.py:543
  79.5 42.3 %all_to_all.22 = bf16[32,200,128]{2,1,0:T(8,128)(2,1)S(1)} all-to-all(bf16[32,200,128]{2,1,0:T(8,128)(2,1)S(1)} %bitcast.15), channel_id=1, replica_groups=mesh['row'=8,'col'=4] {'col','row'}, dimensions={0} | all-to-all | bytes 3276800 | tf_op jit(solution)/shard_map/all_to_all | solution.py:498
  121.8 3.8 %triangle.3 = bf16[3200,128]{1,0:T(8,128)(2,1)S(1)} custom-call(bf16[6400,128]{1,0:T(8,128)(2,1)S(1)} %bitcast.11), custom_call_target="tpu_custom_call" | custom-call | tf_op jit(solution)/shard_map/triangle/pallas_call | solution.py:502
  125.6 24.7 %all_to_all.23 = bf16[32,25,4,128]{3,2,1,0:T(4,128)(2,1)S(1)} all-to-all(bf16[32,25,4,128]{3,2,1,0:T(4,128)(2,1)S(1)} %bitcast.13), channel_id=1, replica_groups=mesh['row'=8,'col'=4] {'col','row'}, dimensions={0} | all-to-all | bytes 1638400 | tf_op jit(solution)/shard_map/all_to_all | solution.py:498
  150.3 1.6 %end.1 = bf16[3200,128]{1,0:T(8,128)(2,1)} custom-call(bf16[3200,128]{1,0:T(8,128)(2,1)S(1)} %bitcast.12, f32[128,3200]{1,0:T(8,128)S(1)} %get-tuple-element.21.field_in, f32[128,3200]{1,0:T(8,128)S(1)} %get-tuple-element.22.gate_in, bf16[896,128]{1,0:T(8,128)(2,1)S(1)} %get-tuple-element.19.prepared), custom_call_target="tpu_custom_call" | custom-call | tf_op jit(solution)/shard_map/end/pallas_call | solution.py:553
Async XLA Ops:
  3.1 47.4 %copy-start = (bf16[2,128,640]{2,1,0:T(8,128)(2,1)S(1)}, bf16[2,128,640]{2,1,0:T(8,128)(2,1)}, u32[]{:S(2)}) copy-start(bf16[2,128,640]{2,1,0:T(8,128)(2,1)} %refs_1_.1) | copy-start | bytes 983044
  3.2 47.3 %copy-start.1 = (bf16[2,128,128]{2,1,0:T(8,128)(2,1)S(1)}, bf16[2,128,128]{2,1,0:T(8,128)(2,1)}, u32[]{:S(2)}) copy-start(bf16[2,128,128]{2,1,0:T(8,128)(2,1)} %refs_2_.1) | copy-start | bytes 196612

commit v13 on v11

--- a/solution.py
+++ b/solution.py
@@ -310,7 +310,7 @@
         got_ref, w_ref, wo_ref, sent_ref, prepared, *refs = refs
     else:
         got_ref, sent_ref, *refs = refs
-    wide, left_ref, right_ref, even_ref, result_ref, packed = refs
+    wide, left_ref, right_ref, even_ref, turned_ref, result_ref, packed = refs
     groups = rows // SUB
     pieces = SUB * cols // LANES
     total = row_devices * rows
@@ -399,19 +399,29 @@
                         put(right_ref, spare, start, block, stacked(before[block][SUB:], now[block][SUB:]))
             before = now
 
-    def product(channel):
+    rights = {}
+
+    def turn(channel):
         spare = channel % 2
+        if direction == 1:
+            turned = matmul(pick, left_ref[spare], ((1,), (1,)))
+            turned_ref[spare] = turned.astype(BF16)
+
+    def product(channel, pair):
+        spare = channel % 2
+        start = pair * 2 * SUB * row_devices
+        at = slice(start, min(start + 2 * SUB * row_devices, groups * SUB * row_devices))
         if direction == 0:
-            right = [even_ref[spare, block, 0:total].astype(BF16) for block in range(blocks)]
-            right = jnp.concatenate(right, axis=1)
-            summed = matmul(left_ref[spare], right, ((1,), (1,)))
+            if pair == 0:
+                right = [even_ref[spare, block, 0:total].astype(BF16) for block in range(blocks)]
+                rights[channel] = jnp.concatenate(right, axis=1)
+            summed = matmul(left_ref[spare, at, :], rights[channel], ((1,), (1,)))
         else:
-            turned = matmul(pick, left_ref[spare], ((1,), (1,))).astype(BF16)
-            summed = matmul(turned, right_ref[spare], ((1,), (0,)))
+            summed = matmul(turned_ref[spare, at, :], right_ref[spare], ((1,), (0,)))
         for block in range(blocks):
             size = min(LANES, total - block * LANES)
             part = summed[:, block * LANES : block * LANES + size].astype(BF16)
-            result_ref[channel, block, :, 0:size] = part
+            result_ref[channel, block, at, 0:size] = part
 
     def send(tiles, targets):
         for col in range(col_devices):
@@ -438,15 +448,15 @@
             at = slice(unit * 2 * SUB, (unit + 1) * 2 * SUB)
             sent_ref[at, :] = packed[at, :].astype(BF16)
 
-    def pack(channel):
-        for pair in range(groups // 2):
+    def pack(channel, pair):
+        if 2 * pair + 1 < groups:
             tiles = {}
             for step in range(SUB):
                 for block in range(blocks):
                     start = (pair * SUB + step) * 2 * SUB
                     tiles[step, block] = result_ref[channel, block, start : start + 2 * SUB, :]
             send(tiles, [(channel, 2 * pair), (channel, 2 * pair + 1)])
-        if groups % 2 and channel % 2:
+        elif channel % 2:
             group = groups - 1
             tiles = {}
             for block in range(blocks):
@@ -467,15 +477,20 @@
         elif direction == 0:
             prepare_weights(w_ref, wo_ref, share, prepared)
         unpack(0, [pair])
+    turn(0)
     for channel in range(share):
-        product(channel)
-        if channel > 0:
-            pack(channel - 1)
+        for pair in range(pairs):
+            product(channel, pair)
+            if channel > 0:
+                pack(channel - 1, pair)
+            if channel + 1 < share:
+                unpack(channel + 1, [pair])
+            elif pair > 0:
+                pack(channel, pair - 1)
         if channel + 1 < share:
-            unpack(channel + 1)
-        else:
-            finish()
-    pack(share - 1)
+            turn(channel + 1)
+    finish()
+    pack(share - 1, pairs - 1)
     finish()
 
 
@@ -522,6 +537,7 @@
                 pltpu.VMEM((2, tall, blocks * LANES), BF16),
                 pltpu.VMEM((2, tall, blocks * LANES), BF16),
                 pltpu.VMEM((2, blocks, total + rows, LANES), F32),
+                pltpu.VMEM((2, tall, tall), BF16),
                 pltpu.VMEM((share, blocks, tall, LANES), BF16),
                 padded_sum,
             ],

time: 151 us -> 151 us (level)
  no operation moved by 1% of the time
where the time goes in v13:
time: 151 us
  blocking collectives  139 us (92%)
  Pallas kernels  11.3 us (7%)
    all_to_all x4, blocking collectives, exchange(): lax.all_to_all(split, ('col', 'row'), 0, 0, tiled=True)  139 us
    pallas_call x2, Pallas kernels, triangle(): pl.pallas_call(functools.partial(triangle_kernel, direction, share, rows,...  4.52 us
    pallas_call x1, Pallas kernels, by_channels(): pl.pallas_call(functools.partial(start_kernel, share, rows, cols), out_sh...  3.2 us

profile of v13, /device:TPU:0, one launch (start us, length us, event | category | flops | bytes accessed | tf_op | source)
XLA Modules:
  0.0 150.5 jit_solution(13475555711066074117)
XLA Ops:
  0.0 3.2 %start.1 = (bf16[32,5,40,128]{3,2,1,0:T(8,128)(2,1)S(1)}, f32[128,3200]{1,0:T(8,128)S(1)}, f32[128,3200]{1,0:T(8,128)S(1)}, f32[1,3200]{1,0:T(1,128)S(1)}) custom-call(s32[320]{0:T(512)} %valid_hbm.1, s32[320]{0:T(512)} %chain_hbm.1, bf16[3200,128]{1,0:T(8,128)(2,1)} %bitcast.18, f32[128]{0:T(128)} %bias_hbm.1, bf16[2,128,640]{2,1,0:T(8,128)(2,1)} %refs_1_.1), custom_call_target="tpu_custom_call" | custom-call | tf_op jit(solution)/shard_map/start/pallas_call | solution.py:550
  3.2 0.0 copy-start
  3.2 0.0 copy-start.1
  3.2 47.3 %all_to_all.20 = bf16[32,200,128]{2,1,0:T(8,128)(2,1)S(1)} all-to-all(bf16[32,200,128]{2,1,0:T(8,128)(2,1)S(1)} %bitcast.16), channel_id=1, replica_groups=mesh['row'=8,'col'=4] {'col','row'}, dimensions={0} | all-to-all | bytes 3276800 | tf_op jit(solution)/shard_map/all_to_all | solution.py:524
  50.6 0.0 copy-done
  50.6 0.0 copy-done.1
  50.6 2.1 %triangle.2 = (bf16[3200,128]{1,0:T(8,128)(2,1)S(1)}, bf16[896,128]{1,0:T(8,128)(2,1)S(1)}) custom-call(bf16[6400,128]{1,0:T(8,128)(2,1)S(1)} %bitcast.10, bf16[2,128,640]{2,1,0:T(8,128)(2,1)S(1)} %copy-done, bf16[2,128,128]{2,1,0:T(8,128)(2,1)S(1)} %copy-done.1), custom_call_target="tpu_custom_call" | custom-call | tf_op jit(solution)/shard_map/triangle/pallas_call | solution.py:528
  52.7 24.8 %all_to_all.21 = bf16[32,25,4,128]{3,2,1,0:T(4,128)(2,1)S(1)} all-to-all(bf16[32,25,4,128]{3,2,1,0:T(4,128)(2,1)S(1)} %bitcast.17), channel_id=1, replica_groups=mesh['row'=8,'col'=4] {'col','row'}, dimensions={0} | all-to-all | bytes 1638400 | tf_op jit(solution)/shard_map/all_to_all | solution.py:524
  77.5 2.0 %middle.1 = (bf16[32,5,40,128]{3,2,1,0:T(8,128)(2,1)S(1)}, f32[128,3200]{1,0:T(8,128)S(1)}, f32[128,3200]{1,0:T(8,128)S(1)}) custom-call(f32[1,3200]{1,0:T(1,128)S(1)} %get-tuple-element.14.mask_ref, bf16[3200,128]{1,0:T(8,128)(2,1)S(1)} %bitcast.14, f32[128,3200]{1,0:T(8,128)S(1)} %get-tuple-element.17.field_in, f32[128,3200]{1,0:T(8,128)S(1)} %get-tuple-element.18.gate_in, ...), custom_call_target="tpu_custom_call" | custom-call | tf_op jit(solution)/shard_map/middle/pallas_call | solution.py:570
  79.5 42.3 %all_to_all.22 = bf16[32,200,128]{2,1,0:T(8,128)(2,1)S(1)} all-to-all(bf16[32,200,128]{2,1,0:T(8,128)(2,1)S(1)} %bitcast.15), channel_id=1, replica_groups=mesh['row'=8,'col'=4] {'col','row'}, dimensions={0} | all-to-all | bytes 3276800 | tf_op jit(solution)/shard_map/all_to_all | solution.py:524
  121.8 2.4 %triangle.3 = bf16[3200,128]{1,0:T(8,128)(2,1)S(1)} custom-call(bf16[6400,128]{1,0:T(8,128)(2,1)S(1)} %bitcast.11), custom_call_target="tpu_custom_call" | custom-call | tf_op jit(solution)/shard_map/triangle/pallas_call | solution.py:528
  124.2 24.8 %all_to_all.23 = bf16[32,25,4,128]{3,2,1,0:T(4,128)(2,1)S(1)} all-to-all(bf16[32,25,4,128]{3,2,1,0:T(4,128)(2,1)S(1)} %bitcast.13), channel_id=1, replica_groups=mesh['row'=8,'col'=4] {'col','row'}, dimensions={0} | all-to-all | bytes 1638400 | tf_op jit(solution)/shard_map/all_to_all | solution.py:524
  148.9 1.6 %end.1 = bf16[3200,128]{1,0:T(8,128)(2,1)} custom-call(bf16[3200,128]{1,0:T(8,128)(2,1)S(1)} %bitcast.12, f32[128,3200]{1,0:T(8,128)S(1)} %get-tuple-element.21.field_in, f32[128,3200]{1,0:T(8,128)S(1)} %get-tuple-element.22.gate_in, bf16[896,128]{1,0:T(8,128)(2,1)S(1)} %get-tuple-element.19.prepared), custom_call_target="tpu_custom_call" | custom-call | tf_op jit(solution)/shard_map/end/pallas_call | solution.py:580
Async XLA Ops:
  3.2 47.4 %copy-start = (bf16[2,128,640]{2,1,0:T(8,128)(2,1)S(1)}, bf16[2,128,640]{2,1,0:T(8,128)(2,1)}, u32[]{:S(2)}) copy-start(bf16[2,128,640]{2,1,0:T(8,128)(2,1)} %refs_1_.1) | copy-start | bytes 983044
  3.2 47.3 %copy-start.1 = (bf16[2,128,128]{2,1,0:T(8,128)(2,1)S(1)}, bf16[2,128,128]{2,1,0:T(8,128)(2,1)}, u32[]{:S(2)}) copy-start(bf16[2,128,128]{2,1,0:T(8,128)(2,1)} %refs_2_.1) | copy-start | bytes 196612

commit v14 on v13

--- a/solution.py
+++ b/solution.py
@@ -411,6 +411,10 @@
         spare = channel % 2
         start = pair * 2 * SUB * row_devices
         at = slice(start, min(start + 2 * SUB * row_devices, groups * SUB * row_devices))
+        if direction == 1:
+            if pair > 0:
+                return
+            at = slice(0, groups * SUB * row_devices)
         if direction == 0:
             if pair == 0:
                 right = [even_ref[spare, block, 0:total].astype(BF16) for block in range(blocks)]

time: 151 us -> 151 us (level)
  no operation moved by 1% of the time
where the time goes in v14:
time: 151 us; the launch traced here: 150 us
  blocking collectives  139 us (92%)
  Pallas kernels  11.2 us (7%)
    all_to_all x4, blocking collectives, exchange(): lax.all_to_all(split, ('col', 'row'), 0, 0, tiled=True)  139 us
    pallas_call x2, Pallas kernels, triangle(): pl.pallas_call(functools.partial(triangle_kernel, direction, share, rows,...  4.44 us
    pallas_call x1, Pallas kernels, by_channels(): pl.pallas_call(functools.partial(start_kernel, share, rows, cols), out_sh...  3.2 us

profile of v14, /device:TPU:0, one launch (start us, length us, event | category | flops | bytes accessed | tf_op | source)
XLA Modules:
  0.0 150.4 jit_solution(9060240553818808061)
XLA Ops:
  0.0 3.2 %start.1 = (bf16[32,5,40,128]{3,2,1,0:T(8,128)(2,1)S(1)}, f32[128,3200]{1,0:T(8,128)S(1)}, f32[128,3200]{1,0:T(8,128)S(1)}, f32[1,3200]{1,0:T(1,128)S(1)}) custom-call(s32[320]{0:T(512)} %valid_hbm.1, s32[320]{0:T(512)} %chain_hbm.1, bf16[3200,128]{1,0:T(8,128)(2,1)} %bitcast.18, f32[128]{0:T(128)} %bias_hbm.1, bf16[2,128,640]{2,1,0:T(8,128)(2,1)} %refs_1_.1), custom_call_target="tpu_custom_call" | custom-call | tf_op jit(solution)/shard_map/start/pallas_call | solution.py:554
  3.2 0.0 copy-start
  3.2 0.0 copy-start.1
  3.2 47.3 %all_to_all.20 = bf16[32,200,128]{2,1,0:T(8,128)(2,1)S(1)} all-to-all(bf16[32,200,128]{2,1,0:T(8,128)(2,1)S(1)} %bitcast.16), channel_id=1, replica_groups=mesh['row'=8,'col'=4] {'col','row'}, dimensions={0} | all-to-all | bytes 3276800 | tf_op jit(solution)/shard_map/all_to_all | solution.py:528
  50.6 0.0 copy-done
  50.6 0.0 copy-done.1
  50.6 2.1 %triangle.2 = (bf16[3200,128]{1,0:T(8,128)(2,1)S(1)}, bf16[896,128]{1,0:T(8,128)(2,1)S(1)}) custom-call(bf16[6400,128]{1,0:T(8,128)(2,1)S(1)} %bitcast.10, bf16[2,128,640]{2,1,0:T(8,128)(2,1)S(1)} %copy-done, bf16[2,128,128]{2,1,0:T(8,128)(2,1)S(1)} %copy-done.1), custom_call_target="tpu_custom_call" | custom-call | tf_op jit(solution)/shard_map/triangle/pallas_call | solution.py:532
  52.7 24.8 %all_to_all.21 = bf16[32,25,4,128]{3,2,1,0:T(4,128)(2,1)S(1)} all-to-all(bf16[32,25,4,128]{3,2,1,0:T(4,128)(2,1)S(1)} %bitcast.17), channel_id=1, replica_groups=mesh['row'=8,'col'=4] {'col','row'}, dimensions={0} | all-to-all | bytes 1638400 | tf_op jit(solution)/shard_map/all_to_all | solution.py:528
  77.5 2.0 %middle.1 = (bf16[32,5,40,128]{3,2,1,0:T(8,128)(2,1)S(1)}, f32[128,3200]{1,0:T(8,128)S(1)}, f32[128,3200]{1,0:T(8,128)S(1)}) custom-call(f32[1,3200]{1,0:T(1,128)S(1)} %get-tuple-element.14.mask_ref, bf16[3200,128]{1,0:T(8,128)(2,1)S(1)} %bitcast.14, f32[128,3200]{1,0:T(8,128)S(1)} %get-tuple-element.17.field_in, f32[128,3200]{1,0:T(8,128)S(1)} %get-tuple-element.18.gate_in, ...), custom_call_target="tpu_custom_call" | custom-call | tf_op jit(solution)/shard_map/middle/pallas_call | solution.py:574
  79.5 42.3 %all_to_all.22 = bf16[32,200,128]{2,1,0:T(8,128)(2,1)S(1)} all-to-all(bf16[32,200,128]{2,1,0:T(8,128)(2,1)S(1)} %bitcast.15), channel_id=1, replica_groups=mesh['row'=8,'col'=4] {'col','row'}, dimensions={0} | all-to-all | bytes 3276800 | tf_op jit(solution)/shard_map/all_to_all | solution.py:528
  121.8 2.3 %triangle.3 = bf16[3200,128]{1,0:T(8,128)(2,1)S(1)} custom-call(bf16[6400,128]{1,0:T(8,128)(2,1)S(1)} %bitcast.11), custom_call_target="tpu_custom_call" | custom-call | tf_op jit(solution)/shard_map/triangle/pallas_call | solution.py:532
  124.1 24.7 %all_to_all.23 = bf16[32,25,4,128]{3,2,1,0:T(4,128)(2,1)S(1)} all-to-all(bf16[32,25,4,128]{3,2,1,0:T(4,128)(2,1)S(1)} %bitcast.13), channel_id=1, replica_groups=mesh['row'=8,'col'=4] {'col','row'}, dimensions={0} | all-to-all | bytes 1638400 | tf_op jit(solution)/shard_map/all_to_all | solution.py:528
  148.9 1.6 %end.1 = bf16[3200,128]{1,0:T(8,128)(2,1)} custom-call(bf16[3200,128]{1,0:T(8,128)(2,1)S(1)} %bitcast.12, f32[128,3200]{1,0:T(8,128)S(1)} %get-tuple-element.21.field_in, f32[128,3200]{1,0:T(8,128)S(1)} %get-tuple-element.22.gate_in, bf16[896,128]{1,0:T(8,128)(2,1)S(1)} %get-tuple-element.19.prepared), custom_call_target="tpu_custom_call" | custom-call | tf_op jit(solution)/shard_map/end/pallas_call | solution.py:584
Async XLA Ops:
  3.2 47.4 %copy-start = (bf16[2,128,640]{2,1,0:T(8,128)(2,1)S(1)}, bf16[2,128,640]{2,1,0:T(8,128)(2,1)}, u32[]{:S(2)}) copy-start(bf16[2,128,640]{2,1,0:T(8,128)(2,1)} %refs_1_.1) | copy-start | bytes 983044
  3.2 47.3 %copy-start.1 = (bf16[2,128,128]{2,1,0:T(8,128)(2,1)S(1)}, bf16[2,128,128]{2,1,0:T(8,128)(2,1)}, u32[]{:S(2)}) copy-start(bf16[2,128,128]{2,1,0:T(8,128)(2,1)} %refs_2_.1) | copy-start | bytes 196612
